TPU v7x, 256 devices: a whole 4x4x8 slice. The times are simulated.
256 devices in a mesh: wa: 64 (over z, y, core), col: 4 (over x).
Axes of the slice: x: 4, y: 4, z: 8, core: 2. Of those that a mesh axis runs over, the one named last changes fastest.
Arguments:
- records: float32 [512, 1024, 1024], P('wa', 'col'), as said below
- bin_weight: float32 [128], replicated, may hold values from 0.5 to 2
Outputs:
- coherence: float32 [2, 128, 1024, 1024], P(None, 'wa', 'col')
Inputs may be any that keep to these rules, and one draw needn't show every extreme that they name: `records`: finite values.
All inputs are finite; a program needn't handle non-finite values.
Results may differ from a plain program's by a relative error of at most 0.0034.
Values may be sent and summed in bfloat16 or wider, within the bound.
No kernel may reach another device: no remote copies, remote signals or barrier semaphores. Data moves between devices by JAX's collectives and lax.ppermute only.
A program may use at most 64 MiB of HBM per device.

v0:
```python
import math

import jax
import jax.numpy as jnp
from jax import lax
from jax.sharding import PartitionSpec as P

K0 = 32


def fourier_table(samples, first_bin, count):
    steps = jnp.arange(samples, dtype=jnp.int32)
    freqs = first_bin + jnp.arange(count, dtype=jnp.int32)
    phases = steps[:, None] * freqs[None, :] % samples
    angles = phases.astype(jnp.float32) * (2.0 * math.pi / samples)
    return jnp.concatenate([jnp.cos(angles), -jnp.sin(angles)], axis=1)


def taper_window(samples):
    steps = jnp.arange(samples, dtype=jnp.int32).astype(jnp.float32)
    return 0.5 - 0.5 * jnp.cos(steps * (2.0 * math.pi / samples))


def body(records, bin_weight):
    windows, local_chan, samples = records.shape
    kept = bin_weight.shape[0]
    table = fourier_table(samples, K0, kept)
    tapered = records * taper_window(samples)[None, None, :]
    spectra = jnp.einsum("wcs,sf->wfc", tapered, table, precision=lax.Precision.HIGHEST)
    real_part = spectra[:, :kept]
    imag_part = spectra[:, kept:]
    power = lax.psum(jnp.sum(real_part * real_part + imag_part * imag_part, axis=2), "col")
    channels = local_chan * lax.axis_size("col")
    factor = bin_weight[None, :] / jnp.sqrt(power / channels + 1e-06)
    whitened = (spectra * jnp.concatenate([factor, factor], axis=1)[:, :, None]).astype(
        jnp.bfloat16
    )
    squares = whitened.astype(jnp.float32)
    partial_energy = jnp.sum(squares * squares, axis=(0, 1))
    row_start = lax.axis_index("col") * local_chan
    summed = lax.psum(partial_energy, "wa")
    energy = lax.all_gather(summed, "col", axis=0, tiled=True)
    inverse = 1.0 / jnp.sqrt(energy)
    total_windows = windows * lax.axis_size("wa")
    scale = math.sqrt(total_windows) * kept
    inverse_rows = lax.dynamic_slice_in_dim(inverse, row_start, local_chan)
    gathered = lax.all_gather(whitened, "col", axis=2, tiled=True)
    stacked = gathered.reshape(windows, 2, kept, channels)
    complete = lax.all_to_all(stacked, "wa", split_axis=2, concat_axis=0, tiled=True)
    owned = lax.dynamic_slice_in_dim(complete, row_start, local_chan, 3)
    rotated = jnp.stack([owned[:, 1], -owned[:, 0]], axis=1)
    block = jnp.einsum(
        "qwpkc,wpkd->qkcd",
        jnp.stack([owned, rotated], axis=0),
        complete,
        preferred_element_type=jnp.float32,
    )
    return block * (inverse_rows[None, None, :, None] * inverse[None, None, None, :] * scale)


def solution(mesh):
    placed = (P("wa", "col", None), P())
    return jax.shard_map(
        body, mesh=mesh, in_specs=placed, out_specs=P(None, "wa", "col", None), check_vma=False
    )
```

profile of v0, /device:TPU:128, one launch (start us, length us, event | category | flops | bytes accessed | tf_op | source)
XLA Modules:
  0.0 346.3 jit_solution(432117216953263219)
XLA Ops:
  6.5 0.0 all-gather.3.cloned.1.call-start
  6.6 2.1 fusion.24
  8.7 0.0 copy-start
  8.7 9.5 %fusion.11 = f32[8,256,256]{2,1,0:T(8,128)S(1)} fusion(f32[8,256,1024]{2,1,0:T(8,128)} %param.2, f32[1024]{0:T(1024)S(1)} %multiply_subtract_fusion, f32[1024,128]{0,1:T(8,128)S(1)} %get-tuple-element.10, f32[1024,128]{0,1:T(8,128)S(1)} %get-tuple-element.9), kind=kOutput, calls=%fused_computation.13 | convolution fusion | flops 6444810240 | bytes 11538432 | tf_op jit(solution)/shard_map/wcs,sf->wfc/dot_general | solution.py:29
  18.3 0.2 fusion.15
  18.5 10.5 %psum.14 = f32[8,128]{1,0:T(8,128)S(1)} all-reduce(f32[8,128]{1,0:T(8,128)S(1)} %fusion.15), channel_id=1, replica_groups=mesh['wa'=64,'col'=4] {'col'}, use_global_device_ids=true, to_apply=%region_1.2 | all-reduce | flops 1024 | bytes 8192 | tf_op jit(solution)/shard_map/psum | solution.py:32
  29.0 0.0 copy-done
  29.0 1.3 multiply_reduce_fusion
  30.3 0.0 all-gather.3.cloned.1.call-update
  30.3 54.0 %all-gather.3.cloned.1.call-done = bf16[8,256,1024]{2,1,0:T(8,128)(2,1)} async-done(((bf16[8,256,256]{2,1,0:T(8,128)(2,1)}), bf16[8,256,1024]{2,1,0:T(8,128)(2,1)}) %all-gather.3.cloned.1.call-update) | async-done | bytes 4194320 | tf_op jit(solution)/shard_map/all_gather | solution.py:47
  84.4 8.6 %copy.6 = bf16[8,2,128,1024]{3,1,0,2:T(2,128)(2,1)} copy(bf16[8,2,128,1024]{3,2,1,0:T(8,128)(2,1)} %bitcast.33) | data formatting | bytes 8388608 | tf_op jit(solution)/shard_map/reshape | solution.py:48
  92.9 10.5 %all-to-all-start = ((bf16[8,2,128,1024]{3,1,0,2:T(2,128)(2,1)}), bf16[8,2,128,1024]{3,1,0,2:T(2,128)(2,1)}, u32[]{:S(2)}, u32[]{:S(2)}) async-start(bf16[8,2,128,1024]{3,1,0,2:T(2,128)(2,1)} %copy.6), calls=%async_computation | async-start | bytes 8388608 | tf_op jit(solution)/shard_map/all_to_all | solution.py:49
  103.4 210.9 %psum.15 = f32[256]{0:T(256)S(1)} all-reduce(f32[256]{0:T(256)S(1)} %get-tuple-element.5), channel_id=1, replica_groups=mesh['wa'=64,'col'=4] {'wa'}, use_global_device_ids=true, to_apply=%region_3.4 | all-reduce | flops 256 | bytes 2048 | tf_op jit(solution)/shard_map/psum | solution.py:41
  314.3 9.0 %all-gather = f32[4,1,256]{2,1,0:T(1,128)S(1)} all-gather(f32[1,1,256]{2,1,0:T(1,128)S(1)} %bitcast.36), channel_id=1, replica_groups=mesh['wa'=64,'col'=4] {'col'}, dimensions={0}, use_global_device_ids=true | all-gather | bytes 5120 | tf_op jit(solution)/shard_map/all_gather | solution.py:42
  323.4 0.1 dynamic_slice.7
  323.4 0.2 multiply_multiply_fusion
  323.6 0.0 all-to-all-done
  323.7 3.5 %copy.21 = bf16[8,2,64,2,1024]{4,0,2,1,3:T(8,128)(2,1)S(1)} copy(bf16[8,2,64,2,1024]{4,1,0,3,2:T(2,128)(2,1)} %bitcast.3) | data formatting | bytes 8388608 | tf_op jit(solution)/shard_map/all_to_all | solution.py:49
  327.2 0.2 constant_dynamic-slice_fusion
  327.4 0.2 maximum_bitcast_fusion.2
  327.6 6.6 %bitcast_multiply_fusion = f32[2,2,256,1024]{2,3,0,1:T(8,128)} fusion(bf16[8,2,64,2,1024]{4,1,0,3,2:T(2,128)(2,1)} %bitcast.3, bf16[1,512,2,2,256]{4,1,2,0,3:T(8,128)(2,1)S(1)} %get-tuple-element.11, bf16[1,512,2,2,256]{4,1,2,0,3:T(8,128)(2,1)S(1)} %get-tuple-element.12, f32[256,1024]{0,1:T(8,128)S(1)} %multiply_multiply_fusion), kind=kOutput, calls=%fused_computation.4 | convolution fusion | flops 2152726528 | bytes 11534336 | tf_op jit(solution)/shard_map/qwpkc,wpkd->qkcd/dot_general | solution.py:52
  334.1 5.3 %copy.9 = f32[2,2,256,1024]{3,2,1,0:T(8,128)} copy(f32[2,2,256,1024]{2,3,0,1:T(8,128)} %bitcast_multiply_fusion) | data formatting | bytes 8388608 | tf_op jit(solution)/shard_map/mul | solution.py:58
  (5 shorter events, 0.1 us)
Async XLA Ops:
  6.5 77.8 %all-gather.3.cloned.1.call-start = ((), (), s32[]{:S(2)}) async-start(), calls=%async_computation.1 | async-start | bytes 5242880 | tf_op jit(solution)/shard_map/all_gather | solution.py:47
  8.7 20.3 %copy-start = (f32[128]{0:T(128)S(1)}, f32[128]{0:T(128)}, u32[]{:S(2)}) copy-start(f32[128]{0:T(128)} %param.3) | copy-start | bytes 1540
  92.9 230.7 %all-to-all-start = ((bf16[8,2,128,1024]{3,1,0,2:T(2,128)(2,1)}), bf16[8,2,128,1024]{3,1,0,2:T(2,128)(2,1)}, u32[]{:S(2)}, u32[]{:S(2)}) async-start(bf16[8,2,128,1024]{3,1,0,2:T(2,128)(2,1)} %copy.6), calls=%async_computation | async-start | bytes 8388608 | tf_op jit(solution)/shard_map/all_to_all | solution.py:49
Sparse Core Ops, SparseCore 0:
  30.5 53.8 all-gather.2
where the time goes:
time: 347 us; the launch traced here: 346 us
  blocking collectives  230 us (66%)
  waiting for transfers between devices  54 us (16%)
  local copies, waits for them, and re-layouts  17.5 us (5%)
  matrix products  16.1 us (5%)
  between operations  13.5 us (4%)
  starting transfers between devices  10.5 us (3%)
  other arithmetic  4.3 us (1%)
    psum x1, blocking collectives, body(): summed = lax.psum(partial_energy, 'wa')  211 us
    all_gather x1, waiting for transfers between devices, body(): gathered = lax.all_gather(whitened, 'col', axis=2, tiled=True)  54 us
    all_to_all x1, starting transfers between devices, body(): lax.all_to_all(stacked, 'wa', split_axis=2, concat_axis=0, tiled=True)  10.5 us
    psum x1, blocking collectives, body(): lax.psum(jnp.sum(real_part * real_part + imag_part * imag_part, axis=2),...  10.5 us
    dot_general x1, matrix products, body(): jnp.einsum('wcs,sf->wfc', tapered, table, precision=lax.Precision.HIGHEST)  9.52 us
    all_gather x1, blocking collectives, body(): energy = lax.all_gather(summed, 'col', axis=0, tiled=True)  9.01 us
    reshape x1, local copies, waits for them, and re-layouts, body(): stacked = gathered.reshape(windows, 2, kept, channels)  8.56 us
  transfers between devices with their start and end apart: 2, of which 1 were waited for; matrix products, arithmetic and copies ran while one was open for 0% of the time, Pallas kernels for 0%

commit v1 on v0

v1 whole, which is shorter than its diff:
```python
import functools
import math

import jax
import jax.numpy as jnp
import numpy as np
from jax import lax
from jax.experimental import pallas as pl
from jax.experimental.pallas import tpu as pltpu
from jax.sharding import PartitionSpec as P

K0 = 32
BF = jnp.bfloat16
F32 = jnp.float32


def split_tables(samples, kept):
    half = samples // 2
    steps = np.arange(half, dtype=np.int64)
    tables = []
    for parity in range(2):
        freqs = K0 + np.arange(parity, kept, 2)
        angles = 2.0 * math.pi / samples * ((steps[None, :] * freqs[:, None]) % samples)
        exact = np.concatenate([np.cos(angles), -np.sin(angles)], axis=0).astype(np.float32)
        high = exact.astype(BF)
        low = (exact - high.astype(np.float32)).astype(BF)
        tables.append(np.concatenate([high, low], axis=0))
    return np.stack(tables)


def taper_window(samples):
    steps = np.arange(samples)
    return (0.5 - 0.5 * np.cos(2.0 * math.pi / samples * steps)).astype(np.float32)[None, :]


def nt(a, b):
    return lax.dot_general(a, b, (((1,), (1,)), ((), ())), preferred_element_type=F32)


def spectra_kernel(records, taper, tables, spec, power):
    w = pl.program_id(0)
    samples = records.shape[2]
    half = samples // 2
    bins = tables.shape[1] // 4
    tapered = records[0] * taper[...]
    first, second = tapered[:, :half], tapered[:, half:]
    ones = jnp.ones((8, records.shape[1]), BF)
    rows = []
    for parity in range(2):
        folded = first + second if parity == 0 else first - second
        high = folded.astype(BF)
        low = (folded - high.astype(F32)).astype(BF)
        both = nt(tables[parity], high)
        result = both[: 2 * bins] + both[2 * bins :] + nt(tables[parity, : 2 * bins], low)
        real, imag = result[:bins], result[bins:]
        for side in range(2):
            lanes = slice(128 * side, 128 * side + 128)
            spec[side, pl.ds(16 * parity + w, bins, stride=32), :] = real[:, lanes]
            spec[side, pl.ds(16 * parity + 8 + w, bins, stride=32), :] = imag[:, lanes]
        square = real * real + imag * imag
        top = square.astype(BF)
        rest = square - top.astype(F32)
        mid = rest.astype(BF)
        end = (rest - mid.astype(F32)).astype(BF)
        rows.append(nt(ones, top) + nt(ones, mid) + nt(ones, end))
    power[pl.ds(w, 1), :] = jnp.concatenate(rows, axis=1)[:1]


def whiten_kernel(channels, spec, power, weight, message):
    bins = power.shape[1] // 2
    factor = weight[...] / jnp.sqrt(power[...] / channels + 1e-06)
    energy = jnp.zeros((8, 256), F32)
    for owner in range(bins):
        for parity in range(2):
            lane = parity * bins + owner
            scale = factor[:, lane : lane + 1]
            start = owner * 32 + parity * 16
            block = jnp.concatenate(
                [spec[0, start : start + 16, :], spec[1, start : start + 16, :]], axis=1
            )
            real = (block[:8] * scale).astype(BF).astype(F32)
            imag = (block[8:] * scale).astype(BF).astype(F32)
            energy = energy + (real * real + imag * imag)
            message[owner, 16 * parity : 16 * parity + 16, :] = jnp.concatenate(
                [real, imag], axis=0
            ).astype(BF)
    total = jnp.sum(energy, axis=0, keepdims=True)
    high = total.astype(BF).astype(F32)
    mid = (total - high).astype(BF).astype(F32)
    low = total - high - mid
    row = lax.broadcasted_iota(jnp.int32, (8, 256), 0)
    tail = jnp.where(row == 0, high, jnp.where(row == 1, mid, jnp.where(row == 2, low, 0.0)))
    tail = tail.astype(BF)
    for owner in range(bins):
        message[owner, 32:40, :] = tail


def gram_kernel(scale, col, own, right, left, far_a, far_b, energy, out, lhs):
    step = pl.program_id(1)
    depth = own.shape[0] * own.shape[1]
    chan = own.shape[2]
    half = depth // 2
    me = col[0]

    def emit(product, which):
        rows = lax.rsqrt(energy[0:1, :]) * scale
        cols = lax.rsqrt(energy[pl.ds(which, 1), :])
        weight = jnp.transpose(jnp.broadcast_to(rows, (8, chan)))[:, :1] * cols
        out[0, 0] = product[:chan] * weight
        out[1, 0] = product[chan:] * weight

    @pl.when(step == 0)
    def _():
        mine = own[...].reshape(depth, chan)
        real = own[:, :8, :]
        turned = jnp.concatenate([own[:, 8:, :], -real], axis=1).reshape(depth, chan)
        lhs[:chan] = jnp.transpose(mine)
        lhs[chan:] = jnp.transpose(turned)
        emit(jnp.dot(lhs[...], mine, preferred_element_type=F32), 0)

    @pl.when(step == 1)
    def _():
        emit(jnp.dot(lhs[...], right[...].reshape(depth, chan), preferred_element_type=F32), 1)

    @pl.when(step == 2)
    def _():
        emit(jnp.dot(lhs[...], left[...].reshape(depth, chan), preferred_element_type=F32), 2)

    @pl.when(step == 3)
    def _():
        product = jnp.dot(
            lhs[:, :half], far_a[...].reshape(half, chan), preferred_element_type=F32
        )
        product += jnp.dot(
            lhs[:, half:], far_b[...].reshape(half, chan), preferred_element_type=F32
        )
        emit(product, 3)


def ring(size, shift):
    return [(i, (i + shift) % size) for i in range(size)]


def body(owners, columns, records, bin_weight):
    windows, chan, samples = records.shape
    kept = bin_weight.shape[0]
    bins = kept // 2
    spec, power = pl.pallas_call(
        spectra_kernel,
        grid=(windows,),
        in_specs=[
            pl.BlockSpec((1, chan, samples), lambda w: (w, 0, 0)),
            pl.BlockSpec((1, samples), lambda w: (0, 0)),
            pl.BlockSpec((2, 2 * kept, samples // 2), lambda w: (0, 0, 0)),
        ],
        out_specs=[
            pl.BlockSpec((2, kept * 16, 128), lambda w: (0, 0, 0)),
            pl.BlockSpec((windows, kept), lambda w: (0, 0)),
        ],
        out_shape=[
            jax.ShapeDtypeStruct((2, kept * 16, 128), F32),
            jax.ShapeDtypeStruct((windows, kept), F32),
        ],
        compiler_params=pltpu.CompilerParams(vmem_limit_bytes=58 << 20),
        name="spectra",
    )(records, taper_window(samples), split_tables(samples, kept))
    power = lax.psum(power, "col")
    weight = bin_weight.reshape(bins, 2).T.reshape(1, kept)
    message = pl.pallas_call(
        functools.partial(whiten_kernel, chan * columns),
        out_shape=jax.ShapeDtypeStruct((owners, 40, chan), BF),
        compiler_params=pltpu.CompilerParams(vmem_limit_bytes=40 << 20),
        name="whiten",
    )(spec, power, weight)
    owned = lax.all_to_all(message, "wa", split_axis=0, concat_axis=0, tiled=True)
    mine = owned[:, :32]
    energy = jnp.sum(owned[:, 32:].astype(F32), axis=(0, 1))[None, :]
    ahead, back = ring(columns, 1), ring(columns, columns - 1)
    from_left = lax.ppermute(mine, "col", ahead)
    from_right = lax.ppermute(mine, "col", back)
    half = owners // 2
    far_a = lax.ppermute(from_left[:half], "col", ahead)
    far_b = lax.ppermute(from_right[half:], "col", back)
    energies = jnp.concatenate(
        [
            energy,
            lax.ppermute(energy, "col", back),
            lax.ppermute(energy, "col", ahead),
            lax.ppermute(energy, "col", ring(columns, 2)),
        ],
        axis=0,
    )
    col = lax.axis_index("col").astype(jnp.int32)[None]
    total_windows = windows * owners
    scale = math.sqrt(total_windows) * kept

    def where(b, s, c):
        shift = jnp.where(s == 2, 3, jnp.where(s == 3, 2, s))
        return (0, b, 0, lax.rem(c[0] + shift, columns))

    bin_block = lambda n: pl.BlockSpec((n, 16, chan), lambda b, s, c: (0, b, 0))
    return pl.pallas_call(
        functools.partial(gram_kernel, scale),
        grid_spec=pltpu.PrefetchScalarGridSpec(
            num_scalar_prefetch=1,
            grid=(2, 4),
            in_specs=[
                bin_block(owners),
                bin_block(owners),
                bin_block(owners),
                bin_block(half),
                bin_block(half),
                pl.BlockSpec((4, chan), lambda b, s, c: (0, 0)),
            ],
            out_specs=pl.BlockSpec((2, 1, chan, chan), where),
            scratch_shapes=[pltpu.VMEM((2 * chan, 16 * owners), BF)],
        ),
        out_shape=jax.ShapeDtypeStruct((2, 2, chan, chan * columns), F32),
        compiler_params=pltpu.CompilerParams(vmem_limit_bytes=40 << 20),
        name="gram",
    )(col, mine, from_right, from_left, far_a, far_b, energies)


def solution(mesh):
    owners, columns = mesh.shape["wa"], mesh.shape["col"]
    return jax.shard_map(
        functools.partial(body, owners, columns),
        mesh=mesh,
        in_specs=(P("wa", "col", None), P()),
        out_specs=P(None, "wa", "col", None),
        check_vma=False,
    )
```

time: 347 us -> 123 us (0.35)
  the two profiles are of different devices: /device:TPU:128 before, /device:TPU:32 now
where the time goes in v1:
time: 123 us; the launch traced here: 122 us
  blocking collectives  55.6 us (45%)
  waiting for transfers between devices  30.6 us (25%)
  Pallas kernels  20.9 us (17%)
  starting transfers between devices  9.95 us (8%)
  local copies, waits for them, and re-layouts  4.32 us (4%)
    all_to_all x1, blocking collectives, body(): lax.all_to_all(message, 'wa', split_axis=0, concat_axis=0, tiled=True)  45.1 us
    ppermute x1, waiting for transfers between devices, body(): from_left = lax.ppermute(mine, 'col', ahead)  23.3 us
    pallas_call x1, Pallas kernels, body(): pl.pallas_call(spectra_kernel, grid=(windows,), in_specs=[pl.BlockSpec((1...  12.9 us
    psum x1, blocking collectives, body(): power = lax.psum(power, 'col')  10.5 us
    pallas_call x1, Pallas kernels, body(): pl.pallas_call(functools.partial(gram_kernel, scale), grid_spec=pltpu.Pre...  7.45 us
    ppermute x1, waiting for transfers between devices, body(): lax.ppermute(energy, 'col', ring(columns, 2))  4.89 us
    ppermute x1, starting transfers between devices, body(): far_b = lax.ppermute(from_right[half:], 'col', back)  3.23 us
    ppermute x1, starting transfers between devices, body(): from_right = lax.ppermute(mine, 'col', back)  3.22 us
  transfers between devices with their start and end apart: 7, of which 4 were waited for; matrix products, arithmetic and copies ran while one was open for 1% of the time, Pallas kernels for 0%

profile of v1, /device:TPU:32, one launch (start us, length us, event | category | flops | bytes accessed | tf_op | source)
XLA Modules:
  0.0 121.5 jit_solution(10504809015839056463)
XLA Ops:
  0.0 0.8 reshape.6
  0.8 0.1 copy.6
  0.9 0.1 reshape.7.weight
  0.9 12.9 %spectra.1 = (f32[2,2048,128]{2,1,0:T(8,128)}, f32[8,128]{1,0:T(8,128)}) custom-call(f32[8,256,1024]{2,1,0:T(8,128)} %records.1, f32[1,1024]{1,0:T(1,128)} %constant.10.clone.taper, bf16[2,256,512]{2,1,0:T(8,128)(2,1)} %constant.11.clone.tables), custom_call_target="tpu_custom_call" | custom-call | tf_op jit(solution)/shard_map/spectra/pallas_call | solution.py:148
  13.9 10.5 %psum.7.power = f32[8,128]{1,0:T(8,128)S(1)} all-reduce(f32[8,128]{1,0:T(8,128)} %get-tuple-element.8), channel_id=1, replica_groups=mesh['wa'=64,'col'=4] {'col'}, use_global_device_ids=true, to_apply=%region_0.0 | all-reduce | flops 1024 | bytes 8192 | tf_op jit(solution)/shard_map/psum | solution.py:167
  24.4 0.0 copy-start
  24.4 1.6 %copy-done = f32[2,2048,128]{2,1,0:T(8,128)S(1)} copy-done((f32[2,2048,128]{2,1,0:T(8,128)S(1)}, f32[2,2048,128]{2,1,0:T(8,128)}, u32[]{:S(2)}) %copy-start) | copy-done | bytes 2097176
  25.9 0.5 whiten.1
  26.4 45.1 %all_to_all.5 = bf16[64,40,256]{2,1,0:T(8,128)(2,1)S(1)} all-to-all(bf16[64,40,256]{2,1,0:T(8,128)(2,1)S(1)} %whiten.1), channel_id=1, replica_groups=mesh['wa'=64,'col'=4] {'wa'}, dimensions={0} | all-to-all | bytes 2621440 | tf_op jit(solution)/shard_map/all_to_all | solution.py:175
  71.6 0.1 slice.16.own
  71.7 0.1 collective-permute-start.1
  71.8 3.2 %collective-permute-start = (bf16[64,32,256]{2,1,0:T(8,128)(2,1)S(1)}, bf16[64,32,256]{2,1,0:T(8,128)(2,1)S(1)}, u32[]{:S(2)}, u32[]{:S(2)}) collective-permute-start(bf16[64,32,256]{2,1,0:T(8,128)(2,1)S(1)} %slice.16.own), channel_id=1, source_target_pairs={{0,3},{1,0},{2,1},{3,2},{4,7},{5,4},{6,5},{7,6},{8,11},{9,8},{10,9... | collective-permute-start | bytes 3145736 | tf_op jit(solution)/shard_map/ppermute | solution.py:180
  75.0 23.3 %collective-permute-done.1.left = bf16[64,32,256]{2,1,0:T(8,128)(2,1)S(1)} collective-permute-done((bf16[64,32,256]{2,1,0:T(8,128)(2,1)S(1)}, bf16[64,32,256]{2,1,0:T(8,128)(2,1)S(1)}, u32[]{:S(2)}, u32[]{:S(2)}) %collective-permute-start.1) | collective-permute-done | bytes 1048608 | tf_op jit(solution)/shard_map/ppermute | solution.py:179
  98.3 0.8 slice.17
  99.1 0.0 collective-permute-start.2
  99.1 0.0 collective-permute-done.right
  99.1 0.8 slice.18
  100.0 3.2 %collective-permute-start.3 = (bf16[32,32,256]{2,1,0:T(8,128)(2,1)}, bf16[32,32,256]{2,1,0:T(8,128)(2,1)}, u32[]{:S(2)}, u32[]{:S(2)}) collective-permute-start(bf16[32,32,256]{2,1,0:T(8,128)(2,1)} %slice.18), channel_id=1, source_target_pairs={{0,3},{1,0},{2,1},{3,2},{4,7},{5,4},{6,5},{7,6},{8,11},{9,8},{10,9... | collective-permute-start | bytes 1572872 | tf_op jit(solution)/shard_map/ppermute | solution.py:183
  103.2 0.1 convert_reduce_fusion
  103.3 0.1 collective-permute-start.6
  103.4 0.8 collective-permute-start.5
  104.2 2.5 %collective-permute-start.4 = (f32[1,256]{1,0:T(1,128)S(1)}, f32[1,256]{1,0:T(1,128)S(1)}, u32[]{:S(2)}, u32[]{:S(2)}) collective-permute-start(f32[1,256]{1,0:T(1,128)S(1)} %bitcast.6), channel_id=1, source_target_pairs={{0,3},{1,0},{2,1},{3,2},{4,7},{5,4},{6,5},{7,6},{8,11},{9,8},{10,9... | collective-permute-start | bytes 3080 | tf_op jit(solution)/shard_map/ppermute | solution.py:187
  106.7 4.9 %collective-permute-done.6 = f32[1,256]{1,0:T(1,128)S(1)} collective-permute-done((f32[1,256]{1,0:T(1,128)S(1)}, f32[1,256]{1,0:T(1,128)S(1)}, u32[]{:S(2)}, u32[]{:S(2)}) %collective-permute-start.6) | collective-permute-done | bytes 1056 | tf_op jit(solution)/shard_map/ppermute | solution.py:189
  111.6 2.3 %collective-permute-done.5 = f32[1,256]{1,0:T(1,128)S(1)} collective-permute-done((f32[1,256]{1,0:T(1,128)S(1)}, f32[1,256]{1,0:T(1,128)S(1)}, u32[]{:S(2)}, u32[]{:S(2)}) %collective-permute-start.5) | collective-permute-done | bytes 1056 | tf_op jit(solution)/shard_map/ppermute | solution.py:188
  113.9 0.1 collective-permute-done.4
  114.1 0.0 collective-permute-done.2.far_a
  114.1 0.0 collective-permute-done.3.far_b
  114.1 7.4 %gram.1 = f32[2,2,256,1024]{3,2,1,0:T(8,128)} custom-call(s32[1]{0:T(128)} %bitcast.col, bf16[64,32,256]{2,1,0:T(8,128)(2,1)S(1)} %slice.16.own, bf16[64,32,256]{2,1,0:T(8,128)(2,1)S(1)} %collective-permute-done.right, bf16[64,32,256]{2,1,0:T(8,128)(2,1)S(1)} %collective-permute-done.1.left, bf16[32,32,256]{2,1,0:T(8,128)(2,1)} %collective-permute-done.2.far_a, ...), custom_call_target="tpu_custom_call" | custom-call | tf_op jit(solution)/shard_map/gram/pallas_call | solution.py:202
  (1 shorter events, 0.0 us)
Async XLA Ops:
  24.4 1.6 %copy-start = (f32[2,2048,128]{2,1,0:T(8,128)S(1)}, f32[2,2048,128]{2,1,0:T(8,128)}, u32[]{:S(2)}) copy-start(f32[2,2048,128]{2,1,0:T(8,128)} %get-tuple-element.7.spec) | copy-start | bytes 6291460
  71.7 26.6 %collective-permute-start.1 = (bf16[64,32,256]{2,1,0:T(8,128)(2,1)S(1)}, bf16[64,32,256]{2,1,0:T(8,128)(2,1)S(1)}, u32[]{:S(2)}, u32[]{:S(2)}) collective-permute-start(bf16[64,32,256]{2,1,0:T(8,128)(2,1)S(1)} %slice.16.own), channel_id=1, source_target_pairs={{0,1},{1,2},{2,3},{3,0},{4,5},{5,6},{6,7},{7,4},{8,9},{9,10},{10,1... | collective-permute-start | bytes 3145736 | tf_op jit(solution)/shard_map/ppermute | solution.py:179
  71.8 27.3 %collective-permute-start = (bf16[64,32,256]{2,1,0:T(8,128)(2,1)S(1)}, bf16[64,32,256]{2,1,0:T(8,128)(2,1)S(1)}, u32[]{:S(2)}, u32[]{:S(2)}) collective-permute-start(bf16[64,32,256]{2,1,0:T(8,128)(2,1)S(1)} %slice.16.own), channel_id=1, source_target_pairs={{0,3},{1,0},{2,1},{3,2},{4,7},{5,4},{6,5},{7,6},{8,11},{9,8},{10,9... | collective-permute-start | bytes 3145736 | tf_op jit(solution)/shard_map/ppermute | solution.py:180
  99.1 14.9 %collective-permute-start.2 = (bf16[32,32,256]{2,1,0:T(8,128)(2,1)}, bf16[32,32,256]{2,1,0:T(8,128)(2,1)}, u32[]{:S(2)}, u32[]{:S(2)}) collective-permute-start(bf16[32,32,256]{2,1,0:T(8,128)(2,1)} %slice.17), channel_id=1, source_target_pairs={{0,1},{1,2},{2,3},{3,0},{4,5},{5,6},{6,7},{7,4},{8,9},{9,10},{10,1... | collective-permute-start | bytes 1572872 | tf_op jit(solution)/shard_map/ppermute | solution.py:182
  100.0 14.1 %collective-permute-start.3 = (bf16[32,32,256]{2,1,0:T(8,128)(2,1)}, bf16[32,32,256]{2,1,0:T(8,128)(2,1)}, u32[]{:S(2)}, u32[]{:S(2)}) collective-permute-start(bf16[32,32,256]{2,1,0:T(8,128)(2,1)} %slice.18), channel_id=1, source_target_pairs={{0,3},{1,0},{2,1},{3,2},{4,7},{5,4},{6,5},{7,6},{8,11},{9,8},{10,9... | collective-permute-start | bytes 1572872 | tf_op jit(solution)/shard_map/ppermute | solution.py:183
  103.3 8.3 %collective-permute-start.6 = (f32[1,256]{1,0:T(1,128)S(1)}, f32[1,256]{1,0:T(1,128)S(1)}, u32[]{:S(2)}, u32[]{:S(2)}) collective-permute-start(f32[1,256]{1,0:T(1,128)S(1)} %bitcast.4), channel_id=1, source_target_pairs={{0,2},{1,3},{2,0},{3,1},{4,6},{5,7},{6,4},{7,5},{8,10},{9,11},{10,... | collective-permute-start | bytes 3080 | tf_op jit(solution)/shard_map/ppermute | solution.py:189
  103.4 10.5 %collective-permute-start.5 = (f32[1,256]{1,0:T(1,128)S(1)}, f32[1,256]{1,0:T(1,128)S(1)}, u32[]{:S(2)}, u32[]{:S(2)}) collective-permute-start(f32[1,256]{1,0:T(1,128)S(1)} %bitcast.5), channel_id=1, source_target_pairs={{0,1},{1,2},{2,3},{3,0},{4,5},{5,6},{6,7},{7,4},{8,9},{9,10},{10,1... | collective-permute-start | bytes 3080 | tf_op jit(solution)/shard_map/ppermute | solution.py:188
  104.2 9.8 %collective-permute-start.4 = (f32[1,256]{1,0:T(1,128)S(1)}, f32[1,256]{1,0:T(1,128)S(1)}, u32[]{:S(2)}, u32[]{:S(2)}) collective-permute-start(f32[1,256]{1,0:T(1,128)S(1)} %bitcast.6), channel_id=1, source_target_pairs={{0,3},{1,0},{2,1},{3,2},{4,7},{5,4},{6,5},{7,6},{8,11},{9,8},{10,9... | collective-permute-start | bytes 3080 | tf_op jit(solution)/shard_map/ppermute | solution.py:187

commit v2 on v0

v2 whole, which is shorter than its diff:
```python
import functools
import math

import jax
import jax.numpy as jnp
import numpy as np
from jax import lax
from jax.experimental import pallas as pl
from jax.experimental.pallas import tpu as pltpu
from jax.sharding import PartitionSpec as P

K0 = 32
BF = jnp.bfloat16
F32 = jnp.float32


def split_tables(samples, kept):
    half = samples // 2
    steps = np.arange(half, dtype=np.int64)
    tables = []
    for parity in range(2):
        freqs = K0 + np.arange(parity, kept, 2)
        angles = 2.0 * math.pi / samples * ((steps[:, None] * freqs[None, :]) % samples)
        exact = np.concatenate([np.cos(angles), -np.sin(angles)], axis=1).astype(np.float32)
        high = exact.astype(BF)
        low = (exact - high.astype(np.float32)).astype(BF)
        tables.append(np.concatenate([high, low], axis=1))
    return np.stack(tables)


def taper_window(samples):
    steps = np.arange(samples)
    return (0.5 - 0.5 * np.cos(2.0 * math.pi / samples * steps)).astype(np.float32)[None, :]


def dot(a, b):
    return jnp.dot(a, b, preferred_element_type=F32)


def spectra_kernel(records, taper, tables, even, odd, power, held, arrived):
    windows = records.shape[0]
    half = records.shape[2] // 2
    kept = tables.shape[2] // 2
    bins = kept // 2

    def fetch(w):
        return pltpu.make_async_copy(records.at[w], held.at[w], arrived.at[w])

    for w in range(windows):
        fetch(w).start()

    @pl.loop(0, windows)
    def _(w):
        fetch(w).wait()
        tapered = held[w] * taper[...]
        first, second = tapered[:, :half], tapered[:, half:]
        rows = []
        for parity, spec in enumerate((even, odd)):
            folded = first + second if parity == 0 else first - second
            high = folded.astype(BF)
            low = (folded - high.astype(F32)).astype(BF)
            both = dot(high, tables[parity])
            result = both[:, :kept] + both[:, kept:] + dot(low, tables[parity, :, :kept])
            square = jnp.sum(result * result, axis=0, keepdims=True)
            rows.append(square[:, :bins] + square[:, bins:])
            turned = jnp.transpose(result)
            for side in range(2):
                lanes = slice(128 * side, 128 * side + 128)
                spec[side, pl.ds(w, bins, stride=16), :] = turned[:bins, lanes]
                spec[side, pl.ds(8 + w, bins, stride=16), :] = turned[bins:, lanes]
        power[pl.ds(w, 1), :] = jnp.concatenate(rows, axis=1)


def whiten_kernel(channels, even, odd, p0, p1, p2, p3, weight, message, energy):
    bins = p0.shape[1] // 2
    power = (p0[...] + p1[...]) + (p2[...] + p3[...])
    factor = weight[...] / jnp.sqrt(power / channels + 1e-06)
    total = jnp.zeros((8, 256), F32)
    for owner in range(bins):
        for parity, spec in enumerate((even, odd)):
            lane = parity * bins + owner
            scale = factor[:, lane : lane + 1]
            start = owner * 16
            block = jnp.concatenate(
                [spec[0, start : start + 16, :], spec[1, start : start + 16, :]], axis=1
            )
            real = (block[:8] * scale).astype(BF).astype(F32)
            imag = (block[8:] * scale).astype(BF).astype(F32)
            total = total + (real * real + imag * imag)
            message[owner, parity * 16 : parity * 16 + 16, :] = jnp.concatenate(
                [real, imag], axis=0
            ).astype(BF)
    energy[...] = jnp.sum(total, axis=0, keepdims=True)


def flat(block):
    return block.reshape(block.shape[0] * block.shape[1], block.shape[2])


def left_side(own, lhs):
    chan = own.shape[2]
    turned = jnp.concatenate([own[:, 8:, :], -own[:, :8, :]], axis=1)
    lhs[:chan] = jnp.transpose(flat(own[...]))
    lhs[chan:] = jnp.transpose(flat(turned))


def emit(product, energy, which, scale, out):
    chan = product.shape[1]
    rows = lax.rsqrt(energy[0:1, :]) * scale
    cols = lax.rsqrt(energy[pl.ds(which, 1), :])
    weight = jnp.transpose(jnp.broadcast_to(rows, (8, chan)))[:, :1] * cols
    out[0, 0] = product[:chan] * weight
    out[1, 0] = product[chan:] * weight


def gram_near_kernel(scale, col, own, right_a, right_b, left_a, left_b, energy, out, lhs):
    step = pl.program_id(1)
    half = lhs.shape[2] // 2

    @pl.when(step == 0)
    def _():
        left_side(own, lhs.at[0])
        emit(dot(lhs[0], flat(own[...])), energy, 0, scale, out)

    for which, first, second in ((1, right_a, right_b), (2, left_a, left_b)):

        @pl.when(step == which)
        def _():
            product = dot(lhs[0, :, :half], flat(first[...]))
            product += dot(lhs[0, :, half:], flat(second[...]))
            emit(product, energy, which, scale, out)


def gram_far_kernel(scale, col, lhs, far_a, far_b, energy, kept, out):
    half = lhs.shape[2] // 2
    product = dot(lhs[0, :, :half], flat(far_a[...])) + dot(lhs[0, :, half:], flat(far_b[...]))
    emit(product, energy, 3, scale, out)


def ring(size, shift):
    return [(i, (i + shift) % size) for i in range(size)]


def body(owners, columns, records, bin_weight):
    windows, chan, samples = records.shape
    kept = bin_weight.shape[0]
    bins = kept // 2
    spec_shape = (2, bins * 16, 128)
    even, odd, power = pl.pallas_call(
        spectra_kernel,
        in_specs=[
            pl.BlockSpec(memory_space=pltpu.HBM),
            pl.BlockSpec(memory_space=pltpu.VMEM),
            pl.BlockSpec(memory_space=pltpu.VMEM),
        ],
        scratch_shapes=[
            pltpu.VMEM((windows, chan, samples), F32),
            pltpu.SemaphoreType.DMA((windows,)),
        ],
        out_shape=[
            jax.ShapeDtypeStruct(spec_shape, F32),
            jax.ShapeDtypeStruct(spec_shape, F32),
            jax.ShapeDtypeStruct((windows, kept), F32),
        ],
        compiler_params=pltpu.CompilerParams(vmem_limit_bytes=50 << 20),
        name="spectra",
    )(records, taper_window(samples), split_tables(samples, kept))
    ahead, back, across = ring(columns, 1), ring(columns, columns - 1), ring(columns, 2)
    powers = [power] + [lax.ppermute(power, "col", p) for p in (ahead, back, across)]
    weight = bin_weight.reshape(bins, 2).T.reshape(1, kept)
    message, energy = pl.pallas_call(
        functools.partial(whiten_kernel, chan * columns),
        out_shape=[
            jax.ShapeDtypeStruct((owners, 32, chan), BF),
            jax.ShapeDtypeStruct((1, chan), F32),
        ],
        compiler_params=pltpu.CompilerParams(vmem_limit_bytes=10 << 20),
        name="whiten",
    )(even, odd, *powers, weight)

    mine = lax.all_to_all(message, "wa", split_axis=0, concat_axis=0, tiled=True)
    energies = jnp.concatenate(
        [energy] + [lax.ppermute(energy, "col", p) for p in (back, ahead, across)], axis=0
    )

    def fold(value, step):
        return value + lax.ppermute(value, "wa", [(i, i ^ step) for i in range(owners)])

    for step in (1, 2, 4):
        energies = fold(energies, step)
    mine, energies = lax.optimization_barrier((mine, energies))

    half = owners // 2
    left_a = lax.ppermute(mine[:half], "col", ahead)
    right_b = lax.ppermute(mine[half:], "col", back)
    energies = fold(fold(energies, 8), 16)
    mine, left_a, right_b, energies = lax.optimization_barrier(
        (mine, left_a, right_b, energies)
    )
    left_b = lax.ppermute(mine[half:], "col", ahead)
    right_a = lax.ppermute(mine[:half], "col", back)
    far_a = lax.ppermute(left_a, "col", ahead)
    far_b = lax.ppermute(right_b, "col", back)
    energies = fold(energies, 32)

    col = lax.axis_index("col").astype(jnp.int32)[None]
    scale = math.sqrt(windows * owners) * kept
    out_shape = jax.ShapeDtypeStruct((2, 2, chan, chan * columns), F32)
    lhs_shape = (2, 2 * chan, 16 * owners)

    def where(s, c):
        shift = jnp.where(s == 2, 3, jnp.where(s == 3, 2, s))
        return lax.rem(c[0] + shift, columns)

    def bin_block(count):
        return pl.BlockSpec((count, 16, chan), lambda b, s, c: (0, b, 0))

    def out_block(first):
        return pl.BlockSpec((2, 1, chan, chan), lambda b, s, c: (0, b, 0, where(s + first, c)))

    energy_block = pl.BlockSpec((columns, chan), lambda b, s, c: (0, 0))
    lhs_block = pl.BlockSpec((1,) + lhs_shape[1:], lambda b, s, c: (b, 0, 0))
    params = pltpu.CompilerParams(vmem_limit_bytes=16 << 20)
    out, lhs = pl.pallas_call(
        functools.partial(gram_near_kernel, scale),
        grid_spec=pltpu.PrefetchScalarGridSpec(
            num_scalar_prefetch=1,
            grid=(2, 3),
            in_specs=[bin_block(owners)] + [bin_block(half)] * 4 + [energy_block],
            out_specs=[out_block(0), lhs_block],
        ),
        out_shape=[out_shape, jax.ShapeDtypeStruct(lhs_shape, BF)],
        compiler_params=params,
        cost_estimate=pl.CostEstimate(
            flops=24 * chan * chan * 16 * owners, bytes_accessed=8 << 20, transcendentals=0
        ),
        name="gram_near",
    )(col, mine, right_a, right_b, left_a, left_b, energies)
    return pl.pallas_call(
        functools.partial(gram_far_kernel, scale),
        grid_spec=pltpu.PrefetchScalarGridSpec(
            num_scalar_prefetch=1,
            grid=(2, 1),
            in_specs=[lhs_block, bin_block(half), bin_block(half), energy_block]
            + [pl.BlockSpec(memory_space=pl.ANY)],
            out_specs=out_block(3),
        ),
        out_shape=out_shape,
        input_output_aliases={5: 0},
        compiler_params=params,
        cost_estimate=pl.CostEstimate(
            flops=8 * chan * chan * 16 * owners, bytes_accessed=4 << 20, transcendentals=0
        ),
        name="gram_far",
    )(col, lhs, far_a, far_b, energies, out)


def solution(mesh):
    owners, columns = mesh.shape["wa"], mesh.shape["col"]
    return jax.shard_map(
        functools.partial(body, owners, columns),
        mesh=mesh,
        in_specs=(P("wa", "col", None), P()),
        out_specs=P(None, "wa", "col", None),
        check_vma=False,
    )
```

time: 347 us -> 103 us (0.30)
  the two profiles are of different devices: /device:TPU:128 before, /device:TPU:32 now
where the time goes in v2:
time: 103 us
  waiting for transfers between devices  44 us (43%)
  starting transfers between devices  39.6 us (38%)
  Pallas kernels  16 us (16%)
  local copies, waits for them, and re-layouts  3.13 us (3%)
    ppermute x6, waiting for transfers between devices, fold(): lax.ppermute(value, 'wa', [(i, i ^ step) for i in range(owners)])  14.3 us
    all_to_all x1, waiting for transfers between devices, body(): lax.all_to_all(message, 'wa', split_axis=0, concat_axis=0, tiled=True)  12.3 us
    all_to_all x1, starting transfers between devices, body(): lax.all_to_all(message, 'wa', split_axis=0, concat_axis=0, tiled=True)  11.8 us
    ppermute x6, starting transfers between devices, fold(): lax.ppermute(value, 'wa', [(i, i ^ step) for i in range(owners)])  11.7 us
    pallas_call x1, Pallas kernels, body(): pl.pallas_call(spectra_kernel, in_specs=[pl.BlockSpec(memory_space=pltpu....  6.46 us
    pallas_call x1, Pallas kernels, body(): pl.pallas_call(functools.partial(gram_near_kernel, scale), grid_spec=pltp...  6.14 us
    ppermute x3, starting transfers between devices, body(): lax.ppermute(power, 'col', p)  5.14 us
    ppermute x1, waiting for transfers between devices, body(): right_b = lax.ppermute(mine[half:], 'col', back)  3.93 us
  transfers between devices with their start and end apart: 19, of which 15 were waited for; matrix products, arithmetic and copies ran while one was open for 0% of the time, Pallas kernels for 6%

profile of v2, /device:TPU:32, one launch (start us, length us, event | category | flops | bytes accessed | tf_op | source)
XLA Modules:
  0.0 102.8 jit_solution(15333788233685157704)
XLA Ops:
  0.0 1.0 %copy-done = bf16[2,512,256]{2,1,0:T(8,128)(2,1)S(1)} copy-done((bf16[2,512,256]{2,1,0:T(8,128)(2,1)S(1)}, bf16[2,512,256]{2,1,0:T(8,128)(2,1)}, u32[]{:S(2)}) %copy-start) | copy-done | bytes 524312
  1.7 6.5 %spectra.1 = (f32[2,1024,128]{2,1,0:T(8,128)S(1)}, f32[2,1024,128]{2,1,0:T(8,128)S(1)}, f32[8,128]{1,0:T(8,128)S(1)}) custom-call(f32[8,256,1024]{2,1,0:T(8,128)} %records.1, f32[1,1024]{1,0:T(1,128)S(1)} %copy-done.1, bf16[2,512,256]{2,1,0:T(8,128)(2,1)S(1)} %copy-done), custom_call_target="tpu_custom_call" | custom-call | tf_op jit(solution)/shard_map/spectra/pallas_call | solution.py:149
  8.2 3.1 %collective-permute-start.2 = (f32[8,128]{1,0:T(8,128)S(1)}, f32[8,128]{1,0:T(8,128)S(1)}, u32[]{:S(2)}, u32[]{:S(2)}) collective-permute-start(f32[8,128]{1,0:T(8,128)S(1)} %get-tuple-element.20.p0), channel_id=1, source_target_pairs={{0,2},{1,3},{2,0},{3,1},{4,6},{5,7},{6,4},{7,5},{8,10},{9,11},{10,... | collective-permute-start | bytes 12296 | tf_op jit(solution)/shard_map/ppermute | solution.py:169
  11.3 1.1 %collective-permute-start.1 = (f32[8,128]{1,0:T(8,128)S(1)}, f32[8,128]{1,0:T(8,128)S(1)}, u32[]{:S(2)}, u32[]{:S(2)}) collective-permute-start(f32[8,128]{1,0:T(8,128)S(1)} %get-tuple-element.20.p0), channel_id=1, source_target_pairs={{0,3},{1,0},{2,1},{3,2},{4,7},{5,4},{6,5},{7,6},{8,11},{9,8},{10,9... | collective-permute-start | bytes 12296 | tf_op jit(solution)/shard_map/ppermute | solution.py:169
  13.6 1.3 %collective-permute-done.1.p2 = f32[8,128]{1,0:T(8,128)S(1)} collective-permute-done((f32[8,128]{1,0:T(8,128)S(1)}, f32[8,128]{1,0:T(8,128)S(1)}, u32[]{:S(2)}, u32[]{:S(2)}) %collective-permute-start.1) | collective-permute-done | bytes 4128 | tf_op jit(solution)/shard_map/ppermute | solution.py:169
  14.9 2.4 %collective-permute-done.p1 = f32[8,128]{1,0:T(8,128)S(1)} collective-permute-done((f32[8,128]{1,0:T(8,128)S(1)}, f32[8,128]{1,0:T(8,128)S(1)}, u32[]{:S(2)}, u32[]{:S(2)}) %collective-permute-start) | collective-permute-done | bytes 4128 | tf_op jit(solution)/shard_map/ppermute | solution.py:169
  17.3 1.4 %whiten.1 = (bf16[64,32,256]{2,1,0:T(8,128)(2,1)}, f32[1,256]{1,0:T(1,128)S(1)}) custom-call(f32[2,1024,128]{2,1,0:T(8,128)S(1)} %get-tuple-element.18.even, f32[2,1024,128]{2,1,0:T(8,128)S(1)} %get-tuple-element.19.odd, f32[8,128]{1,0:T(8,128)S(1)} %get-tuple-element.20.p0, f32[8,128]{1,0:T(8,128)S(1)} %collective-permute-done.p1, ...), custom_call_target="tpu_custom_call" | custom-call | tf_op jit(solution)/shard_map/whiten/pallas_call | solution.py:171
  18.7 11.8 %all-to-all-start = ((bf16[64,32,256]{2,1,0:T(8,128)(2,1)}), bf16[64,32,256]{2,1,0:T(8,128)(2,1)S(1)}, u32[]{:S(2)}, u32[]{:S(2)}) async-start(bf16[64,32,256]{2,1,0:T(8,128)(2,1)} %get-tuple-element.21), calls=%async_computation | async-start | bytes 2097152 | tf_op jit(solution)/shard_map/all_to_all | solution.py:181
  31.4 2.7 %collective-permute-start.3 = (f32[1,256]{1,0:T(1,128)S(1)}, f32[1,256]{1,0:T(1,128)S(1)}, u32[]{:S(2)}, u32[]{:S(2)}) collective-permute-start(f32[1,256]{1,0:T(1,128)S(1)} %get-tuple-element.22), channel_id=1, source_target_pairs={{0,3},{1,0},{2,1},{3,2},{4,7},{5,4},{6,5},{7,6},{8,11},{9,8},{10,9... | collective-permute-start | bytes 3080 | tf_op jit(solution)/shard_map/ppermute | solution.py:183
  34.1 1.5 %collective-permute-done.5 = f32[1,256]{1,0:T(1,128)S(1)} collective-permute-done((f32[1,256]{1,0:T(1,128)S(1)}, f32[1,256]{1,0:T(1,128)S(1)}, u32[]{:S(2)}, u32[]{:S(2)}) %collective-permute-start.5) | collective-permute-done | bytes 1056 | tf_op jit(solution)/shard_map/ppermute | solution.py:183
  35.8 1.2 %collective-permute-done.6 = f32[4,256]{1,0:T(4,128)S(1)} collective-permute-done((f32[4,256]{1,0:T(4,128)S(1)}, f32[4,256]{1,0:T(4,128)S(1)}, u32[]{:S(2)}, u32[]{:S(2)}) %collective-permute-start.6) | collective-permute-done | bytes 4128 | tf_op jit(solution)/shard_map/ppermute | solution.py:187
  36.9 1.6 %collective-permute-start.7 = (f32[4,256]{1,0:T(4,128)S(1)}, f32[4,256]{1,0:T(4,128)S(1)}, u32[]{:S(2)}, u32[]{:S(2)}) collective-permute-start(f32[4,256]{1,0:T(4,128)S(1)} %fusion), channel_id=1, source_target_pairs={{0,8},{4,12},{8,0},{12,4},{16,24},{20,28},{24,16},{28,20},{32,40},... | collective-permute-start | bytes 12296 | tf_op jit(solution)/shard_map/ppermute | solution.py:187
  38.5 2.2 %collective-permute-done.7 = f32[4,256]{1,0:T(4,128)S(1)} collective-permute-done((f32[4,256]{1,0:T(4,128)S(1)}, f32[4,256]{1,0:T(4,128)S(1)}, u32[]{:S(2)}, u32[]{:S(2)}) %collective-permute-start.7) | collective-permute-done | bytes 4128 | tf_op jit(solution)/shard_map/ppermute | solution.py:187
  40.7 3.1 %collective-permute-start.8 = (f32[4,256]{1,0:T(4,128)S(1)}, f32[4,256]{1,0:T(4,128)S(1)}, u32[]{:S(2)}, u32[]{:S(2)}) collective-permute-start(f32[4,256]{1,0:T(4,128)S(1)} %fusion.3), channel_id=1, source_target_pairs={{0,16},{4,20},{8,24},{12,28},{16,0},{20,4},{24,8},{28,12},{32,48},... | collective-permute-start | bytes 12296 | tf_op jit(solution)/shard_map/ppermute | solution.py:187
  43.7 2.4 %collective-permute-done.8 = f32[4,256]{1,0:T(4,128)S(1)} collective-permute-done((f32[4,256]{1,0:T(4,128)S(1)}, f32[4,256]{1,0:T(4,128)S(1)}, u32[]{:S(2)}, u32[]{:S(2)}) %collective-permute-start.8) | collective-permute-done | bytes 4128 | tf_op jit(solution)/shard_map/ppermute | solution.py:187
  46.1 12.3 %all-to-all-done.own = bf16[64,32,256]{2,1,0:T(8,128)(2,1)S(1)} async-done(((bf16[64,32,256]{2,1,0:T(8,128)(2,1)}), bf16[64,32,256]{2,1,0:T(8,128)(2,1)S(1)}, u32[]{:S(2)}, u32[]{:S(2)}) %all-to-all-start) | async-done | bytes 1048608 | tf_op jit(solution)/shard_map/all_to_all | solution.py:181
  58.6 2.0 %collective-permute-start.9 = (bf16[32,32,256]{2,1,0:T(8,128)(2,1)S(1)}, bf16[32,32,256]{2,1,0:T(8,128)(2,1)S(1)}, u32[]{:S(2)}, u32[]{:S(2)}) collective-permute-start(bf16[32,32,256]{2,1,0:T(8,128)(2,1)S(1)} %get-tuple-element.34), channel_id=1, source_target_pairs={{0,1},{1,2},{2,3},{3,0},{4,5},{5,6},{6,7},{7,4},{8,9},{9,10},{10,1... | collective-permute-start | bytes 1572872 | tf_op jit(solution)/shard_map/ppermute | solution.py:194
  60.6 1.4 %collective-permute-start.11 = (f32[4,256]{1,0:T(4,128)S(1)}, f32[4,256]{1,0:T(4,128)S(1)}, u32[]{:S(2)}, u32[]{:S(2)}) collective-permute-start(f32[4,256]{1,0:T(4,128)S(1)} %add.20), channel_id=1, source_target_pairs={{0,32},{4,36},{8,40},{12,44},{16,48},{20,52},{24,56},{28,60},{32,0... | collective-permute-start | bytes 12296 | tf_op jit(solution)/shard_map/ppermute | solution.py:187
  62.0 2.2 %collective-permute-done.11 = f32[4,256]{1,0:T(4,128)S(1)} collective-permute-done((f32[4,256]{1,0:T(4,128)S(1)}, f32[4,256]{1,0:T(4,128)S(1)}, u32[]{:S(2)}, u32[]{:S(2)}) %collective-permute-start.11) | collective-permute-done | bytes 4128 | tf_op jit(solution)/shard_map/ppermute | solution.py:187
  64.2 2.6 %collective-permute-start.12 = (f32[4,256]{1,0:T(4,128)S(1)}, f32[4,256]{1,0:T(4,128)S(1)}, u32[]{:S(2)}, u32[]{:S(2)}) collective-permute-start(f32[4,256]{1,0:T(4,128)S(1)} %add.21), channel_id=1, source_target_pairs={{0,64},{4,68},{8,72},{12,76},{16,80},{20,84},{24,88},{28,92},{32,9... | collective-permute-start | bytes 12296 | tf_op jit(solution)/shard_map/ppermute | solution.py:187
  66.8 1.9 %collective-permute-done.12 = f32[4,256]{1,0:T(4,128)S(1)} collective-permute-done((f32[4,256]{1,0:T(4,128)S(1)}, f32[4,256]{1,0:T(4,128)S(1)}, u32[]{:S(2)}, u32[]{:S(2)}) %collective-permute-start.12) | collective-permute-done | bytes 4128 | tf_op jit(solution)/shard_map/ppermute | solution.py:187
  68.7 3.9 %collective-permute-done.10.right_b = bf16[32,32,256]{2,1,0:T(8,128)(2,1)S(1)} collective-permute-done((bf16[32,32,256]{2,1,0:T(8,128)(2,1)S(1)}, bf16[32,32,256]{2,1,0:T(8,128)(2,1)S(1)}, u32[]{:S(2)}, u32[]{:S(2)}) %collective-permute-start.10) | collective-permute-done | bytes 524320 | tf_op jit(solution)/shard_map/ppermute | solution.py:195
  72.6 1.3 %collective-permute-done.9.left_a = bf16[32,32,256]{2,1,0:T(8,128)(2,1)S(1)} collective-permute-done((bf16[32,32,256]{2,1,0:T(8,128)(2,1)S(1)}, bf16[32,32,256]{2,1,0:T(8,128)(2,1)S(1)}, u32[]{:S(2)}, u32[]{:S(2)}) %collective-permute-start.9) | collective-permute-done | bytes 524320 | tf_op jit(solution)/shard_map/ppermute | solution.py:194
  73.9 1.1 %fusion.1 = (bf16[32,32,256]{2,1,0:T(8,128)(2,1)}, bf16[32,32,256]{2,1,0:T(8,128)(2,1)}) fusion(bf16[64,32,256]{2,1,0:T(8,128)(2,1)S(1)} %all-to-all-done.own), kind=kLoop, calls=%fused_computation.2 | loop fusion | bytes 2097152 | tf_op jit(solution)/shard_map/slice | solution.py:200
  75.4 2.8 %collective-permute-start.13 = (bf16[32,32,256]{2,1,0:T(8,128)(2,1)}, bf16[32,32,256]{2,1,0:T(8,128)(2,1)}, u32[]{:S(2)}, u32[]{:S(2)}) collective-permute-start(bf16[32,32,256]{2,1,0:T(8,128)(2,1)} %get-tuple-element.32), channel_id=1, source_target_pairs={{0,3},{1,0},{2,1},{3,2},{4,7},{5,4},{6,5},{7,6},{8,11},{9,8},{10,9... | collective-permute-start | bytes 1572872 | tf_op jit(solution)/shard_map/ppermute | solution.py:201
  78.3 2.0 %collective-permute-start.16 = (bf16[32,32,256]{2,1,0:T(8,128)(2,1)S(1)}, bf16[32,32,256]{2,1,0:T(8,128)(2,1)S(1)}, u32[]{:S(2)}, u32[]{:S(2)}) collective-permute-start(bf16[32,32,256]{2,1,0:T(8,128)(2,1)S(1)} %collective-permute-done.9.left_a), channel_id=1, source_target_pairs={{0,1},{1,2},{2,3},{3,0},{4,5},{5,6},{6,7},{7,4},{8,9},{9,10},{10,1... | collective-permute-start | bytes 1572872 | tf_op jit(solution)/shard_map/ppermute | solution.py:202
  80.3 3.0 %collective-permute-start.15 = (f32[4,256]{1,0:T(4,128)S(1)}, f32[4,256]{1,0:T(4,128)S(1)}, u32[]{:S(2)}, u32[]{:S(2)}) collective-permute-start(f32[4,256]{1,0:T(4,128)S(1)} %add.22), channel_id=1, source_target_pairs={{0,128},{4,132},{8,136},{12,140},{16,144},{20,148},{24,152},{28,15... | collective-permute-start | bytes 12296 | tf_op jit(solution)/shard_map/ppermute | solution.py:187
  83.2 4.5 %collective-permute-done.15 = f32[4,256]{1,0:T(4,128)S(1)} collective-permute-done((f32[4,256]{1,0:T(4,128)S(1)}, f32[4,256]{1,0:T(4,128)S(1)}, u32[]{:S(2)}, u32[]{:S(2)}) %collective-permute-start.15) | collective-permute-done | bytes 4128 | tf_op jit(solution)/shard_map/ppermute | solution.py:187
  87.8 3.6 %collective-permute-done.14.left_b = bf16[32,32,256]{2,1,0:T(8,128)(2,1)} collective-permute-done((bf16[32,32,256]{2,1,0:T(8,128)(2,1)}, bf16[32,32,256]{2,1,0:T(8,128)(2,1)}, u32[]{:S(2)}, u32[]{:S(2)}) %collective-permute-start.14) | collective-permute-done | bytes 524320 | tf_op jit(solution)/shard_map/ppermute | solution.py:200
  91.4 6.1 %gram_near.1 = (f32[2,2,256,1024]{3,2,1,0:T(8,128)}, bf16[2,512,1024]{2,1,0:T(8,128)(2,1)S(1)}) custom-call(s32[1]{0:T(128)} %bitcast.col, bf16[64,32,256]{2,1,0:T(8,128)(2,1)S(1)} %all-to-all-done.own, bf16[32,32,256]{2,1,0:T(8,128)(2,1)} %collective-permute-done.13.right_a, bf16[32,32,256]{2,1,0:T(8,128)(2,1)S(1)} %collective-permute-done.10.right_b, ...), custom_call_target="tpu_custom_call" | custom-call | flops 1610612736 | bytes 8388608 | tf_op jit(solution)/shard_map/gram_near/pallas_call | solution.py:224
  97.5 2.7 %collective-permute-done.17.far_b = bf16[32,32,256]{2,1,0:T(8,128)(2,1)S(1)} collective-permute-done((bf16[32,32,256]{2,1,0:T(8,128)(2,1)S(1)}, bf16[32,32,256]{2,1,0:T(8,128)(2,1)S(1)}, u32[]{:S(2)}, u32[]{:S(2)}) %collective-permute-start.17) | collective-permute-done | bytes 524320 | tf_op jit(solution)/shard_map/ppermute | solution.py:203
  100.9 1.9 %gram_far.1 = f32[2,2,256,1024]{3,2,1,0:T(8,128)} custom-call(s32[1]{0:T(128)} %bitcast.col, bf16[2,512,1024]{2,1,0:T(8,128)(2,1)S(1)} %get-tuple-element.29.lhs, bf16[32,32,256]{2,1,0:T(8,128)(2,1)S(1)} %collective-permute-done.16.far_a, bf16[32,32,256]{2,1,0:T(8,128)(2,1)S(1)} %collective-permute-done.17.far_b, ...), custom_call_target="tpu_custom_call", output_to_operand_aliasing={{}: (5, {})} | custom-call | flops 536870912 | bytes 4194304 | tf_op jit(solution)/shard_map/gram_far/pallas_call | solution.py:239
  (28 shorter events, 4.3 us)
Async XLA Ops:
  0.0 1.0 %copy-start = (bf16[2,512,256]{2,1,0:T(8,128)(2,1)S(1)}, bf16[2,512,256]{2,1,0:T(8,128)(2,1)}, u32[]{:S(2)}) copy-start(bf16[2,512,256]{2,1,0:T(8,128)(2,1)} %constant.9.clone.tables) | copy-start | bytes 1572868
  1.0 0.7 copy-start.1
  1.7 11.6 %copy-start.2 = (f32[128]{0:T(128)S(1)}, f32[128]{0:T(128)}, u32[]{:S(2)}) copy-start(f32[128]{0:T(128)} %param.5) | copy-start | bytes 1540
  8.2 5.4 %collective-permute-start.2 = (f32[8,128]{1,0:T(8,128)S(1)}, f32[8,128]{1,0:T(8,128)S(1)}, u32[]{:S(2)}, u32[]{:S(2)}) collective-permute-start(f32[8,128]{1,0:T(8,128)S(1)} %get-tuple-element.20.p0), channel_id=1, source_target_pairs={{0,2},{1,3},{2,0},{3,1},{4,6},{5,7},{6,4},{7,5},{8,10},{9,11},{10,... | collective-permute-start | bytes 12296 | tf_op jit(solution)/shard_map/ppermute | solution.py:169
  11.3 3.6 %collective-permute-start.1 = (f32[8,128]{1,0:T(8,128)S(1)}, f32[8,128]{1,0:T(8,128)S(1)}, u32[]{:S(2)}, u32[]{:S(2)}) collective-permute-start(f32[8,128]{1,0:T(8,128)S(1)} %get-tuple-element.20.p0), channel_id=1, source_target_pairs={{0,3},{1,0},{2,1},{3,2},{4,7},{5,4},{6,5},{7,6},{8,11},{9,8},{10,9... | collective-permute-start | bytes 12296 | tf_op jit(solution)/shard_map/ppermute | solution.py:169
  12.5 4.8 %collective-permute-start = (f32[8,128]{1,0:T(8,128)S(1)}, f32[8,128]{1,0:T(8,128)S(1)}, u32[]{:S(2)}, u32[]{:S(2)}) collective-permute-start(f32[8,128]{1,0:T(8,128)S(1)} %get-tuple-element.20.p0), channel_id=1, source_target_pairs={{0,1},{1,2},{2,3},{3,0},{4,5},{5,6},{6,7},{7,4},{8,9},{9,10},{10,1... | collective-permute-start | bytes 12296 | tf_op jit(solution)/shard_map/ppermute | solution.py:169
  18.7 39.7 %all-to-all-start = ((bf16[64,32,256]{2,1,0:T(8,128)(2,1)}), bf16[64,32,256]{2,1,0:T(8,128)(2,1)S(1)}, u32[]{:S(2)}, u32[]{:S(2)}) async-start(bf16[64,32,256]{2,1,0:T(8,128)(2,1)} %get-tuple-element.21), calls=%async_computation | async-start | bytes 2097152 | tf_op jit(solution)/shard_map/all_to_all | solution.py:181
  30.5 5.2 %collective-permute-start.5 = (f32[1,256]{1,0:T(1,128)S(1)}, f32[1,256]{1,0:T(1,128)S(1)}, u32[]{:S(2)}, u32[]{:S(2)}) collective-permute-start(f32[1,256]{1,0:T(1,128)S(1)} %get-tuple-element.22), channel_id=1, source_target_pairs={{0,2},{1,3},{2,0},{3,1},{4,6},{5,7},{6,4},{7,5},{8,10},{9,11},{10,... | collective-permute-start | bytes 3080 | tf_op jit(solution)/shard_map/ppermute | solution.py:183
  30.9 4.8 %collective-permute-start.4 = (f32[1,256]{1,0:T(1,128)S(1)}, f32[1,256]{1,0:T(1,128)S(1)}, u32[]{:S(2)}, u32[]{:S(2)}) collective-permute-start(f32[1,256]{1,0:T(1,128)S(1)} %get-tuple-element.22), channel_id=1, source_target_pairs={{0,1},{1,2},{2,3},{3,0},{4,5},{5,6},{6,7},{7,4},{8,9},{9,10},{10,1... | collective-permute-start | bytes 3080 | tf_op jit(solution)/shard_map/ppermute | solution.py:183
  31.4 4.2 %collective-permute-start.3 = (f32[1,256]{1,0:T(1,128)S(1)}, f32[1,256]{1,0:T(1,128)S(1)}, u32[]{:S(2)}, u32[]{:S(2)}) collective-permute-start(f32[1,256]{1,0:T(1,128)S(1)} %get-tuple-element.22), channel_id=1, source_target_pairs={{0,3},{1,0},{2,1},{3,2},{4,7},{5,4},{6,5},{7,6},{8,11},{9,8},{10,9... | collective-permute-start | bytes 3080 | tf_op jit(solution)/shard_map/ppermute | solution.py:183
  35.7 1.3 %collective-permute-start.6 = (f32[4,256]{1,0:T(4,128)S(1)}, f32[4,256]{1,0:T(4,128)S(1)}, u32[]{:S(2)}, u32[]{:S(2)}) collective-permute-start(f32[4,256]{1,0:T(4,128)S(1)} %pad_maximum_fusion), channel_id=1, source_target_pairs={{0,4},{4,0},{8,12},{12,8},{16,20},{20,16},{24,28},{28,24},{32,36},... | collective-permute-start | bytes 12296 | tf_op jit(solution)/shard_map/ppermute | solution.py:187
  36.9 3.7 %collective-permute-start.7 = (f32[4,256]{1,0:T(4,128)S(1)}, f32[4,256]{1,0:T(4,128)S(1)}, u32[]{:S(2)}, u32[]{:S(2)}) collective-permute-start(f32[4,256]{1,0:T(4,128)S(1)} %fusion), channel_id=1, source_target_pairs={{0,8},{4,12},{8,0},{12,4},{16,24},{20,28},{24,16},{28,20},{32,40},... | collective-permute-start | bytes 12296 | tf_op jit(solution)/shard_map/ppermute | solution.py:187
  40.7 5.4 %collective-permute-start.8 = (f32[4,256]{1,0:T(4,128)S(1)}, f32[4,256]{1,0:T(4,128)S(1)}, u32[]{:S(2)}, u32[]{:S(2)}) collective-permute-start(f32[4,256]{1,0:T(4,128)S(1)} %fusion.3), channel_id=1, source_target_pairs={{0,16},{4,20},{8,24},{12,28},{16,0},{20,4},{24,8},{28,12},{32,48},... | collective-permute-start | bytes 12296 | tf_op jit(solution)/shard_map/ppermute | solution.py:187
  58.5 14.2 %collective-permute-start.10 = (bf16[32,32,256]{2,1,0:T(8,128)(2,1)S(1)}, bf16[32,32,256]{2,1,0:T(8,128)(2,1)S(1)}, u32[]{:S(2)}, u32[]{:S(2)}) collective-permute-start(bf16[32,32,256]{2,1,0:T(8,128)(2,1)S(1)} %get-tuple-element.33), channel_id=1, source_target_pairs={{0,3},{1,0},{2,1},{3,2},{4,7},{5,4},{6,5},{7,6},{8,11},{9,8},{10,9... | collective-permute-start | bytes 1572872 | tf_op jit(solution)/shard_map/ppermute | solution.py:195
  58.6 15.4 %collective-permute-start.9 = (bf16[32,32,256]{2,1,0:T(8,128)(2,1)S(1)}, bf16[32,32,256]{2,1,0:T(8,128)(2,1)S(1)}, u32[]{:S(2)}, u32[]{:S(2)}) collective-permute-start(bf16[32,32,256]{2,1,0:T(8,128)(2,1)S(1)} %get-tuple-element.34), channel_id=1, source_target_pairs={{0,1},{1,2},{2,3},{3,0},{4,5},{5,6},{6,7},{7,4},{8,9},{9,10},{10,1... | collective-permute-start | bytes 1572872 | tf_op jit(solution)/shard_map/ppermute | solution.py:194
  60.6 3.6 %collective-permute-start.11 = (f32[4,256]{1,0:T(4,128)S(1)}, f32[4,256]{1,0:T(4,128)S(1)}, u32[]{:S(2)}, u32[]{:S(2)}) collective-permute-start(f32[4,256]{1,0:T(4,128)S(1)} %add.20), channel_id=1, source_target_pairs={{0,32},{4,36},{8,40},{12,44},{16,48},{20,52},{24,56},{28,60},{32,0... | collective-permute-start | bytes 12296 | tf_op jit(solution)/shard_map/ppermute | solution.py:187
  64.2 4.5 %collective-permute-start.12 = (f32[4,256]{1,0:T(4,128)S(1)}, f32[4,256]{1,0:T(4,128)S(1)}, u32[]{:S(2)}, u32[]{:S(2)}) collective-permute-start(f32[4,256]{1,0:T(4,128)S(1)} %add.21), channel_id=1, source_target_pairs={{0,64},{4,68},{8,72},{12,76},{16,80},{20,84},{24,88},{28,92},{32,9... | collective-permute-start | bytes 12296 | tf_op jit(solution)/shard_map/ppermute | solution.py:187
  75.0 16.4 %collective-permute-start.14 = (bf16[32,32,256]{2,1,0:T(8,128)(2,1)}, bf16[32,32,256]{2,1,0:T(8,128)(2,1)}, u32[]{:S(2)}, u32[]{:S(2)}) collective-permute-start(bf16[32,32,256]{2,1,0:T(8,128)(2,1)} %get-tuple-element.31), channel_id=1, source_target_pairs={{0,1},{1,2},{2,3},{3,0},{4,5},{5,6},{6,7},{7,4},{8,9},{9,10},{10,1... | collective-permute-start | bytes 1572872 | tf_op jit(solution)/shard_map/ppermute | solution.py:200
  75.4 15.9 %collective-permute-start.13 = (bf16[32,32,256]{2,1,0:T(8,128)(2,1)}, bf16[32,32,256]{2,1,0:T(8,128)(2,1)}, u32[]{:S(2)}, u32[]{:S(2)}) collective-permute-start(bf16[32,32,256]{2,1,0:T(8,128)(2,1)} %get-tuple-element.32), channel_id=1, source_target_pairs={{0,3},{1,0},{2,1},{3,2},{4,7},{5,4},{6,5},{7,6},{8,11},{9,8},{10,9... | collective-permute-start | bytes 1572872 | tf_op jit(solution)/shard_map/ppermute | solution.py:201
  78.2 21.9 %collective-permute-start.17 = (bf16[32,32,256]{2,1,0:T(8,128)(2,1)S(1)}, bf16[32,32,256]{2,1,0:T(8,128)(2,1)S(1)}, u32[]{:S(2)}, u32[]{:S(2)}) collective-permute-start(bf16[32,32,256]{2,1,0:T(8,128)(2,1)S(1)} %collective-permute-done.10.right_b), channel_id=1, source_target_pairs={{0,3},{1,0},{2,1},{3,2},{4,7},{5,4},{6,5},{7,6},{8,11},{9,8},{10,9... | collective-permute-start | bytes 1572872 | tf_op jit(solution)/shard_map/ppermute | solution.py:203
  78.3 22.6 %collective-permute-start.16 = (bf16[32,32,256]{2,1,0:T(8,128)(2,1)S(1)}, bf16[32,32,256]{2,1,0:T(8,128)(2,1)S(1)}, u32[]{:S(2)}, u32[]{:S(2)}) collective-permute-start(bf16[32,32,256]{2,1,0:T(8,128)(2,1)S(1)} %collective-permute-done.9.left_a), channel_id=1, source_target_pairs={{0,1},{1,2},{2,3},{3,0},{4,5},{5,6},{6,7},{7,4},{8,9},{9,10},{10,1... | collective-permute-start | bytes 1572872 | tf_op jit(solution)/shard_map/ppermute | solution.py:202
  80.3 7.5 %collective-permute-start.15 = (f32[4,256]{1,0:T(4,128)S(1)}, f32[4,256]{1,0:T(4,128)S(1)}, u32[]{:S(2)}, u32[]{:S(2)}) collective-permute-start(f32[4,256]{1,0:T(4,128)S(1)} %add.22), channel_id=1, source_target_pairs={{0,128},{4,132},{8,136},{12,140},{16,144},{20,148},{24,152},{28,15... | collective-permute-start | bytes 12296 | tf_op jit(solution)/shard_map/ppermute | solution.py:187

commit v3 on v2

--- a/solution.py
+++ b/solution.py
@@ -28,18 +28,13 @@
     return np.stack(tables)
 
 
-def taper_window(samples):
-    steps = np.arange(samples)
-    return (0.5 - 0.5 * np.cos(2.0 * math.pi / samples * steps)).astype(np.float32)[None, :]
-
-
 def dot(a, b):
     return jnp.dot(a, b, preferred_element_type=F32)
 
 
-def spectra_kernel(records, taper, tables, even, odd, power, held, arrived):
-    windows = records.shape[0]
-    half = records.shape[2] // 2
+def spectra_kernel(records, tables, even, odd, power, held, results, arrived):
+    windows, _, samples = records.shape
+    half = samples // 2
     kept = tables.shape[2] // 2
     bins = kept // 2
 
@@ -48,27 +43,32 @@
 
     for w in range(windows):
         fetch(w).start()
-
-    @pl.loop(0, windows)
-    def _(w):
-        fetch(w).wait()
-        tapered = held[w] * taper[...]
-        first, second = tapered[:, :half], tapered[:, half:]
-        rows = []
-        for parity, spec in enumerate((even, odd)):
-            folded = first + second if parity == 0 else first - second
-            high = folded.astype(BF)
-            low = (folded - high.astype(F32)).astype(BF)
-            both = dot(high, tables[parity])
-            result = both[:, :kept] + both[:, kept:] + dot(low, tables[parity, :, :kept])
-            square = jnp.sum(result * result, axis=0, keepdims=True)
-            rows.append(square[:, :bins] + square[:, bins:])
-            turned = jnp.transpose(result)
-            for side in range(2):
-                lanes = slice(128 * side, 128 * side + 128)
-                spec[side, pl.ds(w, bins, stride=16), :] = turned[:bins, lanes]
-                spec[side, pl.ds(8 + w, bins, stride=16), :] = turned[bins:, lanes]
-        power[pl.ds(w, 1), :] = jnp.concatenate(rows, axis=1)
+    steps = lax.broadcasted_iota(jnp.int32, (1, samples), 1).astype(F32)
+    taper = 0.5 - 0.5 * jnp.cos(steps * (2.0 * math.pi / samples))
+
+    for w in range(windows + 1):
+        if w < windows:
+            fetch(w).wait()
+            tapered = held[w] * taper
+            first, second = tapered[:, :half], tapered[:, half:]
+            rows = []
+            for parity in range(2):
+                folded = first + second if parity == 0 else first - second
+                high = folded.astype(BF)
+                low = (folded - high.astype(F32)).astype(BF)
+                both = dot(high, tables[parity])
+                result = both[:, :kept] + both[:, kept:] + dot(low, tables[parity, :, :kept])
+                results[w % 2, parity] = result
+                square = jnp.sum(result * result, axis=0, keepdims=True)
+                rows.append(square[:, :bins] + square[:, bins:])
+            power[w : w + 1, :] = jnp.concatenate(rows, axis=1)
+        if w > 0:
+            for parity, spec in enumerate((even, odd)):
+                turned = jnp.transpose(results[(w - 1) % 2, parity])
+                for side in range(2):
+                    lanes = slice(128 * side, 128 * side + 128)
+                    spec[side, pl.ds(w - 1, bins, stride=16), :] = turned[:bins, lanes]
+                    spec[side, pl.ds(7 + w, bins, stride=16), :] = turned[bins:, lanes]
 
 
 def whiten_kernel(channels, even, odd, p0, p1, p2, p3, weight, message, energy):
@@ -151,20 +151,20 @@
         in_specs=[
             pl.BlockSpec(memory_space=pltpu.HBM),
             pl.BlockSpec(memory_space=pltpu.VMEM),
-            pl.BlockSpec(memory_space=pltpu.VMEM),
-        ],
-        scratch_shapes=[
-            pltpu.VMEM((windows, chan, samples), F32),
-            pltpu.SemaphoreType.DMA((windows,)),
         ],
         out_shape=[
             jax.ShapeDtypeStruct(spec_shape, F32),
             jax.ShapeDtypeStruct(spec_shape, F32),
             jax.ShapeDtypeStruct((windows, kept), F32),
         ],
+        scratch_shapes=[
+            pltpu.VMEM((windows, chan, samples), F32),
+            pltpu.VMEM((2, 2, chan, kept), F32),
+            pltpu.SemaphoreType.DMA((windows,)),
+        ],
         compiler_params=pltpu.CompilerParams(vmem_limit_bytes=50 << 20),
         name="spectra",
-    )(records, taper_window(samples), split_tables(samples, kept))
+    )(records, split_tables(samples, kept))
     ahead, back, across = ring(columns, 1), ring(columns, columns - 1), ring(columns, 2)
     powers = [power] + [lax.ppermute(power, "col", p) for p in (ahead, back, across)]
     weight = bin_weight.reshape(bins, 2).T.reshape(1, kept)
@@ -193,12 +193,10 @@
     half = owners // 2
     left_a = lax.ppermute(mine[:half], "col", ahead)
     right_b = lax.ppermute(mine[half:], "col", back)
-    energies = fold(fold(energies, 8), 16)
-    mine, left_a, right_b, energies = lax.optimization_barrier(
-        (mine, left_a, right_b, energies)
-    )
     left_b = lax.ppermute(mine[half:], "col", ahead)
     right_a = lax.ppermute(mine[:half], "col", back)
+    energies = fold(fold(energies, 8), 16)
+    left_a, right_b, energies = lax.optimization_barrier((left_a, right_b, energies))
     far_a = lax.ppermute(left_a, "col", ahead)
     far_b = lax.ppermute(right_b, "col", back)
     energies = fold(energies, 32)

time: 103 us -> 98.9 us (0.960)
  waiting for transfers between devices: 44 us -> 40.5 us
    ppermute x1, waiting for transfers between devices: 3.93 us -> 1.58 us  [body(): right_b = lax.ppermute(mine[half:], 'col', back)]
    ppermute x1, waiting for transfers between devices: 3.6 us -> 1.79 us  [body(): left_b = lax.ppermute(mine[half:], 'col', ahead)]
    slice x1 -> x0, local copies, waits for them, and re-layouts: 1.05 us -> none  [body(): left_b = lax.ppermute(mine[half:], 'col', ahead)]
where the time goes in v3:
time: 98.9 us; the launch traced here: 98.6 us
  waiting for transfers between devices  40.5 us (41%)
  starting transfers between devices  39.7 us (40%)
  Pallas kernels  15.9 us (16%)
  local copies, waits for them, and re-layouts  2.37 us (2%)
    ppermute x6, waiting for transfers between devices, fold(): lax.ppermute(value, 'wa', [(i, i ^ step) for i in range(owners)])  14.1 us
    all_to_all x1, waiting for transfers between devices, body(): lax.all_to_all(message, 'wa', split_axis=0, concat_axis=0, tiled=True)  12.3 us
    ppermute x6, starting transfers between devices, fold(): lax.ppermute(value, 'wa', [(i, i ^ step) for i in range(owners)])  11.9 us
    all_to_all x1, starting transfers between devices, body(): lax.all_to_all(message, 'wa', split_axis=0, concat_axis=0, tiled=True)  11.8 us
    pallas_call x1, Pallas kernels, body(): pl.pallas_call(spectra_kernel, in_specs=[pl.BlockSpec(memory_space=pltpu....  6.41 us
    pallas_call x1, Pallas kernels, body(): pl.pallas_call(functools.partial(gram_near_kernel, scale), grid_spec=pltp...  6.15 us
    ppermute x3, starting transfers between devices, body(): lax.ppermute(power, 'col', p)  5.13 us
    ppermute x3, waiting for transfers between devices, body(): lax.ppermute(power, 'col', p)  3.64 us
  transfers between devices with their start and end apart: 19, of which 15 were waited for; matrix products, arithmetic and copies ran while one was open for 0% of the time, Pallas kernels for 6%

profile of v3, /device:TPU:32, one launch (start us, length us, event | category | flops | bytes accessed | tf_op | source)
XLA Modules:
  0.0 98.6 jit_solution(2570697873766449328)
XLA Ops:
  1.0 6.4 %spectra.1 = (f32[2,1024,128]{2,1,0:T(8,128)S(1)}, f32[2,1024,128]{2,1,0:T(8,128)S(1)}, f32[8,128]{1,0:T(8,128)S(1)}) custom-call(f32[8,256,1024]{2,1,0:T(8,128)} %records.1, bf16[2,512,256]{2,1,0:T(8,128)(2,1)S(1)} %copy-done), custom_call_target="tpu_custom_call" | custom-call | tf_op jit(solution)/shard_map/spectra/pallas_call | solution.py:149
  7.5 3.1 %collective-permute-start.2 = (f32[8,128]{1,0:T(8,128)S(1)}, f32[8,128]{1,0:T(8,128)S(1)}, u32[]{:S(2)}, u32[]{:S(2)}) collective-permute-start(f32[8,128]{1,0:T(8,128)S(1)} %get-tuple-element.19.p0), channel_id=1, source_target_pairs={{0,2},{1,3},{2,0},{3,1},{4,6},{5,7},{6,4},{7,5},{8,10},{9,11},{10,... | collective-permute-start | bytes 12296 | tf_op jit(solution)/shard_map/ppermute | solution.py:169
  10.6 1.1 %collective-permute-start.1 = (f32[8,128]{1,0:T(8,128)S(1)}, f32[8,128]{1,0:T(8,128)S(1)}, u32[]{:S(2)}, u32[]{:S(2)}) collective-permute-start(f32[8,128]{1,0:T(8,128)S(1)} %get-tuple-element.19.p0), channel_id=1, source_target_pairs={{0,3},{1,0},{2,1},{3,2},{4,7},{5,4},{6,5},{7,6},{8,11},{9,8},{10,9... | collective-permute-start | bytes 12296 | tf_op jit(solution)/shard_map/ppermute | solution.py:169
  12.9 1.3 %collective-permute-done.1.p2 = f32[8,128]{1,0:T(8,128)S(1)} collective-permute-done((f32[8,128]{1,0:T(8,128)S(1)}, f32[8,128]{1,0:T(8,128)S(1)}, u32[]{:S(2)}, u32[]{:S(2)}) %collective-permute-start.1) | collective-permute-done | bytes 4128 | tf_op jit(solution)/shard_map/ppermute | solution.py:169
  14.2 2.4 %collective-permute-done.p1 = f32[8,128]{1,0:T(8,128)S(1)} collective-permute-done((f32[8,128]{1,0:T(8,128)S(1)}, f32[8,128]{1,0:T(8,128)S(1)}, u32[]{:S(2)}, u32[]{:S(2)}) %collective-permute-start) | collective-permute-done | bytes 4128 | tf_op jit(solution)/shard_map/ppermute | solution.py:169
  16.5 1.4 %whiten.1 = (bf16[64,32,256]{2,1,0:T(8,128)(2,1)}, f32[1,256]{1,0:T(1,128)S(1)}) custom-call(f32[2,1024,128]{2,1,0:T(8,128)S(1)} %get-tuple-element.17.even, f32[2,1024,128]{2,1,0:T(8,128)S(1)} %get-tuple-element.18.odd, f32[8,128]{1,0:T(8,128)S(1)} %get-tuple-element.19.p0, f32[8,128]{1,0:T(8,128)S(1)} %collective-permute-done.p1, ...), custom_call_target="tpu_custom_call" | custom-call | tf_op jit(solution)/shard_map/whiten/pallas_call | solution.py:171
  18.0 11.8 %all-to-all-start = ((bf16[64,32,256]{2,1,0:T(8,128)(2,1)}), bf16[64,32,256]{2,1,0:T(8,128)(2,1)S(1)}, u32[]{:S(2)}, u32[]{:S(2)}) async-start(bf16[64,32,256]{2,1,0:T(8,128)(2,1)} %get-tuple-element.20), calls=%async_computation | async-start | bytes 2097152 | tf_op jit(solution)/shard_map/all_to_all | solution.py:181
  30.7 2.7 %collective-permute-start.3 = (f32[1,256]{1,0:T(1,128)S(1)}, f32[1,256]{1,0:T(1,128)S(1)}, u32[]{:S(2)}, u32[]{:S(2)}) collective-permute-start(f32[1,256]{1,0:T(1,128)S(1)} %get-tuple-element.21), channel_id=1, source_target_pairs={{0,3},{1,0},{2,1},{3,2},{4,7},{5,4},{6,5},{7,6},{8,11},{9,8},{10,9... | collective-permute-start | bytes 3080 | tf_op jit(solution)/shard_map/ppermute | solution.py:183
  33.4 1.5 %collective-permute-done.5 = f32[1,256]{1,0:T(1,128)S(1)} collective-permute-done((f32[1,256]{1,0:T(1,128)S(1)}, f32[1,256]{1,0:T(1,128)S(1)}, u32[]{:S(2)}, u32[]{:S(2)}) %collective-permute-start.5) | collective-permute-done | bytes 1056 | tf_op jit(solution)/shard_map/ppermute | solution.py:183
  35.0 1.2 %collective-permute-done.6 = f32[4,256]{1,0:T(4,128)S(1)} collective-permute-done((f32[4,256]{1,0:T(4,128)S(1)}, f32[4,256]{1,0:T(4,128)S(1)}, u32[]{:S(2)}, u32[]{:S(2)}) %collective-permute-start.6) | collective-permute-done | bytes 4128 | tf_op jit(solution)/shard_map/ppermute | solution.py:187
  36.2 1.6 %collective-permute-start.7 = (f32[4,256]{1,0:T(4,128)S(1)}, f32[4,256]{1,0:T(4,128)S(1)}, u32[]{:S(2)}, u32[]{:S(2)}) collective-permute-start(f32[4,256]{1,0:T(4,128)S(1)} %fusion), channel_id=1, source_target_pairs={{0,8},{4,12},{8,0},{12,4},{16,24},{20,28},{24,16},{28,20},{32,40},... | collective-permute-start | bytes 12296 | tf_op jit(solution)/shard_map/ppermute | solution.py:187
  37.8 2.2 %collective-permute-done.7 = f32[4,256]{1,0:T(4,128)S(1)} collective-permute-done((f32[4,256]{1,0:T(4,128)S(1)}, f32[4,256]{1,0:T(4,128)S(1)}, u32[]{:S(2)}, u32[]{:S(2)}) %collective-permute-start.7) | collective-permute-done | bytes 4128 | tf_op jit(solution)/shard_map/ppermute | solution.py:187
  39.9 3.1 %collective-permute-start.8 = (f32[4,256]{1,0:T(4,128)S(1)}, f32[4,256]{1,0:T(4,128)S(1)}, u32[]{:S(2)}, u32[]{:S(2)}) collective-permute-start(f32[4,256]{1,0:T(4,128)S(1)} %fusion.2), channel_id=1, source_target_pairs={{0,16},{4,20},{8,24},{12,28},{16,0},{20,4},{24,8},{28,12},{32,48},... | collective-permute-start | bytes 12296 | tf_op jit(solution)/shard_map/ppermute | solution.py:187
  43.0 2.4 %collective-permute-done.8 = f32[4,256]{1,0:T(4,128)S(1)} collective-permute-done((f32[4,256]{1,0:T(4,128)S(1)}, f32[4,256]{1,0:T(4,128)S(1)}, u32[]{:S(2)}, u32[]{:S(2)}) %collective-permute-start.8) | collective-permute-done | bytes 4128 | tf_op jit(solution)/shard_map/ppermute | solution.py:187
  45.3 12.3 %all-to-all-done.own = bf16[64,32,256]{2,1,0:T(8,128)(2,1)S(1)} async-done(((bf16[64,32,256]{2,1,0:T(8,128)(2,1)}), bf16[64,32,256]{2,1,0:T(8,128)(2,1)S(1)}, u32[]{:S(2)}, u32[]{:S(2)}) %all-to-all-start) | async-done | bytes 1048608 | tf_op jit(solution)/shard_map/all_to_all | solution.py:181
  57.7 1.0 %fusion.1 = (bf16[32,32,256]{2,1,0:T(8,128)(2,1)}, bf16[32,32,256]{2,1,0:T(8,128)(2,1)}) fusion(bf16[64,32,256]{2,1,0:T(8,128)(2,1)S(1)} %all-to-all-done.own), kind=kLoop, calls=%fused_computation.2 | loop fusion | bytes 2097152 | tf_op jit(solution)/shard_map/slice | solution.py:195
  58.7 2.0 %collective-permute-start.10 = (bf16[32,32,256]{2,1,0:T(8,128)(2,1)}, bf16[32,32,256]{2,1,0:T(8,128)(2,1)S(1)}, u32[]{:S(2)}, u32[]{:S(2)}) collective-permute-start(bf16[32,32,256]{2,1,0:T(8,128)(2,1)} %get-tuple-element.30), channel_id=1, source_target_pairs={{0,1},{1,2},{2,3},{3,0},{4,5},{5,6},{6,7},{7,4},{8,9},{9,10},{10,1... | collective-permute-start | bytes 1572872 | tf_op jit(solution)/shard_map/ppermute | solution.py:194
  60.8 3.2 %collective-permute-start.9 = (bf16[32,32,256]{2,1,0:T(8,128)(2,1)}, bf16[32,32,256]{2,1,0:T(8,128)(2,1)}, u32[]{:S(2)}, u32[]{:S(2)}) collective-permute-start(bf16[32,32,256]{2,1,0:T(8,128)(2,1)} %get-tuple-element.30), channel_id=1, source_target_pairs={{0,3},{1,0},{2,1},{3,2},{4,7},{5,4},{6,5},{7,6},{8,11},{9,8},{10,9... | collective-permute-start | bytes 1572872 | tf_op jit(solution)/shard_map/ppermute | solution.py:197
  64.0 1.4 %collective-permute-start.12 = (f32[4,256]{1,0:T(4,128)S(1)}, f32[4,256]{1,0:T(4,128)S(1)}, u32[]{:S(2)}, u32[]{:S(2)}) collective-permute-start(f32[4,256]{1,0:T(4,128)S(1)} %add.20), channel_id=1, source_target_pairs={{0,32},{4,36},{8,40},{12,44},{16,48},{20,52},{24,56},{28,60},{32,0... | collective-permute-start | bytes 12296 | tf_op jit(solution)/shard_map/ppermute | solution.py:187
  65.4 2.2 %collective-permute-done.12 = f32[4,256]{1,0:T(4,128)S(1)} collective-permute-done((f32[4,256]{1,0:T(4,128)S(1)}, f32[4,256]{1,0:T(4,128)S(1)}, u32[]{:S(2)}, u32[]{:S(2)}) %collective-permute-start.12) | collective-permute-done | bytes 4128 | tf_op jit(solution)/shard_map/ppermute | solution.py:187
  67.6 2.6 %collective-permute-start.13 = (f32[4,256]{1,0:T(4,128)S(1)}, f32[4,256]{1,0:T(4,128)S(1)}, u32[]{:S(2)}, u32[]{:S(2)}) collective-permute-start(f32[4,256]{1,0:T(4,128)S(1)} %add.21), channel_id=1, source_target_pairs={{0,64},{4,68},{8,72},{12,76},{16,80},{20,84},{24,88},{28,92},{32,9... | collective-permute-start | bytes 12296 | tf_op jit(solution)/shard_map/ppermute | solution.py:187
  70.2 1.9 %collective-permute-done.13 = f32[4,256]{1,0:T(4,128)S(1)} collective-permute-done((f32[4,256]{1,0:T(4,128)S(1)}, f32[4,256]{1,0:T(4,128)S(1)}, u32[]{:S(2)}, u32[]{:S(2)}) %collective-permute-start.13) | collective-permute-done | bytes 4128 | tf_op jit(solution)/shard_map/ppermute | solution.py:187
  72.1 1.6 %collective-permute-done.11.right_b = bf16[32,32,256]{2,1,0:T(8,128)(2,1)S(1)} collective-permute-done((bf16[32,32,256]{2,1,0:T(8,128)(2,1)}, bf16[32,32,256]{2,1,0:T(8,128)(2,1)S(1)}, u32[]{:S(2)}, u32[]{:S(2)}) %collective-permute-start.11) | collective-permute-done | bytes 524320 | tf_op jit(solution)/shard_map/ppermute | solution.py:195
  73.7 1.2 %collective-permute-done.10.left_a = bf16[32,32,256]{2,1,0:T(8,128)(2,1)S(1)} collective-permute-done((bf16[32,32,256]{2,1,0:T(8,128)(2,1)}, bf16[32,32,256]{2,1,0:T(8,128)(2,1)S(1)}, u32[]{:S(2)}, u32[]{:S(2)}) %collective-permute-start.10) | collective-permute-done | bytes 524320 | tf_op jit(solution)/shard_map/ppermute | solution.py:194
  74.9 2.0 %collective-permute-start.16 = (bf16[32,32,256]{2,1,0:T(8,128)(2,1)S(1)}, bf16[32,32,256]{2,1,0:T(8,128)(2,1)S(1)}, u32[]{:S(2)}, u32[]{:S(2)}) collective-permute-start(bf16[32,32,256]{2,1,0:T(8,128)(2,1)S(1)} %collective-permute-done.10.left_a), channel_id=1, source_target_pairs={{0,1},{1,2},{2,3},{3,0},{4,5},{5,6},{6,7},{7,4},{8,9},{9,10},{10,1... | collective-permute-start | bytes 1572872 | tf_op jit(solution)/shard_map/ppermute | solution.py:200
  76.9 3.1 %collective-permute-start.15 = (f32[4,256]{1,0:T(4,128)S(1)}, f32[4,256]{1,0:T(4,128)S(1)}, u32[]{:S(2)}, u32[]{:S(2)}) collective-permute-start(f32[4,256]{1,0:T(4,128)S(1)} %add.22), channel_id=1, source_target_pairs={{0,128},{4,132},{8,136},{12,140},{16,144},{20,148},{24,152},{28,15... | collective-permute-start | bytes 12296 | tf_op jit(solution)/shard_map/ppermute | solution.py:187
  80.1 4.4 %collective-permute-done.15 = f32[4,256]{1,0:T(4,128)S(1)} collective-permute-done((f32[4,256]{1,0:T(4,128)S(1)}, f32[4,256]{1,0:T(4,128)S(1)}, u32[]{:S(2)}, u32[]{:S(2)}) %collective-permute-start.15) | collective-permute-done | bytes 4128 | tf_op jit(solution)/shard_map/ppermute | solution.py:187
  84.4 1.8 %collective-permute-done.14.left_b = bf16[32,32,256]{2,1,0:T(8,128)(2,1)} collective-permute-done((bf16[32,32,256]{2,1,0:T(8,128)(2,1)}, bf16[32,32,256]{2,1,0:T(8,128)(2,1)}, u32[]{:S(2)}, u32[]{:S(2)}) %collective-permute-start.14) | collective-permute-done | bytes 524320 | tf_op jit(solution)/shard_map/ppermute | solution.py:196
  86.2 6.1 %gram_near.1 = (f32[2,2,256,1024]{3,2,1,0:T(8,128)}, bf16[2,512,1024]{2,1,0:T(8,128)(2,1)S(1)}) custom-call(s32[1]{0:T(128)} %bitcast.col, bf16[64,32,256]{2,1,0:T(8,128)(2,1)S(1)} %all-to-all-done.own, bf16[32,32,256]{2,1,0:T(8,128)(2,1)} %collective-permute-done.9.right_a, bf16[32,32,256]{2,1,0:T(8,128)(2,1)S(1)} %collective-permute-done.11.right_b, ...), custom_call_target="tpu_custom_call" | custom-call | flops 1610612736 | bytes 8388608 | tf_op jit(solution)/shard_map/gram_near/pallas_call | solution.py:222
  92.4 3.1 %collective-permute-done.17.far_b = bf16[32,32,256]{2,1,0:T(8,128)(2,1)S(1)} collective-permute-done((bf16[32,32,256]{2,1,0:T(8,128)(2,1)S(1)}, bf16[32,32,256]{2,1,0:T(8,128)(2,1)S(1)}, u32[]{:S(2)}, u32[]{:S(2)}) %collective-permute-start.17) | collective-permute-done | bytes 524320 | tf_op jit(solution)/shard_map/ppermute | solution.py:201
  95.5 1.2 %collective-permute-done.16.far_a = bf16[32,32,256]{2,1,0:T(8,128)(2,1)S(1)} collective-permute-done((bf16[32,32,256]{2,1,0:T(8,128)(2,1)S(1)}, bf16[32,32,256]{2,1,0:T(8,128)(2,1)S(1)}, u32[]{:S(2)}, u32[]{:S(2)}) %collective-permute-start.16) | collective-permute-done | bytes 524320 | tf_op jit(solution)/shard_map/ppermute | solution.py:200
  96.7 1.9 %gram_far.1 = f32[2,2,256,1024]{3,2,1,0:T(8,128)} custom-call(s32[1]{0:T(128)} %bitcast.col, bf16[2,512,1024]{2,1,0:T(8,128)(2,1)S(1)} %get-tuple-element.27.lhs, bf16[32,32,256]{2,1,0:T(8,128)(2,1)S(1)} %collective-permute-done.16.far_a, bf16[32,32,256]{2,1,0:T(8,128)(2,1)S(1)} %collective-permute-done.17.far_b, ...), custom_call_target="tpu_custom_call", output_to_operand_aliasing={{}: (5, {})} | custom-call | flops 536870912 | bytes 4194304 | tf_op jit(solution)/shard_map/gram_far/pallas_call | solution.py:237
  (25 shorter events, 3.4 us)
Async XLA Ops:
  0.0 1.0 %copy-start = (bf16[2,512,256]{2,1,0:T(8,128)(2,1)S(1)}, bf16[2,512,256]{2,1,0:T(8,128)(2,1)}, u32[]{:S(2)}) copy-start(bf16[2,512,256]{2,1,0:T(8,128)(2,1)} %constant.6.clone.tables) | copy-start | bytes 1572868
  1.0 11.6 %copy-start.1 = (f32[128]{0:T(128)S(1)}, f32[128]{0:T(128)}, u32[]{:S(2)}) copy-start(f32[128]{0:T(128)} %param.4) | copy-start | bytes 1540
  7.5 5.4 %collective-permute-start.2 = (f32[8,128]{1,0:T(8,128)S(1)}, f32[8,128]{1,0:T(8,128)S(1)}, u32[]{:S(2)}, u32[]{:S(2)}) collective-permute-start(f32[8,128]{1,0:T(8,128)S(1)} %get-tuple-element.19.p0), channel_id=1, source_target_pairs={{0,2},{1,3},{2,0},{3,1},{4,6},{5,7},{6,4},{7,5},{8,10},{9,11},{10,... | collective-permute-start | bytes 12296 | tf_op jit(solution)/shard_map/ppermute | solution.py:169
  10.6 3.6 %collective-permute-start.1 = (f32[8,128]{1,0:T(8,128)S(1)}, f32[8,128]{1,0:T(8,128)S(1)}, u32[]{:S(2)}, u32[]{:S(2)}) collective-permute-start(f32[8,128]{1,0:T(8,128)S(1)} %get-tuple-element.19.p0), channel_id=1, source_target_pairs={{0,3},{1,0},{2,1},{3,2},{4,7},{5,4},{6,5},{7,6},{8,11},{9,8},{10,9... | collective-permute-start | bytes 12296 | tf_op jit(solution)/shard_map/ppermute | solution.py:169
  11.7 4.8 %collective-permute-start = (f32[8,128]{1,0:T(8,128)S(1)}, f32[8,128]{1,0:T(8,128)S(1)}, u32[]{:S(2)}, u32[]{:S(2)}) collective-permute-start(f32[8,128]{1,0:T(8,128)S(1)} %get-tuple-element.19.p0), channel_id=1, source_target_pairs={{0,1},{1,2},{2,3},{3,0},{4,5},{5,6},{6,7},{7,4},{8,9},{9,10},{10,1... | collective-permute-start | bytes 12296 | tf_op jit(solution)/shard_map/ppermute | solution.py:169
  18.0 39.7 %all-to-all-start = ((bf16[64,32,256]{2,1,0:T(8,128)(2,1)}), bf16[64,32,256]{2,1,0:T(8,128)(2,1)S(1)}, u32[]{:S(2)}, u32[]{:S(2)}) async-start(bf16[64,32,256]{2,1,0:T(8,128)(2,1)} %get-tuple-element.20), calls=%async_computation | async-start | bytes 2097152 | tf_op jit(solution)/shard_map/all_to_all | solution.py:181
  29.7 5.2 %collective-permute-start.5 = (f32[1,256]{1,0:T(1,128)S(1)}, f32[1,256]{1,0:T(1,128)S(1)}, u32[]{:S(2)}, u32[]{:S(2)}) collective-permute-start(f32[1,256]{1,0:T(1,128)S(1)} %get-tuple-element.21), channel_id=1, source_target_pairs={{0,2},{1,3},{2,0},{3,1},{4,6},{5,7},{6,4},{7,5},{8,10},{9,11},{10,... | collective-permute-start | bytes 3080 | tf_op jit(solution)/shard_map/ppermute | solution.py:183
  30.1 4.8 %collective-permute-start.4 = (f32[1,256]{1,0:T(1,128)S(1)}, f32[1,256]{1,0:T(1,128)S(1)}, u32[]{:S(2)}, u32[]{:S(2)}) collective-permute-start(f32[1,256]{1,0:T(1,128)S(1)} %get-tuple-element.21), channel_id=1, source_target_pairs={{0,1},{1,2},{2,3},{3,0},{4,5},{5,6},{6,7},{7,4},{8,9},{9,10},{10,1... | collective-permute-start | bytes 3080 | tf_op jit(solution)/shard_map/ppermute | solution.py:183
  30.7 4.2 %collective-permute-start.3 = (f32[1,256]{1,0:T(1,128)S(1)}, f32[1,256]{1,0:T(1,128)S(1)}, u32[]{:S(2)}, u32[]{:S(2)}) collective-permute-start(f32[1,256]{1,0:T(1,128)S(1)} %get-tuple-element.21), channel_id=1, source_target_pairs={{0,3},{1,0},{2,1},{3,2},{4,7},{5,4},{6,5},{7,6},{8,11},{9,8},{10,9... | collective-permute-start | bytes 3080 | tf_op jit(solution)/shard_map/ppermute | solution.py:183
  34.9 1.3 %collective-permute-start.6 = (f32[4,256]{1,0:T(4,128)S(1)}, f32[4,256]{1,0:T(4,128)S(1)}, u32[]{:S(2)}, u32[]{:S(2)}) collective-permute-start(f32[4,256]{1,0:T(4,128)S(1)} %pad_maximum_fusion), channel_id=1, source_target_pairs={{0,4},{4,0},{8,12},{12,8},{16,20},{20,16},{24,28},{28,24},{32,36},... | collective-permute-start | bytes 12296 | tf_op jit(solution)/shard_map/ppermute | solution.py:187
  36.2 3.7 %collective-permute-start.7 = (f32[4,256]{1,0:T(4,128)S(1)}, f32[4,256]{1,0:T(4,128)S(1)}, u32[]{:S(2)}, u32[]{:S(2)}) collective-permute-start(f32[4,256]{1,0:T(4,128)S(1)} %fusion), channel_id=1, source_target_pairs={{0,8},{4,12},{8,0},{12,4},{16,24},{20,28},{24,16},{28,20},{32,40},... | collective-permute-start | bytes 12296 | tf_op jit(solution)/shard_map/ppermute | solution.py:187
  39.9 5.4 %collective-permute-start.8 = (f32[4,256]{1,0:T(4,128)S(1)}, f32[4,256]{1,0:T(4,128)S(1)}, u32[]{:S(2)}, u32[]{:S(2)}) collective-permute-start(f32[4,256]{1,0:T(4,128)S(1)} %fusion.2), channel_id=1, source_target_pairs={{0,16},{4,20},{8,24},{12,28},{16,0},{20,4},{24,8},{28,12},{32,48},... | collective-permute-start | bytes 12296 | tf_op jit(solution)/shard_map/ppermute | solution.py:187
  58.7 15.0 %collective-permute-start.11 = (bf16[32,32,256]{2,1,0:T(8,128)(2,1)}, bf16[32,32,256]{2,1,0:T(8,128)(2,1)S(1)}, u32[]{:S(2)}, u32[]{:S(2)}) collective-permute-start(bf16[32,32,256]{2,1,0:T(8,128)(2,1)} %get-tuple-element.29), channel_id=1, source_target_pairs={{0,3},{1,0},{2,1},{3,2},{4,7},{5,4},{6,5},{7,6},{8,11},{9,8},{10,9... | collective-permute-start | bytes 1572872 | tf_op jit(solution)/shard_map/ppermute | solution.py:195
  58.7 16.2 %collective-permute-start.10 = (bf16[32,32,256]{2,1,0:T(8,128)(2,1)}, bf16[32,32,256]{2,1,0:T(8,128)(2,1)S(1)}, u32[]{:S(2)}, u32[]{:S(2)}) collective-permute-start(bf16[32,32,256]{2,1,0:T(8,128)(2,1)} %get-tuple-element.30), channel_id=1, source_target_pairs={{0,1},{1,2},{2,3},{3,0},{4,5},{5,6},{6,7},{7,4},{8,9},{9,10},{10,1... | collective-permute-start | bytes 1572872 | tf_op jit(solution)/shard_map/ppermute | solution.py:194
  60.7 25.5 %collective-permute-start.14 = (bf16[32,32,256]{2,1,0:T(8,128)(2,1)}, bf16[32,32,256]{2,1,0:T(8,128)(2,1)}, u32[]{:S(2)}, u32[]{:S(2)}) collective-permute-start(bf16[32,32,256]{2,1,0:T(8,128)(2,1)} %get-tuple-element.29), channel_id=1, source_target_pairs={{0,1},{1,2},{2,3},{3,0},{4,5},{5,6},{6,7},{7,4},{8,9},{9,10},{10,1... | collective-permute-start | bytes 1572872 | tf_op jit(solution)/shard_map/ppermute | solution.py:196
  60.8 25.5 %collective-permute-start.9 = (bf16[32,32,256]{2,1,0:T(8,128)(2,1)}, bf16[32,32,256]{2,1,0:T(8,128)(2,1)}, u32[]{:S(2)}, u32[]{:S(2)}) collective-permute-start(bf16[32,32,256]{2,1,0:T(8,128)(2,1)} %get-tuple-element.30), channel_id=1, source_target_pairs={{0,3},{1,0},{2,1},{3,2},{4,7},{5,4},{6,5},{7,6},{8,11},{9,8},{10,9... | collective-permute-start | bytes 1572872 | tf_op jit(solution)/shard_map/ppermute | solution.py:197
  64.0 3.6 %collective-permute-start.12 = (f32[4,256]{1,0:T(4,128)S(1)}, f32[4,256]{1,0:T(4,128)S(1)}, u32[]{:S(2)}, u32[]{:S(2)}) collective-permute-start(f32[4,256]{1,0:T(4,128)S(1)} %add.20), channel_id=1, source_target_pairs={{0,32},{4,36},{8,40},{12,44},{16,48},{20,52},{24,56},{28,60},{32,0... | collective-permute-start | bytes 12296 | tf_op jit(solution)/shard_map/ppermute | solution.py:187
  67.6 4.5 %collective-permute-start.13 = (f32[4,256]{1,0:T(4,128)S(1)}, f32[4,256]{1,0:T(4,128)S(1)}, u32[]{:S(2)}, u32[]{:S(2)}) collective-permute-start(f32[4,256]{1,0:T(4,128)S(1)} %add.21), channel_id=1, source_target_pairs={{0,64},{4,68},{8,72},{12,76},{16,80},{20,84},{24,88},{28,92},{32,9... | collective-permute-start | bytes 12296 | tf_op jit(solution)/shard_map/ppermute | solution.py:187
  74.9 20.6 %collective-permute-start.17 = (bf16[32,32,256]{2,1,0:T(8,128)(2,1)S(1)}, bf16[32,32,256]{2,1,0:T(8,128)(2,1)S(1)}, u32[]{:S(2)}, u32[]{:S(2)}) collective-permute-start(bf16[32,32,256]{2,1,0:T(8,128)(2,1)S(1)} %collective-permute-done.11.right_b), channel_id=1, source_target_pairs={{0,3},{1,0},{2,1},{3,2},{4,7},{5,4},{6,5},{7,6},{8,11},{9,8},{10,9... | collective-permute-start | bytes 1572872 | tf_op jit(solution)/shard_map/ppermute | solution.py:201
  74.9 21.8 %collective-permute-start.16 = (bf16[32,32,256]{2,1,0:T(8,128)(2,1)S(1)}, bf16[32,32,256]{2,1,0:T(8,128)(2,1)S(1)}, u32[]{:S(2)}, u32[]{:S(2)}) collective-permute-start(bf16[32,32,256]{2,1,0:T(8,128)(2,1)S(1)} %collective-permute-done.10.left_a), channel_id=1, source_target_pairs={{0,1},{1,2},{2,3},{3,0},{4,5},{5,6},{6,7},{7,4},{8,9},{9,10},{10,1... | collective-permute-start | bytes 1572872 | tf_op jit(solution)/shard_map/ppermute | solution.py:200
  76.9 7.5 %collective-permute-start.15 = (f32[4,256]{1,0:T(4,128)S(1)}, f32[4,256]{1,0:T(4,128)S(1)}, u32[]{:S(2)}, u32[]{:S(2)}) collective-permute-start(f32[4,256]{1,0:T(4,128)S(1)} %add.22), channel_id=1, source_target_pairs={{0,128},{4,132},{8,136},{12,140},{16,144},{20,148},{24,152},{28,15... | collective-permute-start | bytes 12296 | tf_op jit(solution)/shard_map/ppermute | solution.py:187

commit v4 on v3

--- a/solution.py
+++ b/solution.py
@@ -46,36 +46,48 @@
     steps = lax.broadcasted_iota(jnp.int32, (1, samples), 1).astype(F32)
     taper = 0.5 - 0.5 * jnp.cos(steps * (2.0 * math.pi / samples))
 
-    for w in range(windows + 1):
-        if w < windows:
-            fetch(w).wait()
-            tapered = held[w] * taper
+    chan = records.shape[1]
+    for pair in range(0, windows + 2, 2):
+        if pair < windows:
+            fetch(pair).wait()
+            fetch(pair + 1).wait()
+            tapered = held[pair : pair + 2].reshape(2 * chan, samples) * taper
             first, second = tapered[:, :half], tapered[:, half:]
-            rows = []
+            rows = [[], []]
             for parity in range(2):
                 folded = first + second if parity == 0 else first - second
                 high = folded.astype(BF)
                 low = (folded - high.astype(F32)).astype(BF)
                 both = dot(high, tables[parity])
                 result = both[:, :kept] + both[:, kept:] + dot(low, tables[parity, :, :kept])
-                results[w % 2, parity] = result
-                square = jnp.sum(result * result, axis=0, keepdims=True)
-                rows.append(square[:, :bins] + square[:, bins:])
-            power[w : w + 1, :] = jnp.concatenate(rows, axis=1)
-        if w > 0:
+                square = result * result
+                for i in range(2):
+                    part = slice(i * chan, i * chan + chan)
+                    results[pair + i, parity] = result[part]
+                    total = jnp.sum(square[part], axis=0, keepdims=True)
+                    rows[i].append(total[:, :bins] + total[:, bins:])
+            for i in range(2):
+                power[pair + i : pair + i + 1, :] = jnp.concatenate(rows[i], axis=1)
+        for w in range(pair - 2, pair) if pair else ():
             for parity, spec in enumerate((even, odd)):
-                turned = jnp.transpose(results[(w - 1) % 2, parity])
+                turned = jnp.transpose(results[w, parity])
                 for side in range(2):
                     lanes = slice(128 * side, 128 * side + 128)
-                    spec[side, pl.ds(w - 1, bins, stride=16), :] = turned[:bins, lanes]
-                    spec[side, pl.ds(7 + w, bins, stride=16), :] = turned[bins:, lanes]
-
-
-def whiten_kernel(channels, even, odd, p0, p1, p2, p3, weight, message, energy):
+                    spec[side, pl.ds(w, bins, stride=16), :] = turned[:bins, lanes]
+                    spec[side, pl.ds(8 + w, bins, stride=16), :] = turned[bins:, lanes]
+
+
+def whiten_kernel(channels, even, odd, p0, p1, p2, p3, weight, message, energy, held, sent):
     bins = p0.shape[1] // 2
+    group = bins // 4
     power = (p0[...] + p1[...]) + (p2[...] + p3[...])
     factor = weight[...] / jnp.sqrt(power / channels + 1e-06)
     total = jnp.zeros((8, 256), F32)
+
+    def send(part):
+        owners = pl.ds(part * group, group)
+        return pltpu.make_async_copy(held.at[owners], message.at[owners], sent.at[part])
+
     for owner in range(bins):
         for parity, spec in enumerate((even, odd)):
             lane = parity * bins + owner
@@ -87,10 +99,14 @@
             real = (block[:8] * scale).astype(BF).astype(F32)
             imag = (block[8:] * scale).astype(BF).astype(F32)
             total = total + (real * real + imag * imag)
-            message[owner, parity * 16 : parity * 16 + 16, :] = jnp.concatenate(
+            held[owner, parity * 16 : parity * 16 + 16, :] = jnp.concatenate(
                 [real, imag], axis=0
             ).astype(BF)
+        if owner % group == group - 1:
+            send(owner // group).start()
     energy[...] = jnp.sum(total, axis=0, keepdims=True)
+    for part in range(4):
+        send(part).wait()
 
 
 def flat(block):
@@ -133,7 +149,10 @@
 
 def gram_far_kernel(scale, col, lhs, far_a, far_b, energy, kept, out):
     half = lhs.shape[2] // 2
-    product = dot(lhs[0, :, :half], flat(far_a[...])) + dot(lhs[0, :, half:], flat(far_b[...]))
+    b = pl.program_id(0)
+    rows = pl.ds(pl.multiple_of(b * 16, 16), 16)
+    product = dot(lhs[b, :, :half], flat(far_a[:, rows, :]))
+    product += dot(lhs[b, :, half:], flat(far_b[:, rows, :]))
     emit(product, energy, 3, scale, out)
 
 
@@ -159,7 +178,7 @@
         ],
         scratch_shapes=[
             pltpu.VMEM((windows, chan, samples), F32),
-            pltpu.VMEM((2, 2, chan, kept), F32),
+            pltpu.VMEM((windows, 2, chan, kept), F32),
             pltpu.SemaphoreType.DMA((windows,)),
         ],
         compiler_params=pltpu.CompilerParams(vmem_limit_bytes=50 << 20),
@@ -174,6 +193,11 @@
             jax.ShapeDtypeStruct((owners, 32, chan), BF),
             jax.ShapeDtypeStruct((1, chan), F32),
         ],
+        out_specs=[pl.BlockSpec(memory_space=pltpu.HBM), pl.BlockSpec(memory_space=pltpu.VMEM)],
+        scratch_shapes=[
+            pltpu.VMEM((owners, 32, chan), BF),
+            pltpu.SemaphoreType.DMA((4,)),
+        ],
         compiler_params=pltpu.CompilerParams(vmem_limit_bytes=10 << 20),
         name="whiten",
     )(even, odd, *powers, weight)
@@ -193,9 +217,11 @@
     half = owners // 2
     left_a = lax.ppermute(mine[:half], "col", ahead)
     right_b = lax.ppermute(mine[half:], "col", back)
-    left_b = lax.ppermute(mine[half:], "col", ahead)
-    right_a = lax.ppermute(mine[:half], "col", back)
-    energies = fold(fold(energies, 8), 16)
+    energies = fold(energies, 8)
+    late, energies = lax.optimization_barrier((mine, energies))
+    left_b = lax.ppermute(late[half:], "col", ahead)
+    right_a = lax.ppermute(late[:half], "col", back)
+    energies = fold(energies, 16)
     left_a, right_b, energies = lax.optimization_barrier((left_a, right_b, energies))
     far_a = lax.ppermute(left_a, "col", ahead)
     far_b = lax.ppermute(right_b, "col", back)
@@ -239,8 +265,8 @@
         grid_spec=pltpu.PrefetchScalarGridSpec(
             num_scalar_prefetch=1,
             grid=(2, 1),
-            in_specs=[lhs_block, bin_block(half), bin_block(half), energy_block]
-            + [pl.BlockSpec(memory_space=pl.ANY)],
+            in_specs=[pl.BlockSpec(memory_space=pltpu.VMEM)] * 3
+            + [energy_block, pl.BlockSpec(memory_space=pl.ANY)],
             out_specs=out_block(3),
         ),
         out_shape=out_shape,

time: 98.9 us -> 96.9 us (0.980)
  Pallas kernels: 15.9 us -> 14.8 us
  waiting for transfers between devices: 40.5 us -> 39.5 us
    ppermute x1, waiting for transfers between devices: 1.58 us -> 0.33 us  [body(): right_b = lax.ppermute(mine[half:], 'col', back)]
    slice x0 -> x1, local copies, waits for them, and re-layouts: none -> 1.04 us  [body(): left_b = lax.ppermute(late[half:], 'col', ahead)]
  transfers between devices with their start and end apart: 19 -> 19, of which waited for: 15 -> 15; matrix products, arithmetic and copies ran while one was open for 0% -> 1% of each run, Pallas kernels for 6% -> 6%
where the time goes in v4:
time: 96.9 us; the launch traced here: 96.6 us
  starting transfers between devices  39.8 us (41%)
  waiting for transfers between devices  39.5 us (41%)
  Pallas kernels  14.8 us (15%)
  local copies, waits for them, and re-layouts  2.44 us (3%)
    ppermute x6, waiting for transfers between devices, fold(): lax.ppermute(value, 'wa', [(i, i ^ step) for i in range(owners)])  14.1 us
    all_to_all x1, waiting for transfers between devices, body(): lax.all_to_all(message, 'wa', split_axis=0, concat_axis=0, tiled=True)  12.4 us
    ppermute x6, starting transfers between devices, fold(): lax.ppermute(value, 'wa', [(i, i ^ step) for i in range(owners)])  11.9 us
    all_to_all x1, starting transfers between devices, body(): lax.all_to_all(message, 'wa', split_axis=0, concat_axis=0, tiled=True)  11.8 us
    pallas_call x1, Pallas kernels, body(): pl.pallas_call(functools.partial(gram_near_kernel, scale), grid_spec=pltp...  6.15 us
    pallas_call x1, Pallas kernels, body(): pl.pallas_call(spectra_kernel, in_specs=[pl.BlockSpec(memory_space=pltpu....  5.61 us
    ppermute x3, starting transfers between devices, body(): lax.ppermute(power, 'col', p)  5.13 us
    ppermute x3, waiting for transfers between devices, body(): lax.ppermute(power, 'col', p)  3.64 us
  transfers between devices with their start and end apart: 19, of which 15 were waited for; matrix products, arithmetic and copies ran while one was open for 1% of the time, Pallas kernels for 6%

profile of v4, /device:TPU:32, one launch (start us, length us, event | category | flops | bytes accessed | tf_op | source)
XLA Modules:
  0.0 96.6 jit_solution(4895179761008591954)
XLA Ops:
  0.0 1.0 %copy-done = bf16[2,512,256]{2,1,0:T(8,128)(2,1)S(1)} copy-done((bf16[2,512,256]{2,1,0:T(8,128)(2,1)S(1)}, bf16[2,512,256]{2,1,0:T(8,128)(2,1)}, u32[]{:S(2)}) %copy-start) | copy-done | bytes 524312
  1.0 5.6 %spectra.1 = (f32[2,1024,128]{2,1,0:T(8,128)S(1)}, f32[2,1024,128]{2,1,0:T(8,128)S(1)}, f32[8,128]{1,0:T(8,128)S(1)}) custom-call(f32[8,256,1024]{2,1,0:T(8,128)} %records.1, bf16[2,512,256]{2,1,0:T(8,128)(2,1)S(1)} %copy-done), custom_call_target="tpu_custom_call" | custom-call | tf_op jit(solution)/shard_map/spectra/pallas_call | solution.py:168
  6.7 3.1 %collective-permute-start.2 = (f32[8,128]{1,0:T(8,128)S(1)}, f32[8,128]{1,0:T(8,128)S(1)}, u32[]{:S(2)}, u32[]{:S(2)}) collective-permute-start(f32[8,128]{1,0:T(8,128)S(1)} %get-tuple-element.21.p0), channel_id=1, source_target_pairs={{0,2},{1,3},{2,0},{3,1},{4,6},{5,7},{6,4},{7,5},{8,10},{9,11},{10,... | collective-permute-start | bytes 12296 | tf_op jit(solution)/shard_map/ppermute | solution.py:188
  9.8 1.1 %collective-permute-start.1 = (f32[8,128]{1,0:T(8,128)S(1)}, f32[8,128]{1,0:T(8,128)S(1)}, u32[]{:S(2)}, u32[]{:S(2)}) collective-permute-start(f32[8,128]{1,0:T(8,128)S(1)} %get-tuple-element.21.p0), channel_id=1, source_target_pairs={{0,3},{1,0},{2,1},{3,2},{4,7},{5,4},{6,5},{7,6},{8,11},{9,8},{10,9... | collective-permute-start | bytes 12296 | tf_op jit(solution)/shard_map/ppermute | solution.py:188
  12.1 1.3 %collective-permute-done.1.p2 = f32[8,128]{1,0:T(8,128)S(1)} collective-permute-done((f32[8,128]{1,0:T(8,128)S(1)}, f32[8,128]{1,0:T(8,128)S(1)}, u32[]{:S(2)}, u32[]{:S(2)}) %collective-permute-start.1) | collective-permute-done | bytes 4128 | tf_op jit(solution)/shard_map/ppermute | solution.py:188
  13.4 2.4 %collective-permute-done.p1 = f32[8,128]{1,0:T(8,128)S(1)} collective-permute-done((f32[8,128]{1,0:T(8,128)S(1)}, f32[8,128]{1,0:T(8,128)S(1)}, u32[]{:S(2)}, u32[]{:S(2)}) %collective-permute-start) | collective-permute-done | bytes 4128 | tf_op jit(solution)/shard_map/ppermute | solution.py:188
  15.7 1.2 %whiten.1 = (bf16[64,32,256]{2,1,0:T(8,128)(2,1)}, f32[1,256]{1,0:T(1,128)S(1)}) custom-call(f32[2,1024,128]{2,1,0:T(8,128)S(1)} %get-tuple-element.19.even, f32[2,1024,128]{2,1,0:T(8,128)S(1)} %get-tuple-element.20.odd, f32[8,128]{1,0:T(8,128)S(1)} %get-tuple-element.21.p0, f32[8,128]{1,0:T(8,128)S(1)} %collective-permute-done.p1, ...), custom_call_target="tpu_custom_call" | custom-call | tf_op jit(solution)/shard_map/whiten/pallas_call | solution.py:190
  17.0 11.8 %all-to-all-start = ((bf16[64,32,256]{2,1,0:T(8,128)(2,1)}), bf16[64,32,256]{2,1,0:T(8,128)(2,1)S(1)}, u32[]{:S(2)}, u32[]{:S(2)}) async-start(bf16[64,32,256]{2,1,0:T(8,128)(2,1)} %get-tuple-element.22), calls=%async_computation | async-start | bytes 2097152 | tf_op jit(solution)/shard_map/all_to_all | solution.py:205
  29.7 2.7 %collective-permute-start.3 = (f32[1,256]{1,0:T(1,128)S(1)}, f32[1,256]{1,0:T(1,128)S(1)}, u32[]{:S(2)}, u32[]{:S(2)}) collective-permute-start(f32[1,256]{1,0:T(1,128)S(1)} %get-tuple-element.23), channel_id=1, source_target_pairs={{0,3},{1,0},{2,1},{3,2},{4,7},{5,4},{6,5},{7,6},{8,11},{9,8},{10,9... | collective-permute-start | bytes 3080 | tf_op jit(solution)/shard_map/ppermute | solution.py:207
  32.4 1.5 %collective-permute-done.5 = f32[1,256]{1,0:T(1,128)S(1)} collective-permute-done((f32[1,256]{1,0:T(1,128)S(1)}, f32[1,256]{1,0:T(1,128)S(1)}, u32[]{:S(2)}, u32[]{:S(2)}) %collective-permute-start.5) | collective-permute-done | bytes 1056 | tf_op jit(solution)/shard_map/ppermute | solution.py:207
  34.0 1.2 %collective-permute-done.6 = f32[4,256]{1,0:T(4,128)S(1)} collective-permute-done((f32[4,256]{1,0:T(4,128)S(1)}, f32[4,256]{1,0:T(4,128)S(1)}, u32[]{:S(2)}, u32[]{:S(2)}) %collective-permute-start.6) | collective-permute-done | bytes 4128 | tf_op jit(solution)/shard_map/ppermute | solution.py:211
  35.2 1.6 %collective-permute-start.7 = (f32[4,256]{1,0:T(4,128)S(1)}, f32[4,256]{1,0:T(4,128)S(1)}, u32[]{:S(2)}, u32[]{:S(2)}) collective-permute-start(f32[4,256]{1,0:T(4,128)S(1)} %fusion), channel_id=1, source_target_pairs={{0,8},{4,12},{8,0},{12,4},{16,24},{20,28},{24,16},{28,20},{32,40},... | collective-permute-start | bytes 12296 | tf_op jit(solution)/shard_map/ppermute | solution.py:211
  36.7 2.2 %collective-permute-done.7 = f32[4,256]{1,0:T(4,128)S(1)} collective-permute-done((f32[4,256]{1,0:T(4,128)S(1)}, f32[4,256]{1,0:T(4,128)S(1)}, u32[]{:S(2)}, u32[]{:S(2)}) %collective-permute-start.7) | collective-permute-done | bytes 4128 | tf_op jit(solution)/shard_map/ppermute | solution.py:211
  38.9 3.1 %collective-permute-start.8 = (f32[4,256]{1,0:T(4,128)S(1)}, f32[4,256]{1,0:T(4,128)S(1)}, u32[]{:S(2)}, u32[]{:S(2)}) collective-permute-start(f32[4,256]{1,0:T(4,128)S(1)} %fusion.3), channel_id=1, source_target_pairs={{0,16},{4,20},{8,24},{12,28},{16,0},{20,4},{24,8},{28,12},{32,48},... | collective-permute-start | bytes 12296 | tf_op jit(solution)/shard_map/ppermute | solution.py:211
  42.0 2.3 %collective-permute-done.8 = f32[4,256]{1,0:T(4,128)S(1)} collective-permute-done((f32[4,256]{1,0:T(4,128)S(1)}, f32[4,256]{1,0:T(4,128)S(1)}, u32[]{:S(2)}, u32[]{:S(2)}) %collective-permute-start.8) | collective-permute-done | bytes 4128 | tf_op jit(solution)/shard_map/ppermute | solution.py:211
  44.3 12.4 %all-to-all-done.own = bf16[64,32,256]{2,1,0:T(8,128)(2,1)S(1)} async-done(((bf16[64,32,256]{2,1,0:T(8,128)(2,1)}), bf16[64,32,256]{2,1,0:T(8,128)(2,1)S(1)}, u32[]{:S(2)}, u32[]{:S(2)}) %all-to-all-start) | async-done | bytes 1048608 | tf_op jit(solution)/shard_map/all_to_all | solution.py:205
  56.8 2.0 %collective-permute-start.11 = (bf16[32,32,256]{2,1,0:T(8,128)(2,1)S(1)}, bf16[32,32,256]{2,1,0:T(8,128)(2,1)S(1)}, u32[]{:S(2)}, u32[]{:S(2)}) collective-permute-start(bf16[32,32,256]{2,1,0:T(8,128)(2,1)S(1)} %get-tuple-element.36), channel_id=1, source_target_pairs={{0,1},{1,2},{2,3},{3,0},{4,5},{5,6},{6,7},{7,4},{8,9},{9,10},{10,1... | collective-permute-start | bytes 1572872 | tf_op jit(solution)/shard_map/ppermute | solution.py:218
  58.8 1.4 %collective-permute-start.9 = (f32[4,256]{1,0:T(4,128)S(1)}, f32[4,256]{1,0:T(4,128)S(1)}, u32[]{:S(2)}, u32[]{:S(2)}) collective-permute-start(f32[4,256]{1,0:T(4,128)S(1)} %add.20), channel_id=1, source_target_pairs={{0,32},{4,36},{8,40},{12,44},{16,48},{20,52},{24,56},{28,60},{32,0... | collective-permute-start | bytes 12296 | tf_op jit(solution)/shard_map/ppermute | solution.py:211
  60.3 2.2 %collective-permute-done.9 = f32[4,256]{1,0:T(4,128)S(1)} collective-permute-done((f32[4,256]{1,0:T(4,128)S(1)}, f32[4,256]{1,0:T(4,128)S(1)}, u32[]{:S(2)}, u32[]{:S(2)}) %collective-permute-start.9) | collective-permute-done | bytes 4128 | tf_op jit(solution)/shard_map/ppermute | solution.py:211
  62.5 1.0 %fusion.1 = (bf16[32,32,256]{2,1,0:T(8,128)(2,1)}, bf16[32,32,256]{2,1,0:T(8,128)(2,1)}) fusion(bf16[64,32,256]{2,1,0:T(8,128)(2,1)S(1)} %all-to-all-done.own), kind=kLoop, calls=%fused_computation.2 | loop fusion | bytes 2097152 | tf_op jit(solution)/shard_map/slice | solution.py:222
  63.5 3.2 %collective-permute-start.10 = (bf16[32,32,256]{2,1,0:T(8,128)(2,1)}, bf16[32,32,256]{2,1,0:T(8,128)(2,1)}, u32[]{:S(2)}, u32[]{:S(2)}) collective-permute-start(bf16[32,32,256]{2,1,0:T(8,128)(2,1)} %get-tuple-element.34), channel_id=1, source_target_pairs={{0,3},{1,0},{2,1},{3,2},{4,7},{5,4},{6,5},{7,6},{8,11},{9,8},{10,9... | collective-permute-start | bytes 1572872 | tf_op jit(solution)/shard_map/ppermute | solution.py:223
  66.7 2.6 %collective-permute-start.13 = (f32[4,256]{1,0:T(4,128)S(1)}, f32[4,256]{1,0:T(4,128)S(1)}, u32[]{:S(2)}, u32[]{:S(2)}) collective-permute-start(f32[4,256]{1,0:T(4,128)S(1)} %add.21), channel_id=1, source_target_pairs={{0,64},{4,68},{8,72},{12,76},{16,80},{20,84},{24,88},{28,92},{32,9... | collective-permute-start | bytes 12296 | tf_op jit(solution)/shard_map/ppermute | solution.py:211
  69.4 1.9 %collective-permute-done.13 = f32[4,256]{1,0:T(4,128)S(1)} collective-permute-done((f32[4,256]{1,0:T(4,128)S(1)}, f32[4,256]{1,0:T(4,128)S(1)}, u32[]{:S(2)}, u32[]{:S(2)}) %collective-permute-start.13) | collective-permute-done | bytes 4128 | tf_op jit(solution)/shard_map/ppermute | solution.py:211
  71.6 1.5 %collective-permute-done.11.left_a = bf16[32,32,256]{2,1,0:T(8,128)(2,1)S(1)} collective-permute-done((bf16[32,32,256]{2,1,0:T(8,128)(2,1)S(1)}, bf16[32,32,256]{2,1,0:T(8,128)(2,1)S(1)}, u32[]{:S(2)}, u32[]{:S(2)}) %collective-permute-start.11) | collective-permute-done | bytes 524320 | tf_op jit(solution)/shard_map/ppermute | solution.py:218
  73.1 2.0 %collective-permute-start.16 = (bf16[32,32,256]{2,1,0:T(8,128)(2,1)S(1)}, bf16[32,32,256]{2,1,0:T(8,128)(2,1)S(1)}, u32[]{:S(2)}, u32[]{:S(2)}) collective-permute-start(bf16[32,32,256]{2,1,0:T(8,128)(2,1)S(1)} %collective-permute-done.11.left_a), channel_id=1, source_target_pairs={{0,1},{1,2},{2,3},{3,0},{4,5},{5,6},{6,7},{7,4},{8,9},{9,10},{10,1... | collective-permute-start | bytes 1572872 | tf_op jit(solution)/shard_map/ppermute | solution.py:226
  75.1 3.2 %collective-permute-start.15 = (f32[4,256]{1,0:T(4,128)S(1)}, f32[4,256]{1,0:T(4,128)S(1)}, u32[]{:S(2)}, u32[]{:S(2)}) collective-permute-start(f32[4,256]{1,0:T(4,128)S(1)} %add.22), channel_id=1, source_target_pairs={{0,128},{4,132},{8,136},{12,140},{16,144},{20,148},{24,152},{28,15... | collective-permute-start | bytes 12296 | tf_op jit(solution)/shard_map/ppermute | solution.py:211
  78.2 4.4 %collective-permute-done.15 = f32[4,256]{1,0:T(4,128)S(1)} collective-permute-done((f32[4,256]{1,0:T(4,128)S(1)}, f32[4,256]{1,0:T(4,128)S(1)}, u32[]{:S(2)}, u32[]{:S(2)}) %collective-permute-start.15) | collective-permute-done | bytes 4128 | tf_op jit(solution)/shard_map/ppermute | solution.py:211
  82.6 1.8 %collective-permute-done.14.left_b = bf16[32,32,256]{2,1,0:T(8,128)(2,1)} collective-permute-done((bf16[32,32,256]{2,1,0:T(8,128)(2,1)}, bf16[32,32,256]{2,1,0:T(8,128)(2,1)}, u32[]{:S(2)}, u32[]{:S(2)}) %collective-permute-start.14) | collective-permute-done | bytes 524320 | tf_op jit(solution)/shard_map/ppermute | solution.py:222
  84.4 6.1 %gram_near.1 = (f32[2,2,256,1024]{3,2,1,0:T(8,128)}, bf16[2,512,1024]{2,1,0:T(8,128)(2,1)S(1)}) custom-call(s32[1]{0:T(128)} %bitcast.col, bf16[64,32,256]{2,1,0:T(8,128)(2,1)S(1)} %all-to-all-done.own, bf16[32,32,256]{2,1,0:T(8,128)(2,1)} %collective-permute-done.10.right_a, bf16[32,32,256]{2,1,0:T(8,128)(2,1)S(1)} %collective-permute-done.12.right_b, ...), custom_call_target="tpu_custom_call" | custom-call | flops 1610612736 | bytes 8388608 | tf_op jit(solution)/shard_map/gram_near/pallas_call | solution.py:248
  90.5 2.8 %collective-permute-done.17.far_b = bf16[32,32,256]{2,1,0:T(8,128)(2,1)S(1)} collective-permute-done((bf16[32,32,256]{2,1,0:T(8,128)(2,1)S(1)}, bf16[32,32,256]{2,1,0:T(8,128)(2,1)S(1)}, u32[]{:S(2)}, u32[]{:S(2)}) %collective-permute-start.17) | collective-permute-done | bytes 524320 | tf_op jit(solution)/shard_map/ppermute | solution.py:227
  93.4 1.5 %collective-permute-done.16.far_a = bf16[32,32,256]{2,1,0:T(8,128)(2,1)S(1)} collective-permute-done((bf16[32,32,256]{2,1,0:T(8,128)(2,1)S(1)}, bf16[32,32,256]{2,1,0:T(8,128)(2,1)S(1)}, u32[]{:S(2)}, u32[]{:S(2)}) %collective-permute-start.16) | collective-permute-done | bytes 524320 | tf_op jit(solution)/shard_map/ppermute | solution.py:226
  94.8 1.8 %gram_far.1 = f32[2,2,256,1024]{3,2,1,0:T(8,128)} custom-call(s32[1]{0:T(128)} %bitcast.col, bf16[2,512,1024]{2,1,0:T(8,128)(2,1)S(1)} %get-tuple-element.31.lhs, bf16[32,32,256]{2,1,0:T(8,128)(2,1)S(1)} %collective-permute-done.16.far_a, bf16[32,32,256]{2,1,0:T(8,128)(2,1)S(1)} %collective-permute-done.17.far_b, ...), custom_call_target="tpu_custom_call", output_to_operand_aliasing={{}: (5, {})} | custom-call | flops 536870912 | bytes 4194304 | tf_op jit(solution)/shard_map/gram_far/pallas_call | solution.py:263
  (26 shorter events, 2.8 us)
Async XLA Ops:
  0.0 1.0 %copy-start = (bf16[2,512,256]{2,1,0:T(8,128)(2,1)S(1)}, bf16[2,512,256]{2,1,0:T(8,128)(2,1)}, u32[]{:S(2)}) copy-start(bf16[2,512,256]{2,1,0:T(8,128)(2,1)} %constant.6.clone.tables) | copy-start | bytes 1572868
  1.0 10.8 %copy-start.1 = (f32[128]{0:T(128)S(1)}, f32[128]{0:T(128)}, u32[]{:S(2)}) copy-start(f32[128]{0:T(128)} %param.4) | copy-start | bytes 1540
  6.7 5.4 %collective-permute-start.2 = (f32[8,128]{1,0:T(8,128)S(1)}, f32[8,128]{1,0:T(8,128)S(1)}, u32[]{:S(2)}, u32[]{:S(2)}) collective-permute-start(f32[8,128]{1,0:T(8,128)S(1)} %get-tuple-element.21.p0), channel_id=1, source_target_pairs={{0,2},{1,3},{2,0},{3,1},{4,6},{5,7},{6,4},{7,5},{8,10},{9,11},{10,... | collective-permute-start | bytes 12296 | tf_op jit(solution)/shard_map/ppermute | solution.py:188
  9.8 3.6 %collective-permute-start.1 = (f32[8,128]{1,0:T(8,128)S(1)}, f32[8,128]{1,0:T(8,128)S(1)}, u32[]{:S(2)}, u32[]{:S(2)}) collective-permute-start(f32[8,128]{1,0:T(8,128)S(1)} %get-tuple-element.21.p0), channel_id=1, source_target_pairs={{0,3},{1,0},{2,1},{3,2},{4,7},{5,4},{6,5},{7,6},{8,11},{9,8},{10,9... | collective-permute-start | bytes 12296 | tf_op jit(solution)/shard_map/ppermute | solution.py:188
  10.9 4.8 %collective-permute-start = (f32[8,128]{1,0:T(8,128)S(1)}, f32[8,128]{1,0:T(8,128)S(1)}, u32[]{:S(2)}, u32[]{:S(2)}) collective-permute-start(f32[8,128]{1,0:T(8,128)S(1)} %get-tuple-element.21.p0), channel_id=1, source_target_pairs={{0,1},{1,2},{2,3},{3,0},{4,5},{5,6},{6,7},{7,4},{8,9},{9,10},{10,1... | collective-permute-start | bytes 12296 | tf_op jit(solution)/shard_map/ppermute | solution.py:188
  17.0 39.7 %all-to-all-start = ((bf16[64,32,256]{2,1,0:T(8,128)(2,1)}), bf16[64,32,256]{2,1,0:T(8,128)(2,1)S(1)}, u32[]{:S(2)}, u32[]{:S(2)}) async-start(bf16[64,32,256]{2,1,0:T(8,128)(2,1)} %get-tuple-element.22), calls=%async_computation | async-start | bytes 2097152 | tf_op jit(solution)/shard_map/all_to_all | solution.py:205
  28.7 5.2 %collective-permute-start.5 = (f32[1,256]{1,0:T(1,128)S(1)}, f32[1,256]{1,0:T(1,128)S(1)}, u32[]{:S(2)}, u32[]{:S(2)}) collective-permute-start(f32[1,256]{1,0:T(1,128)S(1)} %get-tuple-element.23), channel_id=1, source_target_pairs={{0,2},{1,3},{2,0},{3,1},{4,6},{5,7},{6,4},{7,5},{8,10},{9,11},{10,... | collective-permute-start | bytes 3080 | tf_op jit(solution)/shard_map/ppermute | solution.py:207
  29.1 4.8 %collective-permute-start.4 = (f32[1,256]{1,0:T(1,128)S(1)}, f32[1,256]{1,0:T(1,128)S(1)}, u32[]{:S(2)}, u32[]{:S(2)}) collective-permute-start(f32[1,256]{1,0:T(1,128)S(1)} %get-tuple-element.23), channel_id=1, source_target_pairs={{0,1},{1,2},{2,3},{3,0},{4,5},{5,6},{6,7},{7,4},{8,9},{9,10},{10,1... | collective-permute-start | bytes 3080 | tf_op jit(solution)/shard_map/ppermute | solution.py:207
  29.7 4.2 %collective-permute-start.3 = (f32[1,256]{1,0:T(1,128)S(1)}, f32[1,256]{1,0:T(1,128)S(1)}, u32[]{:S(2)}, u32[]{:S(2)}) collective-permute-start(f32[1,256]{1,0:T(1,128)S(1)} %get-tuple-element.23), channel_id=1, source_target_pairs={{0,3},{1,0},{2,1},{3,2},{4,7},{5,4},{6,5},{7,6},{8,11},{9,8},{10,9... | collective-permute-start | bytes 3080 | tf_op jit(solution)/shard_map/ppermute | solution.py:207
  33.9 1.3 %collective-permute-start.6 = (f32[4,256]{1,0:T(4,128)S(1)}, f32[4,256]{1,0:T(4,128)S(1)}, u32[]{:S(2)}, u32[]{:S(2)}) collective-permute-start(f32[4,256]{1,0:T(4,128)S(1)} %pad_maximum_fusion), channel_id=1, source_target_pairs={{0,4},{4,0},{8,12},{12,8},{16,20},{20,16},{24,28},{28,24},{32,36},... | collective-permute-start | bytes 12296 | tf_op jit(solution)/shard_map/ppermute | solution.py:211
  35.2 3.7 %collective-permute-start.7 = (f32[4,256]{1,0:T(4,128)S(1)}, f32[4,256]{1,0:T(4,128)S(1)}, u32[]{:S(2)}, u32[]{:S(2)}) collective-permute-start(f32[4,256]{1,0:T(4,128)S(1)} %fusion), channel_id=1, source_target_pairs={{0,8},{4,12},{8,0},{12,4},{16,24},{20,28},{24,16},{28,20},{32,40},... | collective-permute-start | bytes 12296 | tf_op jit(solution)/shard_map/ppermute | solution.py:211
  38.9 5.4 %collective-permute-start.8 = (f32[4,256]{1,0:T(4,128)S(1)}, f32[4,256]{1,0:T(4,128)S(1)}, u32[]{:S(2)}, u32[]{:S(2)}) collective-permute-start(f32[4,256]{1,0:T(4,128)S(1)} %fusion.3), channel_id=1, source_target_pairs={{0,16},{4,20},{8,24},{12,28},{16,0},{20,4},{24,8},{28,12},{32,48},... | collective-permute-start | bytes 12296 | tf_op jit(solution)/shard_map/ppermute | solution.py:211
  56.7 14.8 %collective-permute-start.12 = (bf16[32,32,256]{2,1,0:T(8,128)(2,1)S(1)}, bf16[32,32,256]{2,1,0:T(8,128)(2,1)S(1)}, u32[]{:S(2)}, u32[]{:S(2)}) collective-permute-start(bf16[32,32,256]{2,1,0:T(8,128)(2,1)S(1)} %get-tuple-element.35), channel_id=1, source_target_pairs={{0,3},{1,0},{2,1},{3,2},{4,7},{5,4},{6,5},{7,6},{8,11},{9,8},{10,9... | collective-permute-start | bytes 1572872 | tf_op jit(solution)/shard_map/ppermute | solution.py:219
  56.8 16.2 %collective-permute-start.11 = (bf16[32,32,256]{2,1,0:T(8,128)(2,1)S(1)}, bf16[32,32,256]{2,1,0:T(8,128)(2,1)S(1)}, u32[]{:S(2)}, u32[]{:S(2)}) collective-permute-start(bf16[32,32,256]{2,1,0:T(8,128)(2,1)S(1)} %get-tuple-element.36), channel_id=1, source_target_pairs={{0,1},{1,2},{2,3},{3,0},{4,5},{5,6},{6,7},{7,4},{8,9},{9,10},{10,1... | collective-permute-start | bytes 1572872 | tf_op jit(solution)/shard_map/ppermute | solution.py:218
  58.8 3.6 %collective-permute-start.9 = (f32[4,256]{1,0:T(4,128)S(1)}, f32[4,256]{1,0:T(4,128)S(1)}, u32[]{:S(2)}, u32[]{:S(2)}) collective-permute-start(f32[4,256]{1,0:T(4,128)S(1)} %add.20), channel_id=1, source_target_pairs={{0,32},{4,36},{8,40},{12,44},{16,48},{20,52},{24,56},{28,60},{32,0... | collective-permute-start | bytes 12296 | tf_op jit(solution)/shard_map/ppermute | solution.py:211
  63.5 20.9 %collective-permute-start.14 = (bf16[32,32,256]{2,1,0:T(8,128)(2,1)}, bf16[32,32,256]{2,1,0:T(8,128)(2,1)}, u32[]{:S(2)}, u32[]{:S(2)}) collective-permute-start(bf16[32,32,256]{2,1,0:T(8,128)(2,1)} %get-tuple-element.33), channel_id=1, source_target_pairs={{0,1},{1,2},{2,3},{3,0},{4,5},{5,6},{6,7},{7,4},{8,9},{9,10},{10,1... | collective-permute-start | bytes 1572872 | tf_op jit(solution)/shard_map/ppermute | solution.py:222
  63.5 20.9 %collective-permute-start.10 = (bf16[32,32,256]{2,1,0:T(8,128)(2,1)}, bf16[32,32,256]{2,1,0:T(8,128)(2,1)}, u32[]{:S(2)}, u32[]{:S(2)}) collective-permute-start(bf16[32,32,256]{2,1,0:T(8,128)(2,1)} %get-tuple-element.34), channel_id=1, source_target_pairs={{0,3},{1,0},{2,1},{3,2},{4,7},{5,4},{6,5},{7,6},{8,11},{9,8},{10,9... | collective-permute-start | bytes 1572872 | tf_op jit(solution)/shard_map/ppermute | solution.py:223
  66.7 4.5 %collective-permute-start.13 = (f32[4,256]{1,0:T(4,128)S(1)}, f32[4,256]{1,0:T(4,128)S(1)}, u32[]{:S(2)}, u32[]{:S(2)}) collective-permute-start(f32[4,256]{1,0:T(4,128)S(1)} %add.21), channel_id=1, source_target_pairs={{0,64},{4,68},{8,72},{12,76},{16,80},{20,84},{24,88},{28,92},{32,9... | collective-permute-start | bytes 12296 | tf_op jit(solution)/shard_map/ppermute | solution.py:211
  73.1 20.3 %collective-permute-start.17 = (bf16[32,32,256]{2,1,0:T(8,128)(2,1)S(1)}, bf16[32,32,256]{2,1,0:T(8,128)(2,1)S(1)}, u32[]{:S(2)}, u32[]{:S(2)}) collective-permute-start(bf16[32,32,256]{2,1,0:T(8,128)(2,1)S(1)} %collective-permute-done.12.right_b), channel_id=1, source_target_pairs={{0,3},{1,0},{2,1},{3,2},{4,7},{5,4},{6,5},{7,6},{8,11},{9,8},{10,9... | collective-permute-start | bytes 1572872 | tf_op jit(solution)/shard_map/ppermute | solution.py:227
  73.1 21.8 %collective-permute-start.16 = (bf16[32,32,256]{2,1,0:T(8,128)(2,1)S(1)}, bf16[32,32,256]{2,1,0:T(8,128)(2,1)S(1)}, u32[]{:S(2)}, u32[]{:S(2)}) collective-permute-start(bf16[32,32,256]{2,1,0:T(8,128)(2,1)S(1)} %collective-permute-done.11.left_a), channel_id=1, source_target_pairs={{0,1},{1,2},{2,3},{3,0},{4,5},{5,6},{6,7},{7,4},{8,9},{9,10},{10,1... | collective-permute-start | bytes 1572872 | tf_op jit(solution)/shard_map/ppermute | solution.py:226
  75.1 7.5 %collective-permute-start.15 = (f32[4,256]{1,0:T(4,128)S(1)}, f32[4,256]{1,0:T(4,128)S(1)}, u32[]{:S(2)}, u32[]{:S(2)}) collective-permute-start(f32[4,256]{1,0:T(4,128)S(1)} %add.22), channel_id=1, source_target_pairs={{0,128},{4,132},{8,136},{12,140},{16,144},{20,148},{24,152},{28,15... | collective-permute-start | bytes 12296 | tf_op jit(solution)/shard_map/ppermute | solution.py:211

commit v5 on v4

--- a/solution.py
+++ b/solution.py
@@ -32,7 +32,7 @@
     return jnp.dot(a, b, preferred_element_type=F32)
 
 
-def spectra_kernel(records, tables, even, odd, power, held, results, arrived):
+def spectra_kernel(records, tables, results, power, held, arrived):
     windows, _, samples = records.shape
     half = samples // 2
     kept = tables.shape[2] // 2
@@ -47,34 +47,38 @@
     taper = 0.5 - 0.5 * jnp.cos(steps * (2.0 * math.pi / samples))
 
     chan = records.shape[1]
-    for pair in range(0, windows + 2, 2):
-        if pair < windows:
-            fetch(pair).wait()
-            fetch(pair + 1).wait()
-            tapered = held[pair : pair + 2].reshape(2 * chan, samples) * taper
-            first, second = tapered[:, :half], tapered[:, half:]
-            rows = [[], []]
-            for parity in range(2):
-                folded = first + second if parity == 0 else first - second
-                high = folded.astype(BF)
-                low = (folded - high.astype(F32)).astype(BF)
-                both = dot(high, tables[parity])
-                result = both[:, :kept] + both[:, kept:] + dot(low, tables[parity, :, :kept])
-                square = result * result
-                for i in range(2):
-                    part = slice(i * chan, i * chan + chan)
-                    results[pair + i, parity] = result[part]
-                    total = jnp.sum(square[part], axis=0, keepdims=True)
-                    rows[i].append(total[:, :bins] + total[:, bins:])
+    for pair in range(0, windows, 2):
+        fetch(pair).wait()
+        fetch(pair + 1).wait()
+        tapered = held[pair : pair + 2].reshape(2 * chan, samples) * taper
+        first, second = tapered[:, :half], tapered[:, half:]
+        rows = [[], []]
+        for parity in range(2):
+            folded = first + second if parity == 0 else first - second
+            high = folded.astype(BF)
+            low = (folded - high.astype(F32)).astype(BF)
+            both = dot(high, tables[parity])
+            result = both[:, :kept] + both[:, kept:] + dot(low, tables[parity, :, :kept])
+            square = result * result
             for i in range(2):
-                power[pair + i : pair + i + 1, :] = jnp.concatenate(rows[i], axis=1)
-        for w in range(pair - 2, pair) if pair else ():
-            for parity, spec in enumerate((even, odd)):
-                turned = jnp.transpose(results[w, parity])
-                for side in range(2):
-                    lanes = slice(128 * side, 128 * side + 128)
-                    spec[side, pl.ds(w, bins, stride=16), :] = turned[:bins, lanes]
-                    spec[side, pl.ds(8 + w, bins, stride=16), :] = turned[bins:, lanes]
+                part = slice(i * chan, i * chan + chan)
+                results[pair + i, parity] = result[part]
+                total = jnp.sum(square[part], axis=0, keepdims=True)
+                rows[i].append(total[:, :bins] + total[:, bins:])
+        for i in range(2):
+            power[pair + i : pair + i + 1, :] = jnp.concatenate(rows[i], axis=1)
+
+
+def turn_kernel(results, even, odd):
+    windows, _, _, kept = results.shape
+    bins = kept // 2
+    for w in range(windows):
+        for parity, spec in enumerate((even, odd)):
+            turned = jnp.transpose(results[w, parity])
+            for side in range(2):
+                lanes = slice(128 * side, 128 * side + 128)
+                spec[side, pl.ds(w, bins, stride=16), :] = turned[:bins, lanes]
+                spec[side, pl.ds(8 + w, bins, stride=16), :] = turned[bins:, lanes]
 
 
 def whiten_kernel(channels, even, odd, p0, p1, p2, p3, weight, message, energy, held, sent):
@@ -165,20 +169,19 @@
     kept = bin_weight.shape[0]
     bins = kept // 2
     spec_shape = (2, bins * 16, 128)
-    even, odd, power = pl.pallas_call(
+    result_shape = (windows, 2, chan, kept)
+    results, power = pl.pallas_call(
         spectra_kernel,
         in_specs=[
             pl.BlockSpec(memory_space=pltpu.HBM),
             pl.BlockSpec(memory_space=pltpu.VMEM),
         ],
         out_shape=[
-            jax.ShapeDtypeStruct(spec_shape, F32),
-            jax.ShapeDtypeStruct(spec_shape, F32),
+            jax.ShapeDtypeStruct(result_shape, F32),
             jax.ShapeDtypeStruct((windows, kept), F32),
         ],
         scratch_shapes=[
             pltpu.VMEM((windows, chan, samples), F32),
-            pltpu.VMEM((windows, 2, chan, kept), F32),
             pltpu.SemaphoreType.DMA((windows,)),
         ],
         compiler_params=pltpu.CompilerParams(vmem_limit_bytes=50 << 20),
@@ -186,6 +189,13 @@
     )(records, split_tables(samples, kept))
     ahead, back, across = ring(columns, 1), ring(columns, columns - 1), ring(columns, 2)
     powers = [power] + [lax.ppermute(power, "col", p) for p in (ahead, back, across)]
+    even, odd = pl.pallas_call(
+        turn_kernel,
+        out_shape=[jax.ShapeDtypeStruct(spec_shape, F32)] * 2,
+        compiler_params=pltpu.CompilerParams(vmem_limit_bytes=10 << 20),
+        cost_estimate=pl.CostEstimate(flops=0, bytes_accessed=6 << 20, transcendentals=0),
+        name="turn",
+    )(results)
     weight = bin_weight.reshape(bins, 2).T.reshape(1, kept)
     message, energy = pl.pallas_call(
         functools.partial(whiten_kernel, chan * columns),

time: 96.9 us -> 96.4 us (level)
  waiting for transfers between devices: 39.5 us -> 38.2 us
    ppermute x3, waiting for transfers between devices: 3.64 us -> 2.47 us  [body(): lax.ppermute(power, 'col', p)]
    pallas_call x0 -> x1, Pallas kernels: none -> 1.16 us  [body(): pl.pallas_call(turn_kernel, out_shape=[jax.ShapeDtypeStruct(spec_shape, F...]
  transfers between devices with their start and end apart: 19 -> 19, of which waited for: 15 -> 15; matrix products, arithmetic and copies ran while one was open for 1% -> 1% of each run, Pallas kernels for 6% -> 8%
where the time goes in v5:
time: 96.4 us; the launch traced here: 96.2 us
  starting transfers between devices  40 us (41%)
  waiting for transfers between devices  38.2 us (40%)
  Pallas kernels  15.4 us (16%)
  local copies, waits for them, and re-layouts  2.45 us (3%)
    ppermute x6, waiting for transfers between devices, fold(): lax.ppermute(value, 'wa', [(i, i ^ step) for i in range(owners)])  14.1 us
    all_to_all x1, waiting for transfers between devices, body(): lax.all_to_all(message, 'wa', split_axis=0, concat_axis=0, tiled=True)  12.4 us
    ppermute x6, starting transfers between devices, fold(): lax.ppermute(value, 'wa', [(i, i ^ step) for i in range(owners)])  11.9 us
    all_to_all x1, starting transfers between devices, body(): lax.all_to_all(message, 'wa', split_axis=0, concat_axis=0, tiled=True)  11.8 us
    pallas_call x1, Pallas kernels, body(): pl.pallas_call(functools.partial(gram_near_kernel, scale), grid_spec=pltp...  6.14 us
    pallas_call x1, Pallas kernels, body(): pl.pallas_call(spectra_kernel, in_specs=[pl.BlockSpec(memory_space=pltpu....  5.13 us
    ppermute x3, starting transfers between devices, body(): lax.ppermute(power, 'col', p)  5.13 us
    ppermute x3, starting transfers between devices, body(): lax.ppermute(energy, 'col', p)  3.62 us
  transfers between devices with their start and end apart: 19, of which 15 were waited for; matrix products, arithmetic and copies ran while one was open for 1% of the time, Pallas kernels for 8%

profile of v5, /device:TPU:32, one launch (start us, length us, event | category | flops | bytes accessed | tf_op | source)
XLA Modules:
  0.0 96.2 jit_solution(17794862826832772844)
XLA Ops:
  0.0 1.0 %copy-done = bf16[2,512,256]{2,1,0:T(8,128)(2,1)S(1)} copy-done((bf16[2,512,256]{2,1,0:T(8,128)(2,1)S(1)}, bf16[2,512,256]{2,1,0:T(8,128)(2,1)}, u32[]{:S(2)}) %copy-start) | copy-done | bytes 524312
  1.0 5.1 %spectra.1 = (f32[8,2,256,128]{3,2,1,0:T(8,128)S(1)}, f32[8,128]{1,0:T(8,128)S(1)}) custom-call(f32[8,256,1024]{2,1,0:T(8,128)} %records.1, bf16[2,512,256]{2,1,0:T(8,128)(2,1)S(1)} %copy-done), custom_call_target="tpu_custom_call" | custom-call | tf_op jit(solution)/shard_map/spectra/pallas_call | solution.py:173
  6.2 3.1 %collective-permute-start.2 = (f32[8,128]{1,0:T(8,128)S(1)}, f32[8,128]{1,0:T(8,128)S(1)}, u32[]{:S(2)}, u32[]{:S(2)}) collective-permute-start(f32[8,128]{1,0:T(8,128)S(1)} %get-tuple-element.23.p0), channel_id=1, source_target_pairs={{0,2},{1,3},{2,0},{3,1},{4,6},{5,7},{6,4},{7,5},{8,10},{9,11},{10,... | collective-permute-start | bytes 12296 | tf_op jit(solution)/shard_map/ppermute | solution.py:191
  9.3 1.1 %collective-permute-start.1 = (f32[8,128]{1,0:T(8,128)S(1)}, f32[8,128]{1,0:T(8,128)S(1)}, u32[]{:S(2)}, u32[]{:S(2)}) collective-permute-start(f32[8,128]{1,0:T(8,128)S(1)} %get-tuple-element.23.p0), channel_id=1, source_target_pairs={{0,3},{1,0},{2,1},{3,2},{4,7},{5,4},{6,5},{7,6},{8,11},{9,8},{10,9... | collective-permute-start | bytes 12296 | tf_op jit(solution)/shard_map/ppermute | solution.py:191
  11.6 1.2 %turn.1 = (f32[2,1024,128]{2,1,0:T(8,128)S(1)}, f32[2,1024,128]{2,1,0:T(8,128)S(1)}) custom-call(f32[8,2,256,128]{3,2,1,0:T(8,128)S(1)} %get-tuple-element.20.results), custom_call_target="tpu_custom_call" | custom-call | bytes 6291456 | tf_op jit(solution)/shard_map/turn/pallas_call | solution.py:192
  12.9 2.4 %collective-permute-done.p1 = f32[8,128]{1,0:T(8,128)S(1)} collective-permute-done((f32[8,128]{1,0:T(8,128)S(1)}, f32[8,128]{1,0:T(8,128)S(1)}, u32[]{:S(2)}, u32[]{:S(2)}) %collective-permute-start) | collective-permute-done | bytes 4128 | tf_op jit(solution)/shard_map/ppermute | solution.py:191
  15.3 1.2 %whiten.1 = (bf16[64,32,256]{2,1,0:T(8,128)(2,1)}, f32[1,256]{1,0:T(1,128)S(1)}) custom-call(f32[2,1024,128]{2,1,0:T(8,128)S(1)} %get-tuple-element.21.even, f32[2,1024,128]{2,1,0:T(8,128)S(1)} %get-tuple-element.22.odd, f32[8,128]{1,0:T(8,128)S(1)} %get-tuple-element.23.p0, f32[8,128]{1,0:T(8,128)S(1)} %collective-permute-done.p1, ...), custom_call_target="tpu_custom_call" | custom-call | tf_op jit(solution)/shard_map/whiten/pallas_call | solution.py:200
  16.5 11.8 %all-to-all-start = ((bf16[64,32,256]{2,1,0:T(8,128)(2,1)}), bf16[64,32,256]{2,1,0:T(8,128)(2,1)S(1)}, u32[]{:S(2)}, u32[]{:S(2)}) async-start(bf16[64,32,256]{2,1,0:T(8,128)(2,1)} %get-tuple-element.24), calls=%async_computation | async-start | bytes 2097152 | tf_op jit(solution)/shard_map/all_to_all | solution.py:215
  29.2 2.7 %collective-permute-start.3 = (f32[1,256]{1,0:T(1,128)S(1)}, f32[1,256]{1,0:T(1,128)S(1)}, u32[]{:S(2)}, u32[]{:S(2)}) collective-permute-start(f32[1,256]{1,0:T(1,128)S(1)} %get-tuple-element.25), channel_id=1, source_target_pairs={{0,3},{1,0},{2,1},{3,2},{4,7},{5,4},{6,5},{7,6},{8,11},{9,8},{10,9... | collective-permute-start | bytes 3080 | tf_op jit(solution)/shard_map/ppermute | solution.py:217
  31.9 1.5 %collective-permute-done.5 = f32[1,256]{1,0:T(1,128)S(1)} collective-permute-done((f32[1,256]{1,0:T(1,128)S(1)}, f32[1,256]{1,0:T(1,128)S(1)}, u32[]{:S(2)}, u32[]{:S(2)}) %collective-permute-start.5) | collective-permute-done | bytes 1056 | tf_op jit(solution)/shard_map/ppermute | solution.py:217
  33.5 1.2 %collective-permute-done.6 = f32[4,256]{1,0:T(4,128)S(1)} collective-permute-done((f32[4,256]{1,0:T(4,128)S(1)}, f32[4,256]{1,0:T(4,128)S(1)}, u32[]{:S(2)}, u32[]{:S(2)}) %collective-permute-start.6) | collective-permute-done | bytes 4128 | tf_op jit(solution)/shard_map/ppermute | solution.py:221
  34.7 1.6 %collective-permute-start.7 = (f32[4,256]{1,0:T(4,128)S(1)}, f32[4,256]{1,0:T(4,128)S(1)}, u32[]{:S(2)}, u32[]{:S(2)}) collective-permute-start(f32[4,256]{1,0:T(4,128)S(1)} %fusion), channel_id=1, source_target_pairs={{0,8},{4,12},{8,0},{12,4},{16,24},{20,28},{24,16},{28,20},{32,40},... | collective-permute-start | bytes 12296 | tf_op jit(solution)/shard_map/ppermute | solution.py:221
  36.3 2.2 %collective-permute-done.7 = f32[4,256]{1,0:T(4,128)S(1)} collective-permute-done((f32[4,256]{1,0:T(4,128)S(1)}, f32[4,256]{1,0:T(4,128)S(1)}, u32[]{:S(2)}, u32[]{:S(2)}) %collective-permute-start.7) | collective-permute-done | bytes 4128 | tf_op jit(solution)/shard_map/ppermute | solution.py:221
  38.4 3.1 %collective-permute-start.8 = (f32[4,256]{1,0:T(4,128)S(1)}, f32[4,256]{1,0:T(4,128)S(1)}, u32[]{:S(2)}, u32[]{:S(2)}) collective-permute-start(f32[4,256]{1,0:T(4,128)S(1)} %fusion.3), channel_id=1, source_target_pairs={{0,16},{4,20},{8,24},{12,28},{16,0},{20,4},{24,8},{28,12},{32,48},... | collective-permute-start | bytes 12296 | tf_op jit(solution)/shard_map/ppermute | solution.py:221
  41.5 2.3 %collective-permute-done.8 = f32[4,256]{1,0:T(4,128)S(1)} collective-permute-done((f32[4,256]{1,0:T(4,128)S(1)}, f32[4,256]{1,0:T(4,128)S(1)}, u32[]{:S(2)}, u32[]{:S(2)}) %collective-permute-start.8) | collective-permute-done | bytes 4128 | tf_op jit(solution)/shard_map/ppermute | solution.py:221
  43.8 12.4 %all-to-all-done.own = bf16[64,32,256]{2,1,0:T(8,128)(2,1)S(1)} async-done(((bf16[64,32,256]{2,1,0:T(8,128)(2,1)}), bf16[64,32,256]{2,1,0:T(8,128)(2,1)S(1)}, u32[]{:S(2)}, u32[]{:S(2)}) %all-to-all-start) | async-done | bytes 1048608 | tf_op jit(solution)/shard_map/all_to_all | solution.py:215
  56.5 2.0 %collective-permute-start.11 = (bf16[32,32,256]{2,1,0:T(8,128)(2,1)S(1)}, bf16[32,32,256]{2,1,0:T(8,128)(2,1)S(1)}, u32[]{:S(2)}, u32[]{:S(2)}) collective-permute-start(bf16[32,32,256]{2,1,0:T(8,128)(2,1)S(1)} %get-tuple-element.38), channel_id=1, source_target_pairs={{0,1},{1,2},{2,3},{3,0},{4,5},{5,6},{6,7},{7,4},{8,9},{9,10},{10,1... | collective-permute-start | bytes 1572872 | tf_op jit(solution)/shard_map/ppermute | solution.py:228
  58.5 1.4 %collective-permute-start.9 = (f32[4,256]{1,0:T(4,128)S(1)}, f32[4,256]{1,0:T(4,128)S(1)}, u32[]{:S(2)}, u32[]{:S(2)}) collective-permute-start(f32[4,256]{1,0:T(4,128)S(1)} %add.20), channel_id=1, source_target_pairs={{0,32},{4,36},{8,40},{12,44},{16,48},{20,52},{24,56},{28,60},{32,0... | collective-permute-start | bytes 12296 | tf_op jit(solution)/shard_map/ppermute | solution.py:221
  59.9 2.2 %collective-permute-done.9 = f32[4,256]{1,0:T(4,128)S(1)} collective-permute-done((f32[4,256]{1,0:T(4,128)S(1)}, f32[4,256]{1,0:T(4,128)S(1)}, u32[]{:S(2)}, u32[]{:S(2)}) %collective-permute-start.9) | collective-permute-done | bytes 4128 | tf_op jit(solution)/shard_map/ppermute | solution.py:221
  62.2 1.1 %fusion.1 = (bf16[32,32,256]{2,1,0:T(8,128)(2,1)}, bf16[32,32,256]{2,1,0:T(8,128)(2,1)}) fusion(bf16[64,32,256]{2,1,0:T(8,128)(2,1)S(1)} %all-to-all-done.own), kind=kLoop, calls=%fused_computation.2 | loop fusion | bytes 2097152 | tf_op jit(solution)/shard_map/slice | solution.py:232
  63.2 3.2 %collective-permute-start.10 = (bf16[32,32,256]{2,1,0:T(8,128)(2,1)}, bf16[32,32,256]{2,1,0:T(8,128)(2,1)}, u32[]{:S(2)}, u32[]{:S(2)}) collective-permute-start(bf16[32,32,256]{2,1,0:T(8,128)(2,1)} %get-tuple-element.36), channel_id=1, source_target_pairs={{0,3},{1,0},{2,1},{3,2},{4,7},{5,4},{6,5},{7,6},{8,11},{9,8},{10,9... | collective-permute-start | bytes 1572872 | tf_op jit(solution)/shard_map/ppermute | solution.py:233
  66.4 2.6 %collective-permute-start.13 = (f32[4,256]{1,0:T(4,128)S(1)}, f32[4,256]{1,0:T(4,128)S(1)}, u32[]{:S(2)}, u32[]{:S(2)}) collective-permute-start(f32[4,256]{1,0:T(4,128)S(1)} %add.21), channel_id=1, source_target_pairs={{0,64},{4,68},{8,72},{12,76},{16,80},{20,84},{24,88},{28,92},{32,9... | collective-permute-start | bytes 12296 | tf_op jit(solution)/shard_map/ppermute | solution.py:221
  69.1 1.9 %collective-permute-done.13 = f32[4,256]{1,0:T(4,128)S(1)} collective-permute-done((f32[4,256]{1,0:T(4,128)S(1)}, f32[4,256]{1,0:T(4,128)S(1)}, u32[]{:S(2)}, u32[]{:S(2)}) %collective-permute-start.13) | collective-permute-done | bytes 4128 | tf_op jit(solution)/shard_map/ppermute | solution.py:221
  71.3 1.3 %collective-permute-done.11.left_a = bf16[32,32,256]{2,1,0:T(8,128)(2,1)S(1)} collective-permute-done((bf16[32,32,256]{2,1,0:T(8,128)(2,1)S(1)}, bf16[32,32,256]{2,1,0:T(8,128)(2,1)S(1)}, u32[]{:S(2)}, u32[]{:S(2)}) %collective-permute-start.11) | collective-permute-done | bytes 524320 | tf_op jit(solution)/shard_map/ppermute | solution.py:228
  72.6 2.0 %collective-permute-start.16 = (bf16[32,32,256]{2,1,0:T(8,128)(2,1)S(1)}, bf16[32,32,256]{2,1,0:T(8,128)(2,1)S(1)}, u32[]{:S(2)}, u32[]{:S(2)}) collective-permute-start(bf16[32,32,256]{2,1,0:T(8,128)(2,1)S(1)} %collective-permute-done.11.left_a), channel_id=1, source_target_pairs={{0,1},{1,2},{2,3},{3,0},{4,5},{5,6},{6,7},{7,4},{8,9},{9,10},{10,1... | collective-permute-start | bytes 1572872 | tf_op jit(solution)/shard_map/ppermute | solution.py:236
  74.6 3.2 %collective-permute-start.15 = (f32[4,256]{1,0:T(4,128)S(1)}, f32[4,256]{1,0:T(4,128)S(1)}, u32[]{:S(2)}, u32[]{:S(2)}) collective-permute-start(f32[4,256]{1,0:T(4,128)S(1)} %add.22), channel_id=1, source_target_pairs={{0,128},{4,132},{8,136},{12,140},{16,144},{20,148},{24,152},{28,15... | collective-permute-start | bytes 12296 | tf_op jit(solution)/shard_map/ppermute | solution.py:221
  77.7 4.4 %collective-permute-done.15 = f32[4,256]{1,0:T(4,128)S(1)} collective-permute-done((f32[4,256]{1,0:T(4,128)S(1)}, f32[4,256]{1,0:T(4,128)S(1)}, u32[]{:S(2)}, u32[]{:S(2)}) %collective-permute-start.15) | collective-permute-done | bytes 4128 | tf_op jit(solution)/shard_map/ppermute | solution.py:221
  82.1 1.8 %collective-permute-done.14.left_b = bf16[32,32,256]{2,1,0:T(8,128)(2,1)} collective-permute-done((bf16[32,32,256]{2,1,0:T(8,128)(2,1)}, bf16[32,32,256]{2,1,0:T(8,128)(2,1)}, u32[]{:S(2)}, u32[]{:S(2)}) %collective-permute-start.14) | collective-permute-done | bytes 524320 | tf_op jit(solution)/shard_map/ppermute | solution.py:232
  83.9 6.1 %gram_near.1 = (f32[2,2,256,1024]{3,2,1,0:T(8,128)}, bf16[2,512,1024]{2,1,0:T(8,128)(2,1)S(1)}) custom-call(s32[1]{0:T(128)} %bitcast.col, bf16[64,32,256]{2,1,0:T(8,128)(2,1)S(1)} %all-to-all-done.own, bf16[32,32,256]{2,1,0:T(8,128)(2,1)} %collective-permute-done.10.right_a, bf16[32,32,256]{2,1,0:T(8,128)(2,1)S(1)} %collective-permute-done.12.right_b, ...), custom_call_target="tpu_custom_call" | custom-call | flops 1610612736 | bytes 8388608 | tf_op jit(solution)/shard_map/gram_near/pallas_call | solution.py:258
  90.1 3.0 %collective-permute-done.17.far_b = bf16[32,32,256]{2,1,0:T(8,128)(2,1)S(1)} collective-permute-done((bf16[32,32,256]{2,1,0:T(8,128)(2,1)S(1)}, bf16[32,32,256]{2,1,0:T(8,128)(2,1)S(1)}, u32[]{:S(2)}, u32[]{:S(2)}) %collective-permute-start.17) | collective-permute-done | bytes 524320 | tf_op jit(solution)/shard_map/ppermute | solution.py:237
  93.1 1.3 %collective-permute-done.16.far_a = bf16[32,32,256]{2,1,0:T(8,128)(2,1)S(1)} collective-permute-done((bf16[32,32,256]{2,1,0:T(8,128)(2,1)S(1)}, bf16[32,32,256]{2,1,0:T(8,128)(2,1)S(1)}, u32[]{:S(2)}, u32[]{:S(2)}) %collective-permute-start.16) | collective-permute-done | bytes 524320 | tf_op jit(solution)/shard_map/ppermute | solution.py:236
  94.4 1.8 %gram_far.1 = f32[2,2,256,1024]{3,2,1,0:T(8,128)} custom-call(s32[1]{0:T(128)} %bitcast.col, bf16[2,512,1024]{2,1,0:T(8,128)(2,1)S(1)} %get-tuple-element.33.lhs, bf16[32,32,256]{2,1,0:T(8,128)(2,1)S(1)} %collective-permute-done.16.far_a, bf16[32,32,256]{2,1,0:T(8,128)(2,1)S(1)} %collective-permute-done.17.far_b, ...), custom_call_target="tpu_custom_call", output_to_operand_aliasing={{}: (5, {})} | custom-call | flops 536870912 | bytes 4194304 | tf_op jit(solution)/shard_map/gram_far/pallas_call | solution.py:273
  (27 shorter events, 3.0 us)
Async XLA Ops:
  0.0 1.0 %copy-start = (bf16[2,512,256]{2,1,0:T(8,128)(2,1)S(1)}, bf16[2,512,256]{2,1,0:T(8,128)(2,1)}, u32[]{:S(2)}) copy-start(bf16[2,512,256]{2,1,0:T(8,128)(2,1)} %constant.6.clone.tables) | copy-start | bytes 1572868
  1.0 10.3 %copy-start.1 = (f32[128]{0:T(128)S(1)}, f32[128]{0:T(128)}, u32[]{:S(2)}) copy-start(f32[128]{0:T(128)} %param.4) | copy-start | bytes 1540
  6.2 6.6 %collective-permute-start.2 = (f32[8,128]{1,0:T(8,128)S(1)}, f32[8,128]{1,0:T(8,128)S(1)}, u32[]{:S(2)}, u32[]{:S(2)}) collective-permute-start(f32[8,128]{1,0:T(8,128)S(1)} %get-tuple-element.23.p0), channel_id=1, source_target_pairs={{0,2},{1,3},{2,0},{3,1},{4,6},{5,7},{6,4},{7,5},{8,10},{9,11},{10,... | collective-permute-start | bytes 12296 | tf_op jit(solution)/shard_map/ppermute | solution.py:191
  9.3 3.6 %collective-permute-start.1 = (f32[8,128]{1,0:T(8,128)S(1)}, f32[8,128]{1,0:T(8,128)S(1)}, u32[]{:S(2)}, u32[]{:S(2)}) collective-permute-start(f32[8,128]{1,0:T(8,128)S(1)} %get-tuple-element.23.p0), channel_id=1, source_target_pairs={{0,3},{1,0},{2,1},{3,2},{4,7},{5,4},{6,5},{7,6},{8,11},{9,8},{10,9... | collective-permute-start | bytes 12296 | tf_op jit(solution)/shard_map/ppermute | solution.py:191
  10.4 4.8 %collective-permute-start = (f32[8,128]{1,0:T(8,128)S(1)}, f32[8,128]{1,0:T(8,128)S(1)}, u32[]{:S(2)}, u32[]{:S(2)}) collective-permute-start(f32[8,128]{1,0:T(8,128)S(1)} %get-tuple-element.23.p0), channel_id=1, source_target_pairs={{0,1},{1,2},{2,3},{3,0},{4,5},{5,6},{6,7},{7,4},{8,9},{9,10},{10,1... | collective-permute-start | bytes 12296 | tf_op jit(solution)/shard_map/ppermute | solution.py:191
  16.5 39.7 %all-to-all-start = ((bf16[64,32,256]{2,1,0:T(8,128)(2,1)}), bf16[64,32,256]{2,1,0:T(8,128)(2,1)S(1)}, u32[]{:S(2)}, u32[]{:S(2)}) async-start(bf16[64,32,256]{2,1,0:T(8,128)(2,1)} %get-tuple-element.24), calls=%async_computation | async-start | bytes 2097152 | tf_op jit(solution)/shard_map/all_to_all | solution.py:215
  28.3 5.2 %collective-permute-start.5 = (f32[1,256]{1,0:T(1,128)S(1)}, f32[1,256]{1,0:T(1,128)S(1)}, u32[]{:S(2)}, u32[]{:S(2)}) collective-permute-start(f32[1,256]{1,0:T(1,128)S(1)} %get-tuple-element.25), channel_id=1, source_target_pairs={{0,2},{1,3},{2,0},{3,1},{4,6},{5,7},{6,4},{7,5},{8,10},{9,11},{10,... | collective-permute-start | bytes 3080 | tf_op jit(solution)/shard_map/ppermute | solution.py:217
  28.6 4.8 %collective-permute-start.4 = (f32[1,256]{1,0:T(1,128)S(1)}, f32[1,256]{1,0:T(1,128)S(1)}, u32[]{:S(2)}, u32[]{:S(2)}) collective-permute-start(f32[1,256]{1,0:T(1,128)S(1)} %get-tuple-element.25), channel_id=1, source_target_pairs={{0,1},{1,2},{2,3},{3,0},{4,5},{5,6},{6,7},{7,4},{8,9},{9,10},{10,1... | collective-permute-start | bytes 3080 | tf_op jit(solution)/shard_map/ppermute | solution.py:217
  29.2 4.2 %collective-permute-start.3 = (f32[1,256]{1,0:T(1,128)S(1)}, f32[1,256]{1,0:T(1,128)S(1)}, u32[]{:S(2)}, u32[]{:S(2)}) collective-permute-start(f32[1,256]{1,0:T(1,128)S(1)} %get-tuple-element.25), channel_id=1, source_target_pairs={{0,3},{1,0},{2,1},{3,2},{4,7},{5,4},{6,5},{7,6},{8,11},{9,8},{10,9... | collective-permute-start | bytes 3080 | tf_op jit(solution)/shard_map/ppermute | solution.py:217
  33.4 1.3 %collective-permute-start.6 = (f32[4,256]{1,0:T(4,128)S(1)}, f32[4,256]{1,0:T(4,128)S(1)}, u32[]{:S(2)}, u32[]{:S(2)}) collective-permute-start(f32[4,256]{1,0:T(4,128)S(1)} %pad_maximum_fusion), channel_id=1, source_target_pairs={{0,4},{4,0},{8,12},{12,8},{16,20},{20,16},{24,28},{28,24},{32,36},... | collective-permute-start | bytes 12296 | tf_op jit(solution)/shard_map/ppermute | solution.py:221
  34.7 3.7 %collective-permute-start.7 = (f32[4,256]{1,0:T(4,128)S(1)}, f32[4,256]{1,0:T(4,128)S(1)}, u32[]{:S(2)}, u32[]{:S(2)}) collective-permute-start(f32[4,256]{1,0:T(4,128)S(1)} %fusion), channel_id=1, source_target_pairs={{0,8},{4,12},{8,0},{12,4},{16,24},{20,28},{24,16},{28,20},{32,40},... | collective-permute-start | bytes 12296 | tf_op jit(solution)/shard_map/ppermute | solution.py:221
  38.4 5.4 %collective-permute-start.8 = (f32[4,256]{1,0:T(4,128)S(1)}, f32[4,256]{1,0:T(4,128)S(1)}, u32[]{:S(2)}, u32[]{:S(2)}) collective-permute-start(f32[4,256]{1,0:T(4,128)S(1)} %fusion.3), channel_id=1, source_target_pairs={{0,16},{4,20},{8,24},{12,28},{16,0},{20,4},{24,8},{28,12},{32,48},... | collective-permute-start | bytes 12296 | tf_op jit(solution)/shard_map/ppermute | solution.py:221
  56.3 15.0 %collective-permute-start.12 = (bf16[32,32,256]{2,1,0:T(8,128)(2,1)S(1)}, bf16[32,32,256]{2,1,0:T(8,128)(2,1)S(1)}, u32[]{:S(2)}, u32[]{:S(2)}) collective-permute-start(bf16[32,32,256]{2,1,0:T(8,128)(2,1)S(1)} %get-tuple-element.37), channel_id=1, source_target_pairs={{0,3},{1,0},{2,1},{3,2},{4,7},{5,4},{6,5},{7,6},{8,11},{9,8},{10,9... | collective-permute-start | bytes 1572872 | tf_op jit(solution)/shard_map/ppermute | solution.py:229
  56.5 16.0 %collective-permute-start.11 = (bf16[32,32,256]{2,1,0:T(8,128)(2,1)S(1)}, bf16[32,32,256]{2,1,0:T(8,128)(2,1)S(1)}, u32[]{:S(2)}, u32[]{:S(2)}) collective-permute-start(bf16[32,32,256]{2,1,0:T(8,128)(2,1)S(1)} %get-tuple-element.38), channel_id=1, source_target_pairs={{0,1},{1,2},{2,3},{3,0},{4,5},{5,6},{6,7},{7,4},{8,9},{9,10},{10,1... | collective-permute-start | bytes 1572872 | tf_op jit(solution)/shard_map/ppermute | solution.py:228
  58.5 3.6 %collective-permute-start.9 = (f32[4,256]{1,0:T(4,128)S(1)}, f32[4,256]{1,0:T(4,128)S(1)}, u32[]{:S(2)}, u32[]{:S(2)}) collective-permute-start(f32[4,256]{1,0:T(4,128)S(1)} %add.20), channel_id=1, source_target_pairs={{0,32},{4,36},{8,40},{12,44},{16,48},{20,52},{24,56},{28,60},{32,0... | collective-permute-start | bytes 12296 | tf_op jit(solution)/shard_map/ppermute | solution.py:221
  63.2 20.7 %collective-permute-start.14 = (bf16[32,32,256]{2,1,0:T(8,128)(2,1)}, bf16[32,32,256]{2,1,0:T(8,128)(2,1)}, u32[]{:S(2)}, u32[]{:S(2)}) collective-permute-start(bf16[32,32,256]{2,1,0:T(8,128)(2,1)} %get-tuple-element.35), channel_id=1, source_target_pairs={{0,1},{1,2},{2,3},{3,0},{4,5},{5,6},{6,7},{7,4},{8,9},{9,10},{10,1... | collective-permute-start | bytes 1572872 | tf_op jit(solution)/shard_map/ppermute | solution.py:232
  63.2 20.7 %collective-permute-start.10 = (bf16[32,32,256]{2,1,0:T(8,128)(2,1)}, bf16[32,32,256]{2,1,0:T(8,128)(2,1)}, u32[]{:S(2)}, u32[]{:S(2)}) collective-permute-start(bf16[32,32,256]{2,1,0:T(8,128)(2,1)} %get-tuple-element.36), channel_id=1, source_target_pairs={{0,3},{1,0},{2,1},{3,2},{4,7},{5,4},{6,5},{7,6},{8,11},{9,8},{10,9... | collective-permute-start | bytes 1572872 | tf_op jit(solution)/shard_map/ppermute | solution.py:233
  66.4 4.5 %collective-permute-start.13 = (f32[4,256]{1,0:T(4,128)S(1)}, f32[4,256]{1,0:T(4,128)S(1)}, u32[]{:S(2)}, u32[]{:S(2)}) collective-permute-start(f32[4,256]{1,0:T(4,128)S(1)} %add.21), channel_id=1, source_target_pairs={{0,64},{4,68},{8,72},{12,76},{16,80},{20,84},{24,88},{28,92},{32,9... | collective-permute-start | bytes 12296 | tf_op jit(solution)/shard_map/ppermute | solution.py:221
  72.6 20.5 %collective-permute-start.17 = (bf16[32,32,256]{2,1,0:T(8,128)(2,1)S(1)}, bf16[32,32,256]{2,1,0:T(8,128)(2,1)S(1)}, u32[]{:S(2)}, u32[]{:S(2)}) collective-permute-start(bf16[32,32,256]{2,1,0:T(8,128)(2,1)S(1)} %collective-permute-done.12.right_b), channel_id=1, source_target_pairs={{0,3},{1,0},{2,1},{3,2},{4,7},{5,4},{6,5},{7,6},{8,11},{9,8},{10,9... | collective-permute-start | bytes 1572872 | tf_op jit(solution)/shard_map/ppermute | solution.py:237
  72.6 21.8 %collective-permute-start.16 = (bf16[32,32,256]{2,1,0:T(8,128)(2,1)S(1)}, bf16[32,32,256]{2,1,0:T(8,128)(2,1)S(1)}, u32[]{:S(2)}, u32[]{:S(2)}) collective-permute-start(bf16[32,32,256]{2,1,0:T(8,128)(2,1)S(1)} %collective-permute-done.11.left_a), channel_id=1, source_target_pairs={{0,1},{1,2},{2,3},{3,0},{4,5},{5,6},{6,7},{7,4},{8,9},{9,10},{10,1... | collective-permute-start | bytes 1572872 | tf_op jit(solution)/shard_map/ppermute | solution.py:236
  74.6 7.5 %collective-permute-start.15 = (f32[4,256]{1,0:T(4,128)S(1)}, f32[4,256]{1,0:T(4,128)S(1)}, u32[]{:S(2)}, u32[]{:S(2)}) collective-permute-start(f32[4,256]{1,0:T(4,128)S(1)} %add.22), channel_id=1, source_target_pairs={{0,128},{4,132},{8,136},{12,140},{16,144},{20,148},{24,152},{28,15... | collective-permute-start | bytes 12296 | tf_op jit(solution)/shard_map/ppermute | solution.py:221

commit v6 on v5

--- a/solution.py
+++ b/solution.py
@@ -32,7 +32,7 @@
     return jnp.dot(a, b, preferred_element_type=F32)
 
 
-def spectra_kernel(records, tables, results, power, held, arrived):
+def spectra_kernel(records, stored, results, power, held, tables, arrived):
     windows, _, samples = records.shape
     half = samples // 2
     kept = tables.shape[2] // 2
@@ -41,11 +41,15 @@
     def fetch(w):
         return pltpu.make_async_copy(records.at[w], held.at[w], arrived.at[w])
 
-    for w in range(windows):
+    table_copy = pltpu.make_async_copy(stored.at[pl.ds(0, 2)], tables, arrived.at[windows])
+    fetch(0).start()
+    table_copy.start()
+    for w in range(1, windows):
         fetch(w).start()
     steps = lax.broadcasted_iota(jnp.int32, (1, samples), 1).astype(F32)
     taper = 0.5 - 0.5 * jnp.cos(steps * (2.0 * math.pi / samples))
 
+    table_copy.wait()
     chan = records.shape[1]
     for pair in range(0, windows, 2):
         fetch(pair).wait()
@@ -174,7 +178,7 @@
         spectra_kernel,
         in_specs=[
             pl.BlockSpec(memory_space=pltpu.HBM),
-            pl.BlockSpec(memory_space=pltpu.VMEM),
+            pl.BlockSpec(memory_space=pltpu.HBM),
         ],
         out_shape=[
             jax.ShapeDtypeStruct(result_shape, F32),
@@ -182,11 +186,12 @@
         ],
         scratch_shapes=[
             pltpu.VMEM((windows, chan, samples), F32),
-            pltpu.SemaphoreType.DMA((windows,)),
-        ],
-        compiler_params=pltpu.CompilerParams(vmem_limit_bytes=50 << 20),
+            pltpu.VMEM((2, samples // 2, 2 * kept), BF),
+            pltpu.SemaphoreType.DMA((windows + 1,)),
+        ],
+        compiler_params=pltpu.CompilerParams(vmem_limit_bytes=51 << 20),
         name="spectra",
-    )(records, split_tables(samples, kept))
+    )(records, np.pad(split_tables(samples, kept), ((0, 14), (0, 0), (0, 0))))
     ahead, back, across = ring(columns, 1), ring(columns, columns - 1), ring(columns, 2)
     powers = [power] + [lax.ppermute(power, "col", p) for p in (ahead, back, across)]
     even, odd = pl.pallas_call(

time: 96.4 us -> 95.5 us (level)
  local copies, waits for them, and re-layouts: 2.45 us -> 1.39 us
    unnamed x4 -> x2, local copies, waits for them, and re-layouts: 1.04 us -> 0.01 us
where the time goes in v6:
time: 95.5 us; the launch traced here: 95.3 us
  starting transfers between devices  40 us (42%)
  waiting for transfers between devices  38.2 us (40%)
  Pallas kernels  15.6 us (16%)
  local copies, waits for them, and re-layouts  1.39 us (1%)
    ppermute x6, waiting for transfers between devices, fold(): lax.ppermute(value, 'wa', [(i, i ^ step) for i in range(owners)])  14.1 us
    all_to_all x1, waiting for transfers between devices, body(): lax.all_to_all(message, 'wa', split_axis=0, concat_axis=0, tiled=True)  12.4 us
    ppermute x6, starting transfers between devices, fold(): lax.ppermute(value, 'wa', [(i, i ^ step) for i in range(owners)])  11.9 us
    all_to_all x1, starting transfers between devices, body(): lax.all_to_all(message, 'wa', split_axis=0, concat_axis=0, tiled=True)  11.8 us
    pallas_call x1, Pallas kernels, body(): pl.pallas_call(functools.partial(gram_near_kernel, scale), grid_spec=pltp...  6.14 us
    pallas_call x1, Pallas kernels, body(): pl.pallas_call(spectra_kernel, in_specs=[pl.BlockSpec(memory_space=pltpu....  5.31 us
    ppermute x3, starting transfers between devices, body(): lax.ppermute(power, 'col', p)  5.13 us
    ppermute x3, starting transfers between devices, body(): lax.ppermute(energy, 'col', p)  3.62 us
  transfers between devices with their start and end apart: 19, of which 15 were waited for; matrix products, arithmetic and copies ran while one was open for 1% of the time, Pallas kernels for 8%

profile of v6, /device:TPU:32, one launch (start us, length us, event | category | flops | bytes accessed | tf_op | source)
XLA Modules:
  0.0 95.3 jit_solution(5729763139520136782)
XLA Ops:
  0.0 5.3 %spectra.1 = (f32[8,2,256,128]{3,2,1,0:T(8,128)S(1)}, f32[8,128]{1,0:T(8,128)S(1)}) custom-call(f32[8,256,1024]{2,1,0:T(8,128)} %records.1, bf16[16,512,256]{2,1,0:T(8,128)(2,1)} %constant.6.clone.stored), custom_call_target="tpu_custom_call" | custom-call | tf_op jit(solution)/shard_map/spectra/pallas_call | solution.py:177
  5.3 3.1 %collective-permute-start.2 = (f32[8,128]{1,0:T(8,128)S(1)}, f32[8,128]{1,0:T(8,128)S(1)}, u32[]{:S(2)}, u32[]{:S(2)}) collective-permute-start(f32[8,128]{1,0:T(8,128)S(1)} %get-tuple-element.23.p0), channel_id=1, source_target_pairs={{0,2},{1,3},{2,0},{3,1},{4,6},{5,7},{6,4},{7,5},{8,10},{9,11},{10,... | collective-permute-start | bytes 12296 | tf_op jit(solution)/shard_map/ppermute | solution.py:196
  8.4 1.1 %collective-permute-start.1 = (f32[8,128]{1,0:T(8,128)S(1)}, f32[8,128]{1,0:T(8,128)S(1)}, u32[]{:S(2)}, u32[]{:S(2)}) collective-permute-start(f32[8,128]{1,0:T(8,128)S(1)} %get-tuple-element.23.p0), channel_id=1, source_target_pairs={{0,3},{1,0},{2,1},{3,2},{4,7},{5,4},{6,5},{7,6},{8,11},{9,8},{10,9... | collective-permute-start | bytes 12296 | tf_op jit(solution)/shard_map/ppermute | solution.py:196
  9.6 0.9 collective-permute-start
  10.7 1.2 %turn.1 = (f32[2,1024,128]{2,1,0:T(8,128)S(1)}, f32[2,1024,128]{2,1,0:T(8,128)S(1)}) custom-call(f32[8,2,256,128]{3,2,1,0:T(8,128)S(1)} %get-tuple-element.20.results), custom_call_target="tpu_custom_call" | custom-call | bytes 6291456 | tf_op jit(solution)/shard_map/turn/pallas_call | solution.py:197
  12.0 2.4 %collective-permute-done.p1 = f32[8,128]{1,0:T(8,128)S(1)} collective-permute-done((f32[8,128]{1,0:T(8,128)S(1)}, f32[8,128]{1,0:T(8,128)S(1)}, u32[]{:S(2)}, u32[]{:S(2)}) %collective-permute-start) | collective-permute-done | bytes 4128 | tf_op jit(solution)/shard_map/ppermute | solution.py:196
  14.4 1.2 %whiten.1 = (bf16[64,32,256]{2,1,0:T(8,128)(2,1)}, f32[1,256]{1,0:T(1,128)S(1)}) custom-call(f32[2,1024,128]{2,1,0:T(8,128)S(1)} %get-tuple-element.21.even, f32[2,1024,128]{2,1,0:T(8,128)S(1)} %get-tuple-element.22.odd, f32[8,128]{1,0:T(8,128)S(1)} %get-tuple-element.23.p0, f32[8,128]{1,0:T(8,128)S(1)} %collective-permute-done.p1, ...), custom_call_target="tpu_custom_call" | custom-call | tf_op jit(solution)/shard_map/whiten/pallas_call | solution.py:205
  15.6 11.8 %all-to-all-start = ((bf16[64,32,256]{2,1,0:T(8,128)(2,1)}), bf16[64,32,256]{2,1,0:T(8,128)(2,1)S(1)}, u32[]{:S(2)}, u32[]{:S(2)}) async-start(bf16[64,32,256]{2,1,0:T(8,128)(2,1)} %get-tuple-element.24), calls=%async_computation | async-start | bytes 2097152 | tf_op jit(solution)/shard_map/all_to_all | solution.py:220
  28.3 2.7 %collective-permute-start.3 = (f32[1,256]{1,0:T(1,128)S(1)}, f32[1,256]{1,0:T(1,128)S(1)}, u32[]{:S(2)}, u32[]{:S(2)}) collective-permute-start(f32[1,256]{1,0:T(1,128)S(1)} %get-tuple-element.25), channel_id=1, source_target_pairs={{0,3},{1,0},{2,1},{3,2},{4,7},{5,4},{6,5},{7,6},{8,11},{9,8},{10,9... | collective-permute-start | bytes 3080 | tf_op jit(solution)/shard_map/ppermute | solution.py:222
  31.0 1.5 %collective-permute-done.5 = f32[1,256]{1,0:T(1,128)S(1)} collective-permute-done((f32[1,256]{1,0:T(1,128)S(1)}, f32[1,256]{1,0:T(1,128)S(1)}, u32[]{:S(2)}, u32[]{:S(2)}) %collective-permute-start.5) | collective-permute-done | bytes 1056 | tf_op jit(solution)/shard_map/ppermute | solution.py:222
  32.7 1.2 %collective-permute-done.6 = f32[4,256]{1,0:T(4,128)S(1)} collective-permute-done((f32[4,256]{1,0:T(4,128)S(1)}, f32[4,256]{1,0:T(4,128)S(1)}, u32[]{:S(2)}, u32[]{:S(2)}) %collective-permute-start.6) | collective-permute-done | bytes 4128 | tf_op jit(solution)/shard_map/ppermute | solution.py:226
  33.8 1.6 %collective-permute-start.7 = (f32[4,256]{1,0:T(4,128)S(1)}, f32[4,256]{1,0:T(4,128)S(1)}, u32[]{:S(2)}, u32[]{:S(2)}) collective-permute-start(f32[4,256]{1,0:T(4,128)S(1)} %fusion), channel_id=1, source_target_pairs={{0,8},{4,12},{8,0},{12,4},{16,24},{20,28},{24,16},{28,20},{32,40},... | collective-permute-start | bytes 12296 | tf_op jit(solution)/shard_map/ppermute | solution.py:226
  35.4 2.2 %collective-permute-done.7 = f32[4,256]{1,0:T(4,128)S(1)} collective-permute-done((f32[4,256]{1,0:T(4,128)S(1)}, f32[4,256]{1,0:T(4,128)S(1)}, u32[]{:S(2)}, u32[]{:S(2)}) %collective-permute-start.7) | collective-permute-done | bytes 4128 | tf_op jit(solution)/shard_map/ppermute | solution.py:226
  37.6 3.1 %collective-permute-start.8 = (f32[4,256]{1,0:T(4,128)S(1)}, f32[4,256]{1,0:T(4,128)S(1)}, u32[]{:S(2)}, u32[]{:S(2)}) collective-permute-start(f32[4,256]{1,0:T(4,128)S(1)} %fusion.3), channel_id=1, source_target_pairs={{0,16},{4,20},{8,24},{12,28},{16,0},{20,4},{24,8},{28,12},{32,48},... | collective-permute-start | bytes 12296 | tf_op jit(solution)/shard_map/ppermute | solution.py:226
  40.6 2.3 %collective-permute-done.8 = f32[4,256]{1,0:T(4,128)S(1)} collective-permute-done((f32[4,256]{1,0:T(4,128)S(1)}, f32[4,256]{1,0:T(4,128)S(1)}, u32[]{:S(2)}, u32[]{:S(2)}) %collective-permute-start.8) | collective-permute-done | bytes 4128 | tf_op jit(solution)/shard_map/ppermute | solution.py:226
  43.0 12.4 %all-to-all-done.own = bf16[64,32,256]{2,1,0:T(8,128)(2,1)S(1)} async-done(((bf16[64,32,256]{2,1,0:T(8,128)(2,1)}), bf16[64,32,256]{2,1,0:T(8,128)(2,1)S(1)}, u32[]{:S(2)}, u32[]{:S(2)}) %all-to-all-start) | async-done | bytes 1048608 | tf_op jit(solution)/shard_map/all_to_all | solution.py:220
  55.7 2.0 %collective-permute-start.11 = (bf16[32,32,256]{2,1,0:T(8,128)(2,1)S(1)}, bf16[32,32,256]{2,1,0:T(8,128)(2,1)S(1)}, u32[]{:S(2)}, u32[]{:S(2)}) collective-permute-start(bf16[32,32,256]{2,1,0:T(8,128)(2,1)S(1)} %get-tuple-element.38), channel_id=1, source_target_pairs={{0,1},{1,2},{2,3},{3,0},{4,5},{5,6},{6,7},{7,4},{8,9},{9,10},{10,1... | collective-permute-start | bytes 1572872 | tf_op jit(solution)/shard_map/ppermute | solution.py:233
  57.7 1.4 %collective-permute-start.9 = (f32[4,256]{1,0:T(4,128)S(1)}, f32[4,256]{1,0:T(4,128)S(1)}, u32[]{:S(2)}, u32[]{:S(2)}) collective-permute-start(f32[4,256]{1,0:T(4,128)S(1)} %add.20), channel_id=1, source_target_pairs={{0,32},{4,36},{8,40},{12,44},{16,48},{20,52},{24,56},{28,60},{32,0... | collective-permute-start | bytes 12296 | tf_op jit(solution)/shard_map/ppermute | solution.py:226
  59.1 2.2 %collective-permute-done.9 = f32[4,256]{1,0:T(4,128)S(1)} collective-permute-done((f32[4,256]{1,0:T(4,128)S(1)}, f32[4,256]{1,0:T(4,128)S(1)}, u32[]{:S(2)}, u32[]{:S(2)}) %collective-permute-start.9) | collective-permute-done | bytes 4128 | tf_op jit(solution)/shard_map/ppermute | solution.py:226
  61.3 1.0 %fusion.1 = (bf16[32,32,256]{2,1,0:T(8,128)(2,1)}, bf16[32,32,256]{2,1,0:T(8,128)(2,1)}) fusion(bf16[64,32,256]{2,1,0:T(8,128)(2,1)S(1)} %all-to-all-done.own), kind=kLoop, calls=%fused_computation.2 | loop fusion | bytes 2097152 | tf_op jit(solution)/shard_map/slice | solution.py:237
  62.3 3.2 %collective-permute-start.10 = (bf16[32,32,256]{2,1,0:T(8,128)(2,1)}, bf16[32,32,256]{2,1,0:T(8,128)(2,1)}, u32[]{:S(2)}, u32[]{:S(2)}) collective-permute-start(bf16[32,32,256]{2,1,0:T(8,128)(2,1)} %get-tuple-element.36), channel_id=1, source_target_pairs={{0,3},{1,0},{2,1},{3,2},{4,7},{5,4},{6,5},{7,6},{8,11},{9,8},{10,9... | collective-permute-start | bytes 1572872 | tf_op jit(solution)/shard_map/ppermute | solution.py:238
  65.6 2.6 %collective-permute-start.13 = (f32[4,256]{1,0:T(4,128)S(1)}, f32[4,256]{1,0:T(4,128)S(1)}, u32[]{:S(2)}, u32[]{:S(2)}) collective-permute-start(f32[4,256]{1,0:T(4,128)S(1)} %add.21), channel_id=1, source_target_pairs={{0,64},{4,68},{8,72},{12,76},{16,80},{20,84},{24,88},{28,92},{32,9... | collective-permute-start | bytes 12296 | tf_op jit(solution)/shard_map/ppermute | solution.py:226
  68.2 1.9 %collective-permute-done.13 = f32[4,256]{1,0:T(4,128)S(1)} collective-permute-done((f32[4,256]{1,0:T(4,128)S(1)}, f32[4,256]{1,0:T(4,128)S(1)}, u32[]{:S(2)}, u32[]{:S(2)}) %collective-permute-start.13) | collective-permute-done | bytes 4128 | tf_op jit(solution)/shard_map/ppermute | solution.py:226
  70.4 1.3 %collective-permute-done.11.left_a = bf16[32,32,256]{2,1,0:T(8,128)(2,1)S(1)} collective-permute-done((bf16[32,32,256]{2,1,0:T(8,128)(2,1)S(1)}, bf16[32,32,256]{2,1,0:T(8,128)(2,1)S(1)}, u32[]{:S(2)}, u32[]{:S(2)}) %collective-permute-start.11) | collective-permute-done | bytes 524320 | tf_op jit(solution)/shard_map/ppermute | solution.py:233
  71.7 2.0 %collective-permute-start.16 = (bf16[32,32,256]{2,1,0:T(8,128)(2,1)S(1)}, bf16[32,32,256]{2,1,0:T(8,128)(2,1)S(1)}, u32[]{:S(2)}, u32[]{:S(2)}) collective-permute-start(bf16[32,32,256]{2,1,0:T(8,128)(2,1)S(1)} %collective-permute-done.11.left_a), channel_id=1, source_target_pairs={{0,1},{1,2},{2,3},{3,0},{4,5},{5,6},{6,7},{7,4},{8,9},{9,10},{10,1... | collective-permute-start | bytes 1572872 | tf_op jit(solution)/shard_map/ppermute | solution.py:241
  73.7 3.2 %collective-permute-start.15 = (f32[4,256]{1,0:T(4,128)S(1)}, f32[4,256]{1,0:T(4,128)S(1)}, u32[]{:S(2)}, u32[]{:S(2)}) collective-permute-start(f32[4,256]{1,0:T(4,128)S(1)} %add.22), channel_id=1, source_target_pairs={{0,128},{4,132},{8,136},{12,140},{16,144},{20,148},{24,152},{28,15... | collective-permute-start | bytes 12296 | tf_op jit(solution)/shard_map/ppermute | solution.py:226
  76.9 4.4 %collective-permute-done.15 = f32[4,256]{1,0:T(4,128)S(1)} collective-permute-done((f32[4,256]{1,0:T(4,128)S(1)}, f32[4,256]{1,0:T(4,128)S(1)}, u32[]{:S(2)}, u32[]{:S(2)}) %collective-permute-start.15) | collective-permute-done | bytes 4128 | tf_op jit(solution)/shard_map/ppermute | solution.py:226
  81.3 1.8 %collective-permute-done.14.left_b = bf16[32,32,256]{2,1,0:T(8,128)(2,1)} collective-permute-done((bf16[32,32,256]{2,1,0:T(8,128)(2,1)}, bf16[32,32,256]{2,1,0:T(8,128)(2,1)}, u32[]{:S(2)}, u32[]{:S(2)}) %collective-permute-start.14) | collective-permute-done | bytes 524320 | tf_op jit(solution)/shard_map/ppermute | solution.py:237
  83.0 6.1 %gram_near.1 = (f32[2,2,256,1024]{3,2,1,0:T(8,128)}, bf16[2,512,1024]{2,1,0:T(8,128)(2,1)S(1)}) custom-call(s32[1]{0:T(128)} %bitcast.col, bf16[64,32,256]{2,1,0:T(8,128)(2,1)S(1)} %all-to-all-done.own, bf16[32,32,256]{2,1,0:T(8,128)(2,1)} %collective-permute-done.10.right_a, bf16[32,32,256]{2,1,0:T(8,128)(2,1)S(1)} %collective-permute-done.12.right_b, ...), custom_call_target="tpu_custom_call" | custom-call | flops 1610612736 | bytes 8388608 | tf_op jit(solution)/shard_map/gram_near/pallas_call | solution.py:263
  89.2 3.0 %collective-permute-done.17.far_b = bf16[32,32,256]{2,1,0:T(8,128)(2,1)S(1)} collective-permute-done((bf16[32,32,256]{2,1,0:T(8,128)(2,1)S(1)}, bf16[32,32,256]{2,1,0:T(8,128)(2,1)S(1)}, u32[]{:S(2)}, u32[]{:S(2)}) %collective-permute-start.17) | collective-permute-done | bytes 524320 | tf_op jit(solution)/shard_map/ppermute | solution.py:242
  92.2 1.3 %collective-permute-done.16.far_a = bf16[32,32,256]{2,1,0:T(8,128)(2,1)S(1)} collective-permute-done((bf16[32,32,256]{2,1,0:T(8,128)(2,1)S(1)}, bf16[32,32,256]{2,1,0:T(8,128)(2,1)S(1)}, u32[]{:S(2)}, u32[]{:S(2)}) %collective-permute-start.16) | collective-permute-done | bytes 524320 | tf_op jit(solution)/shard_map/ppermute | solution.py:241
  93.5 1.8 %gram_far.1 = f32[2,2,256,1024]{3,2,1,0:T(8,128)} custom-call(s32[1]{0:T(128)} %bitcast.col, bf16[2,512,1024]{2,1,0:T(8,128)(2,1)S(1)} %get-tuple-element.33.lhs, bf16[32,32,256]{2,1,0:T(8,128)(2,1)S(1)} %collective-permute-done.16.far_a, bf16[32,32,256]{2,1,0:T(8,128)(2,1)S(1)} %collective-permute-done.17.far_b, ...), custom_call_target="tpu_custom_call", output_to_operand_aliasing={{}: (5, {})} | custom-call | flops 536870912 | bytes 4194304 | tf_op jit(solution)/shard_map/gram_far/pallas_call | solution.py:278
  (25 shorter events, 2.2 us)
Async XLA Ops:
  0.0 10.5 %copy-start = (f32[128]{0:T(128)S(1)}, f32[128]{0:T(128)}, u32[]{:S(2)}) copy-start(f32[128]{0:T(128)} %param.4) | copy-start | bytes 1540
  5.3 6.6 %collective-permute-start.2 = (f32[8,128]{1,0:T(8,128)S(1)}, f32[8,128]{1,0:T(8,128)S(1)}, u32[]{:S(2)}, u32[]{:S(2)}) collective-permute-start(f32[8,128]{1,0:T(8,128)S(1)} %get-tuple-element.23.p0), channel_id=1, source_target_pairs={{0,2},{1,3},{2,0},{3,1},{4,6},{5,7},{6,4},{7,5},{8,10},{9,11},{10,... | collective-permute-start | bytes 12296 | tf_op jit(solution)/shard_map/ppermute | solution.py:196
  8.4 3.6 %collective-permute-start.1 = (f32[8,128]{1,0:T(8,128)S(1)}, f32[8,128]{1,0:T(8,128)S(1)}, u32[]{:S(2)}, u32[]{:S(2)}) collective-permute-start(f32[8,128]{1,0:T(8,128)S(1)} %get-tuple-element.23.p0), channel_id=1, source_target_pairs={{0,3},{1,0},{2,1},{3,2},{4,7},{5,4},{6,5},{7,6},{8,11},{9,8},{10,9... | collective-permute-start | bytes 12296 | tf_op jit(solution)/shard_map/ppermute | solution.py:196
  9.6 4.8 %collective-permute-start = (f32[8,128]{1,0:T(8,128)S(1)}, f32[8,128]{1,0:T(8,128)S(1)}, u32[]{:S(2)}, u32[]{:S(2)}) collective-permute-start(f32[8,128]{1,0:T(8,128)S(1)} %get-tuple-element.23.p0), channel_id=1, source_target_pairs={{0,1},{1,2},{2,3},{3,0},{4,5},{5,6},{6,7},{7,4},{8,9},{9,10},{10,1... | collective-permute-start | bytes 12296 | tf_op jit(solution)/shard_map/ppermute | solution.py:196
  15.6 39.7 %all-to-all-start = ((bf16[64,32,256]{2,1,0:T(8,128)(2,1)}), bf16[64,32,256]{2,1,0:T(8,128)(2,1)S(1)}, u32[]{:S(2)}, u32[]{:S(2)}) async-start(bf16[64,32,256]{2,1,0:T(8,128)(2,1)} %get-tuple-element.24), calls=%async_computation | async-start | bytes 2097152 | tf_op jit(solution)/shard_map/all_to_all | solution.py:220
  27.4 5.2 %collective-permute-start.5 = (f32[1,256]{1,0:T(1,128)S(1)}, f32[1,256]{1,0:T(1,128)S(1)}, u32[]{:S(2)}, u32[]{:S(2)}) collective-permute-start(f32[1,256]{1,0:T(1,128)S(1)} %get-tuple-element.25), channel_id=1, source_target_pairs={{0,2},{1,3},{2,0},{3,1},{4,6},{5,7},{6,4},{7,5},{8,10},{9,11},{10,... | collective-permute-start | bytes 3080 | tf_op jit(solution)/shard_map/ppermute | solution.py:222
  27.8 4.8 %collective-permute-start.4 = (f32[1,256]{1,0:T(1,128)S(1)}, f32[1,256]{1,0:T(1,128)S(1)}, u32[]{:S(2)}, u32[]{:S(2)}) collective-permute-start(f32[1,256]{1,0:T(1,128)S(1)} %get-tuple-element.25), channel_id=1, source_target_pairs={{0,1},{1,2},{2,3},{3,0},{4,5},{5,6},{6,7},{7,4},{8,9},{9,10},{10,1... | collective-permute-start | bytes 3080 | tf_op jit(solution)/shard_map/ppermute | solution.py:222
  28.3 4.2 %collective-permute-start.3 = (f32[1,256]{1,0:T(1,128)S(1)}, f32[1,256]{1,0:T(1,128)S(1)}, u32[]{:S(2)}, u32[]{:S(2)}) collective-permute-start(f32[1,256]{1,0:T(1,128)S(1)} %get-tuple-element.25), channel_id=1, source_target_pairs={{0,3},{1,0},{2,1},{3,2},{4,7},{5,4},{6,5},{7,6},{8,11},{9,8},{10,9... | collective-permute-start | bytes 3080 | tf_op jit(solution)/shard_map/ppermute | solution.py:222
  32.6 1.3 %collective-permute-start.6 = (f32[4,256]{1,0:T(4,128)S(1)}, f32[4,256]{1,0:T(4,128)S(1)}, u32[]{:S(2)}, u32[]{:S(2)}) collective-permute-start(f32[4,256]{1,0:T(4,128)S(1)} %pad_maximum_fusion), channel_id=1, source_target_pairs={{0,4},{4,0},{8,12},{12,8},{16,20},{20,16},{24,28},{28,24},{32,36},... | collective-permute-start | bytes 12296 | tf_op jit(solution)/shard_map/ppermute | solution.py:226
  33.8 3.7 %collective-permute-start.7 = (f32[4,256]{1,0:T(4,128)S(1)}, f32[4,256]{1,0:T(4,128)S(1)}, u32[]{:S(2)}, u32[]{:S(2)}) collective-permute-start(f32[4,256]{1,0:T(4,128)S(1)} %fusion), channel_id=1, source_target_pairs={{0,8},{4,12},{8,0},{12,4},{16,24},{20,28},{24,16},{28,20},{32,40},... | collective-permute-start | bytes 12296 | tf_op jit(solution)/shard_map/ppermute | solution.py:226
  37.6 5.4 %collective-permute-start.8 = (f32[4,256]{1,0:T(4,128)S(1)}, f32[4,256]{1,0:T(4,128)S(1)}, u32[]{:S(2)}, u32[]{:S(2)}) collective-permute-start(f32[4,256]{1,0:T(4,128)S(1)} %fusion.3), channel_id=1, source_target_pairs={{0,16},{4,20},{8,24},{12,28},{16,0},{20,4},{24,8},{28,12},{32,48},... | collective-permute-start | bytes 12296 | tf_op jit(solution)/shard_map/ppermute | solution.py:226
  55.4 15.0 %collective-permute-start.12 = (bf16[32,32,256]{2,1,0:T(8,128)(2,1)S(1)}, bf16[32,32,256]{2,1,0:T(8,128)(2,1)S(1)}, u32[]{:S(2)}, u32[]{:S(2)}) collective-permute-start(bf16[32,32,256]{2,1,0:T(8,128)(2,1)S(1)} %get-tuple-element.37), channel_id=1, source_target_pairs={{0,3},{1,0},{2,1},{3,2},{4,7},{5,4},{6,5},{7,6},{8,11},{9,8},{10,9... | collective-permute-start | bytes 1572872 | tf_op jit(solution)/shard_map/ppermute | solution.py:234
  55.7 16.0 %collective-permute-start.11 = (bf16[32,32,256]{2,1,0:T(8,128)(2,1)S(1)}, bf16[32,32,256]{2,1,0:T(8,128)(2,1)S(1)}, u32[]{:S(2)}, u32[]{:S(2)}) collective-permute-start(bf16[32,32,256]{2,1,0:T(8,128)(2,1)S(1)} %get-tuple-element.38), channel_id=1, source_target_pairs={{0,1},{1,2},{2,3},{3,0},{4,5},{5,6},{6,7},{7,4},{8,9},{9,10},{10,1... | collective-permute-start | bytes 1572872 | tf_op jit(solution)/shard_map/ppermute | solution.py:233
  57.7 3.6 %collective-permute-start.9 = (f32[4,256]{1,0:T(4,128)S(1)}, f32[4,256]{1,0:T(4,128)S(1)}, u32[]{:S(2)}, u32[]{:S(2)}) collective-permute-start(f32[4,256]{1,0:T(4,128)S(1)} %add.20), channel_id=1, source_target_pairs={{0,32},{4,36},{8,40},{12,44},{16,48},{20,52},{24,56},{28,60},{32,0... | collective-permute-start | bytes 12296 | tf_op jit(solution)/shard_map/ppermute | solution.py:226
  62.3 20.7 %collective-permute-start.14 = (bf16[32,32,256]{2,1,0:T(8,128)(2,1)}, bf16[32,32,256]{2,1,0:T(8,128)(2,1)}, u32[]{:S(2)}, u32[]{:S(2)}) collective-permute-start(bf16[32,32,256]{2,1,0:T(8,128)(2,1)} %get-tuple-element.35), channel_id=1, source_target_pairs={{0,1},{1,2},{2,3},{3,0},{4,5},{5,6},{6,7},{7,4},{8,9},{9,10},{10,1... | collective-permute-start | bytes 1572872 | tf_op jit(solution)/shard_map/ppermute | solution.py:237
  62.3 20.7 %collective-permute-start.10 = (bf16[32,32,256]{2,1,0:T(8,128)(2,1)}, bf16[32,32,256]{2,1,0:T(8,128)(2,1)}, u32[]{:S(2)}, u32[]{:S(2)}) collective-permute-start(bf16[32,32,256]{2,1,0:T(8,128)(2,1)} %get-tuple-element.36), channel_id=1, source_target_pairs={{0,3},{1,0},{2,1},{3,2},{4,7},{5,4},{6,5},{7,6},{8,11},{9,8},{10,9... | collective-permute-start | bytes 1572872 | tf_op jit(solution)/shard_map/ppermute | solution.py:238
  65.6 4.5 %collective-permute-start.13 = (f32[4,256]{1,0:T(4,128)S(1)}, f32[4,256]{1,0:T(4,128)S(1)}, u32[]{:S(2)}, u32[]{:S(2)}) collective-permute-start(f32[4,256]{1,0:T(4,128)S(1)} %add.21), channel_id=1, source_target_pairs={{0,64},{4,68},{8,72},{12,76},{16,80},{20,84},{24,88},{28,92},{32,9... | collective-permute-start | bytes 12296 | tf_op jit(solution)/shard_map/ppermute | solution.py:226
  71.7 20.5 %collective-permute-start.17 = (bf16[32,32,256]{2,1,0:T(8,128)(2,1)S(1)}, bf16[32,32,256]{2,1,0:T(8,128)(2,1)S(1)}, u32[]{:S(2)}, u32[]{:S(2)}) collective-permute-start(bf16[32,32,256]{2,1,0:T(8,128)(2,1)S(1)} %collective-permute-done.12.right_b), channel_id=1, source_target_pairs={{0,3},{1,0},{2,1},{3,2},{4,7},{5,4},{6,5},{7,6},{8,11},{9,8},{10,9... | collective-permute-start | bytes 1572872 | tf_op jit(solution)/shard_map/ppermute | solution.py:242
  71.7 21.8 %collective-permute-start.16 = (bf16[32,32,256]{2,1,0:T(8,128)(2,1)S(1)}, bf16[32,32,256]{2,1,0:T(8,128)(2,1)S(1)}, u32[]{:S(2)}, u32[]{:S(2)}) collective-permute-start(bf16[32,32,256]{2,1,0:T(8,128)(2,1)S(1)} %collective-permute-done.11.left_a), channel_id=1, source_target_pairs={{0,1},{1,2},{2,3},{3,0},{4,5},{5,6},{6,7},{7,4},{8,9},{9,10},{10,1... | collective-permute-start | bytes 1572872 | tf_op jit(solution)/shard_map/ppermute | solution.py:241
  73.7 7.5 %collective-permute-start.15 = (f32[4,256]{1,0:T(4,128)S(1)}, f32[4,256]{1,0:T(4,128)S(1)}, u32[]{:S(2)}, u32[]{:S(2)}) collective-permute-start(f32[4,256]{1,0:T(4,128)S(1)} %add.22), channel_id=1, source_target_pairs={{0,128},{4,132},{8,136},{12,140},{16,144},{20,148},{24,152},{28,15... | collective-permute-start | bytes 12296 | tf_op jit(solution)/shard_map/ppermute | solution.py:226

commit v7 on v6

--- a/solution.py
+++ b/solution.py
@@ -51,12 +51,13 @@
 
     table_copy.wait()
     chan = records.shape[1]
-    for pair in range(0, windows, 2):
-        fetch(pair).wait()
-        fetch(pair + 1).wait()
-        tapered = held[pair : pair + 2].reshape(2 * chan, samples) * taper
+    pairs = [(w, 2) for w in range(0, windows - 2, 2)]
+    for pair, count in pairs + [(windows - 2, 1), (windows - 1, 1)]:
+        for i in range(count):
+            fetch(pair + i).wait()
+        tapered = held[pair : pair + count].reshape(count * chan, samples) * taper
         first, second = tapered[:, :half], tapered[:, half:]
-        rows = [[], []]
+        rows = [[] for _ in range(count)]
         for parity in range(2):
             folded = first + second if parity == 0 else first - second
             high = folded.astype(BF)
@@ -64,12 +65,12 @@
             both = dot(high, tables[parity])
             result = both[:, :kept] + both[:, kept:] + dot(low, tables[parity, :, :kept])
             square = result * result
-            for i in range(2):
+            for i in range(count):
                 part = slice(i * chan, i * chan + chan)
                 results[pair + i, parity] = result[part]
                 total = jnp.sum(square[part], axis=0, keepdims=True)
                 rows[i].append(total[:, :bins] + total[:, bins:])
-        for i in range(2):
+        for i in range(count):
             power[pair + i : pair + i + 1, :] = jnp.concatenate(rows[i], axis=1)
 
 

time: 95.5 us -> 95.8 us (level)
  no operation moved by 1% of the time
where the time goes in v7:
time: 95.8 us; the launch traced here: 95.6 us
  starting transfers between devices  40 us (42%)
  waiting for transfers between devices  38.2 us (40%)
  Pallas kernels  15.9 us (17%)
  local copies, waits for them, and re-layouts  1.39 us (1%)
    ppermute x6, waiting for transfers between devices, fold(): lax.ppermute(value, 'wa', [(i, i ^ step) for i in range(owners)])  14.1 us
    all_to_all x1, waiting for transfers between devices, body(): lax.all_to_all(message, 'wa', split_axis=0, concat_axis=0, tiled=True)  12.4 us
    ppermute x6, starting transfers between devices, fold(): lax.ppermute(value, 'wa', [(i, i ^ step) for i in range(owners)])  11.9 us
    all_to_all x1, starting transfers between devices, body(): lax.all_to_all(message, 'wa', split_axis=0, concat_axis=0, tiled=True)  11.8 us
    pallas_call x1, Pallas kernels, body(): pl.pallas_call(functools.partial(gram_near_kernel, scale), grid_spec=pltp...  6.15 us
    pallas_call x1, Pallas kernels, body(): pl.pallas_call(spectra_kernel, in_specs=[pl.BlockSpec(memory_space=pltpu....  5.58 us
    ppermute x3, starting transfers between devices, body(): lax.ppermute(power, 'col', p)  5.13 us
    ppermute x3, starting transfers between devices, body(): lax.ppermute(energy, 'col', p)  3.62 us
  transfers between devices with their start and end apart: 19, of which 15 were waited for; matrix products, arithmetic and copies ran while one was open for 1% of the time, Pallas kernels for 8%

profile of v7, /device:TPU:32, one launch (start us, length us, event | category | flops | bytes accessed | tf_op | source)
XLA Modules:
  0.0 95.6 jit_solution(16083092385346472887)
XLA Ops:
  0.0 5.6 %spectra.1 = (f32[8,2,256,128]{3,2,1,0:T(8,128)S(1)}, f32[8,128]{1,0:T(8,128)S(1)}) custom-call(f32[8,256,1024]{2,1,0:T(8,128)} %records.1, bf16[16,512,256]{2,1,0:T(8,128)(2,1)} %constant.6.clone.stored), custom_call_target="tpu_custom_call" | custom-call | tf_op jit(solution)/shard_map/spectra/pallas_call | solution.py:178
  5.6 3.1 %collective-permute-start.2 = (f32[8,128]{1,0:T(8,128)S(1)}, f32[8,128]{1,0:T(8,128)S(1)}, u32[]{:S(2)}, u32[]{:S(2)}) collective-permute-start(f32[8,128]{1,0:T(8,128)S(1)} %get-tuple-element.23.p0), channel_id=1, source_target_pairs={{0,2},{1,3},{2,0},{3,1},{4,6},{5,7},{6,4},{7,5},{8,10},{9,11},{10,... | collective-permute-start | bytes 12296 | tf_op jit(solution)/shard_map/ppermute | solution.py:197
  8.7 1.1 %collective-permute-start.1 = (f32[8,128]{1,0:T(8,128)S(1)}, f32[8,128]{1,0:T(8,128)S(1)}, u32[]{:S(2)}, u32[]{:S(2)}) collective-permute-start(f32[8,128]{1,0:T(8,128)S(1)} %get-tuple-element.23.p0), channel_id=1, source_target_pairs={{0,3},{1,0},{2,1},{3,2},{4,7},{5,4},{6,5},{7,6},{8,11},{9,8},{10,9... | collective-permute-start | bytes 12296 | tf_op jit(solution)/shard_map/ppermute | solution.py:197
  9.8 0.9 collective-permute-start
  11.0 1.2 %turn.1 = (f32[2,1024,128]{2,1,0:T(8,128)S(1)}, f32[2,1024,128]{2,1,0:T(8,128)S(1)}) custom-call(f32[8,2,256,128]{3,2,1,0:T(8,128)S(1)} %get-tuple-element.20.results), custom_call_target="tpu_custom_call" | custom-call | bytes 6291456 | tf_op jit(solution)/shard_map/turn/pallas_call | solution.py:198
  12.3 2.4 %collective-permute-done.p1 = f32[8,128]{1,0:T(8,128)S(1)} collective-permute-done((f32[8,128]{1,0:T(8,128)S(1)}, f32[8,128]{1,0:T(8,128)S(1)}, u32[]{:S(2)}, u32[]{:S(2)}) %collective-permute-start) | collective-permute-done | bytes 4128 | tf_op jit(solution)/shard_map/ppermute | solution.py:197
  14.7 1.2 %whiten.1 = (bf16[64,32,256]{2,1,0:T(8,128)(2,1)}, f32[1,256]{1,0:T(1,128)S(1)}) custom-call(f32[2,1024,128]{2,1,0:T(8,128)S(1)} %get-tuple-element.21.even, f32[2,1024,128]{2,1,0:T(8,128)S(1)} %get-tuple-element.22.odd, f32[8,128]{1,0:T(8,128)S(1)} %get-tuple-element.23.p0, f32[8,128]{1,0:T(8,128)S(1)} %collective-permute-done.p1, ...), custom_call_target="tpu_custom_call" | custom-call | tf_op jit(solution)/shard_map/whiten/pallas_call | solution.py:206
  15.9 11.8 %all-to-all-start = ((bf16[64,32,256]{2,1,0:T(8,128)(2,1)}), bf16[64,32,256]{2,1,0:T(8,128)(2,1)S(1)}, u32[]{:S(2)}, u32[]{:S(2)}) async-start(bf16[64,32,256]{2,1,0:T(8,128)(2,1)} %get-tuple-element.24), calls=%async_computation | async-start | bytes 2097152 | tf_op jit(solution)/shard_map/all_to_all | solution.py:221
  28.6 2.7 %collective-permute-start.3 = (f32[1,256]{1,0:T(1,128)S(1)}, f32[1,256]{1,0:T(1,128)S(1)}, u32[]{:S(2)}, u32[]{:S(2)}) collective-permute-start(f32[1,256]{1,0:T(1,128)S(1)} %get-tuple-element.25), channel_id=1, source_target_pairs={{0,3},{1,0},{2,1},{3,2},{4,7},{5,4},{6,5},{7,6},{8,11},{9,8},{10,9... | collective-permute-start | bytes 3080 | tf_op jit(solution)/shard_map/ppermute | solution.py:223
  31.3 1.5 %collective-permute-done.5 = f32[1,256]{1,0:T(1,128)S(1)} collective-permute-done((f32[1,256]{1,0:T(1,128)S(1)}, f32[1,256]{1,0:T(1,128)S(1)}, u32[]{:S(2)}, u32[]{:S(2)}) %collective-permute-start.5) | collective-permute-done | bytes 1056 | tf_op jit(solution)/shard_map/ppermute | solution.py:223
  33.0 1.2 %collective-permute-done.6 = f32[4,256]{1,0:T(4,128)S(1)} collective-permute-done((f32[4,256]{1,0:T(4,128)S(1)}, f32[4,256]{1,0:T(4,128)S(1)}, u32[]{:S(2)}, u32[]{:S(2)}) %collective-permute-start.6) | collective-permute-done | bytes 4128 | tf_op jit(solution)/shard_map/ppermute | solution.py:227
  34.1 1.6 %collective-permute-start.7 = (f32[4,256]{1,0:T(4,128)S(1)}, f32[4,256]{1,0:T(4,128)S(1)}, u32[]{:S(2)}, u32[]{:S(2)}) collective-permute-start(f32[4,256]{1,0:T(4,128)S(1)} %fusion), channel_id=1, source_target_pairs={{0,8},{4,12},{8,0},{12,4},{16,24},{20,28},{24,16},{28,20},{32,40},... | collective-permute-start | bytes 12296 | tf_op jit(solution)/shard_map/ppermute | solution.py:227
  35.7 2.2 %collective-permute-done.7 = f32[4,256]{1,0:T(4,128)S(1)} collective-permute-done((f32[4,256]{1,0:T(4,128)S(1)}, f32[4,256]{1,0:T(4,128)S(1)}, u32[]{:S(2)}, u32[]{:S(2)}) %collective-permute-start.7) | collective-permute-done | bytes 4128 | tf_op jit(solution)/shard_map/ppermute | solution.py:227
  37.8 3.1 %collective-permute-start.8 = (f32[4,256]{1,0:T(4,128)S(1)}, f32[4,256]{1,0:T(4,128)S(1)}, u32[]{:S(2)}, u32[]{:S(2)}) collective-permute-start(f32[4,256]{1,0:T(4,128)S(1)} %fusion.3), channel_id=1, source_target_pairs={{0,16},{4,20},{8,24},{12,28},{16,0},{20,4},{24,8},{28,12},{32,48},... | collective-permute-start | bytes 12296 | tf_op jit(solution)/shard_map/ppermute | solution.py:227
  40.9 2.3 %collective-permute-done.8 = f32[4,256]{1,0:T(4,128)S(1)} collective-permute-done((f32[4,256]{1,0:T(4,128)S(1)}, f32[4,256]{1,0:T(4,128)S(1)}, u32[]{:S(2)}, u32[]{:S(2)}) %collective-permute-start.8) | collective-permute-done | bytes 4128 | tf_op jit(solution)/shard_map/ppermute | solution.py:227
  43.2 12.4 %all-to-all-done.own = bf16[64,32,256]{2,1,0:T(8,128)(2,1)S(1)} async-done(((bf16[64,32,256]{2,1,0:T(8,128)(2,1)}), bf16[64,32,256]{2,1,0:T(8,128)(2,1)S(1)}, u32[]{:S(2)}, u32[]{:S(2)}) %all-to-all-start) | async-done | bytes 1048608 | tf_op jit(solution)/shard_map/all_to_all | solution.py:221
  55.9 2.0 %collective-permute-start.11 = (bf16[32,32,256]{2,1,0:T(8,128)(2,1)S(1)}, bf16[32,32,256]{2,1,0:T(8,128)(2,1)S(1)}, u32[]{:S(2)}, u32[]{:S(2)}) collective-permute-start(bf16[32,32,256]{2,1,0:T(8,128)(2,1)S(1)} %get-tuple-element.38), channel_id=1, source_target_pairs={{0,1},{1,2},{2,3},{3,0},{4,5},{5,6},{6,7},{7,4},{8,9},{9,10},{10,1... | collective-permute-start | bytes 1572872 | tf_op jit(solution)/shard_map/ppermute | solution.py:234
  58.0 1.4 %collective-permute-start.9 = (f32[4,256]{1,0:T(4,128)S(1)}, f32[4,256]{1,0:T(4,128)S(1)}, u32[]{:S(2)}, u32[]{:S(2)}) collective-permute-start(f32[4,256]{1,0:T(4,128)S(1)} %add.20), channel_id=1, source_target_pairs={{0,32},{4,36},{8,40},{12,44},{16,48},{20,52},{24,56},{28,60},{32,0... | collective-permute-start | bytes 12296 | tf_op jit(solution)/shard_map/ppermute | solution.py:227
  59.4 2.2 %collective-permute-done.9 = f32[4,256]{1,0:T(4,128)S(1)} collective-permute-done((f32[4,256]{1,0:T(4,128)S(1)}, f32[4,256]{1,0:T(4,128)S(1)}, u32[]{:S(2)}, u32[]{:S(2)}) %collective-permute-start.9) | collective-permute-done | bytes 4128 | tf_op jit(solution)/shard_map/ppermute | solution.py:227
  61.6 1.0 %fusion.1 = (bf16[32,32,256]{2,1,0:T(8,128)(2,1)}, bf16[32,32,256]{2,1,0:T(8,128)(2,1)}) fusion(bf16[64,32,256]{2,1,0:T(8,128)(2,1)S(1)} %all-to-all-done.own), kind=kLoop, calls=%fused_computation.2 | loop fusion | bytes 2097152 | tf_op jit(solution)/shard_map/slice | solution.py:238
  62.6 3.2 %collective-permute-start.10 = (bf16[32,32,256]{2,1,0:T(8,128)(2,1)}, bf16[32,32,256]{2,1,0:T(8,128)(2,1)}, u32[]{:S(2)}, u32[]{:S(2)}) collective-permute-start(bf16[32,32,256]{2,1,0:T(8,128)(2,1)} %get-tuple-element.36), channel_id=1, source_target_pairs={{0,3},{1,0},{2,1},{3,2},{4,7},{5,4},{6,5},{7,6},{8,11},{9,8},{10,9... | collective-permute-start | bytes 1572872 | tf_op jit(solution)/shard_map/ppermute | solution.py:239
  65.8 2.6 %collective-permute-start.13 = (f32[4,256]{1,0:T(4,128)S(1)}, f32[4,256]{1,0:T(4,128)S(1)}, u32[]{:S(2)}, u32[]{:S(2)}) collective-permute-start(f32[4,256]{1,0:T(4,128)S(1)} %add.21), channel_id=1, source_target_pairs={{0,64},{4,68},{8,72},{12,76},{16,80},{20,84},{24,88},{28,92},{32,9... | collective-permute-start | bytes 12296 | tf_op jit(solution)/shard_map/ppermute | solution.py:227
  68.5 1.9 %collective-permute-done.13 = f32[4,256]{1,0:T(4,128)S(1)} collective-permute-done((f32[4,256]{1,0:T(4,128)S(1)}, f32[4,256]{1,0:T(4,128)S(1)}, u32[]{:S(2)}, u32[]{:S(2)}) %collective-permute-start.13) | collective-permute-done | bytes 4128 | tf_op jit(solution)/shard_map/ppermute | solution.py:227
  70.7 1.3 %collective-permute-done.11.left_a = bf16[32,32,256]{2,1,0:T(8,128)(2,1)S(1)} collective-permute-done((bf16[32,32,256]{2,1,0:T(8,128)(2,1)S(1)}, bf16[32,32,256]{2,1,0:T(8,128)(2,1)S(1)}, u32[]{:S(2)}, u32[]{:S(2)}) %collective-permute-start.11) | collective-permute-done | bytes 524320 | tf_op jit(solution)/shard_map/ppermute | solution.py:234
  72.0 2.0 %collective-permute-start.16 = (bf16[32,32,256]{2,1,0:T(8,128)(2,1)S(1)}, bf16[32,32,256]{2,1,0:T(8,128)(2,1)S(1)}, u32[]{:S(2)}, u32[]{:S(2)}) collective-permute-start(bf16[32,32,256]{2,1,0:T(8,128)(2,1)S(1)} %collective-permute-done.11.left_a), channel_id=1, source_target_pairs={{0,1},{1,2},{2,3},{3,0},{4,5},{5,6},{6,7},{7,4},{8,9},{9,10},{10,1... | collective-permute-start | bytes 1572872 | tf_op jit(solution)/shard_map/ppermute | solution.py:242
  74.0 3.2 %collective-permute-start.15 = (f32[4,256]{1,0:T(4,128)S(1)}, f32[4,256]{1,0:T(4,128)S(1)}, u32[]{:S(2)}, u32[]{:S(2)}) collective-permute-start(f32[4,256]{1,0:T(4,128)S(1)} %add.22), channel_id=1, source_target_pairs={{0,128},{4,132},{8,136},{12,140},{16,144},{20,148},{24,152},{28,15... | collective-permute-start | bytes 12296 | tf_op jit(solution)/shard_map/ppermute | solution.py:227
  77.2 4.4 %collective-permute-done.15 = f32[4,256]{1,0:T(4,128)S(1)} collective-permute-done((f32[4,256]{1,0:T(4,128)S(1)}, f32[4,256]{1,0:T(4,128)S(1)}, u32[]{:S(2)}, u32[]{:S(2)}) %collective-permute-start.15) | collective-permute-done | bytes 4128 | tf_op jit(solution)/shard_map/ppermute | solution.py:227
  81.5 1.8 %collective-permute-done.14.left_b = bf16[32,32,256]{2,1,0:T(8,128)(2,1)} collective-permute-done((bf16[32,32,256]{2,1,0:T(8,128)(2,1)}, bf16[32,32,256]{2,1,0:T(8,128)(2,1)}, u32[]{:S(2)}, u32[]{:S(2)}) %collective-permute-start.14) | collective-permute-done | bytes 524320 | tf_op jit(solution)/shard_map/ppermute | solution.py:238
  83.3 6.1 %gram_near.1 = (f32[2,2,256,1024]{3,2,1,0:T(8,128)}, bf16[2,512,1024]{2,1,0:T(8,128)(2,1)S(1)}) custom-call(s32[1]{0:T(128)} %bitcast.col, bf16[64,32,256]{2,1,0:T(8,128)(2,1)S(1)} %all-to-all-done.own, bf16[32,32,256]{2,1,0:T(8,128)(2,1)} %collective-permute-done.10.right_a, bf16[32,32,256]{2,1,0:T(8,128)(2,1)S(1)} %collective-permute-done.12.right_b, ...), custom_call_target="tpu_custom_call" | custom-call | flops 1610612736 | bytes 8388608 | tf_op jit(solution)/shard_map/gram_near/pallas_call | solution.py:264
  89.5 3.0 %collective-permute-done.17.far_b = bf16[32,32,256]{2,1,0:T(8,128)(2,1)S(1)} collective-permute-done((bf16[32,32,256]{2,1,0:T(8,128)(2,1)S(1)}, bf16[32,32,256]{2,1,0:T(8,128)(2,1)S(1)}, u32[]{:S(2)}, u32[]{:S(2)}) %collective-permute-start.17) | collective-permute-done | bytes 524320 | tf_op jit(solution)/shard_map/ppermute | solution.py:243
  92.5 1.3 %collective-permute-done.16.far_a = bf16[32,32,256]{2,1,0:T(8,128)(2,1)S(1)} collective-permute-done((bf16[32,32,256]{2,1,0:T(8,128)(2,1)S(1)}, bf16[32,32,256]{2,1,0:T(8,128)(2,1)S(1)}, u32[]{:S(2)}, u32[]{:S(2)}) %collective-permute-start.16) | collective-permute-done | bytes 524320 | tf_op jit(solution)/shard_map/ppermute | solution.py:242
  93.8 1.8 %gram_far.1 = f32[2,2,256,1024]{3,2,1,0:T(8,128)} custom-call(s32[1]{0:T(128)} %bitcast.col, bf16[2,512,1024]{2,1,0:T(8,128)(2,1)S(1)} %get-tuple-element.33.lhs, bf16[32,32,256]{2,1,0:T(8,128)(2,1)S(1)} %collective-permute-done.16.far_a, bf16[32,32,256]{2,1,0:T(8,128)(2,1)S(1)} %collective-permute-done.17.far_b, ...), custom_call_target="tpu_custom_call", output_to_operand_aliasing={{}: (5, {})} | custom-call | flops 536870912 | bytes 4194304 | tf_op jit(solution)/shard_map/gram_far/pallas_call | solution.py:279
  (25 shorter events, 2.2 us)
Async XLA Ops:
  0.0 10.7 %copy-start = (f32[128]{0:T(128)S(1)}, f32[128]{0:T(128)}, u32[]{:S(2)}) copy-start(f32[128]{0:T(128)} %param.4) | copy-start | bytes 1540
  5.6 6.6 %collective-permute-start.2 = (f32[8,128]{1,0:T(8,128)S(1)}, f32[8,128]{1,0:T(8,128)S(1)}, u32[]{:S(2)}, u32[]{:S(2)}) collective-permute-start(f32[8,128]{1,0:T(8,128)S(1)} %get-tuple-element.23.p0), channel_id=1, source_target_pairs={{0,2},{1,3},{2,0},{3,1},{4,6},{5,7},{6,4},{7,5},{8,10},{9,11},{10,... | collective-permute-start | bytes 12296 | tf_op jit(solution)/shard_map/ppermute | solution.py:197
  8.7 3.6 %collective-permute-start.1 = (f32[8,128]{1,0:T(8,128)S(1)}, f32[8,128]{1,0:T(8,128)S(1)}, u32[]{:S(2)}, u32[]{:S(2)}) collective-permute-start(f32[8,128]{1,0:T(8,128)S(1)} %get-tuple-element.23.p0), channel_id=1, source_target_pairs={{0,3},{1,0},{2,1},{3,2},{4,7},{5,4},{6,5},{7,6},{8,11},{9,8},{10,9... | collective-permute-start | bytes 12296 | tf_op jit(solution)/shard_map/ppermute | solution.py:197
  9.8 4.8 %collective-permute-start = (f32[8,128]{1,0:T(8,128)S(1)}, f32[8,128]{1,0:T(8,128)S(1)}, u32[]{:S(2)}, u32[]{:S(2)}) collective-permute-start(f32[8,128]{1,0:T(8,128)S(1)} %get-tuple-element.23.p0), channel_id=1, source_target_pairs={{0,1},{1,2},{2,3},{3,0},{4,5},{5,6},{6,7},{7,4},{8,9},{9,10},{10,1... | collective-permute-start | bytes 12296 | tf_op jit(solution)/shard_map/ppermute | solution.py:197
  15.9 39.7 %all-to-all-start = ((bf16[64,32,256]{2,1,0:T(8,128)(2,1)}), bf16[64,32,256]{2,1,0:T(8,128)(2,1)S(1)}, u32[]{:S(2)}, u32[]{:S(2)}) async-start(bf16[64,32,256]{2,1,0:T(8,128)(2,1)} %get-tuple-element.24), calls=%async_computation | async-start | bytes 2097152 | tf_op jit(solution)/shard_map/all_to_all | solution.py:221
  27.7 5.2 %collective-permute-start.5 = (f32[1,256]{1,0:T(1,128)S(1)}, f32[1,256]{1,0:T(1,128)S(1)}, u32[]{:S(2)}, u32[]{:S(2)}) collective-permute-start(f32[1,256]{1,0:T(1,128)S(1)} %get-tuple-element.25), channel_id=1, source_target_pairs={{0,2},{1,3},{2,0},{3,1},{4,6},{5,7},{6,4},{7,5},{8,10},{9,11},{10,... | collective-permute-start | bytes 3080 | tf_op jit(solution)/shard_map/ppermute | solution.py:223
  28.0 4.8 %collective-permute-start.4 = (f32[1,256]{1,0:T(1,128)S(1)}, f32[1,256]{1,0:T(1,128)S(1)}, u32[]{:S(2)}, u32[]{:S(2)}) collective-permute-start(f32[1,256]{1,0:T(1,128)S(1)} %get-tuple-element.25), channel_id=1, source_target_pairs={{0,1},{1,2},{2,3},{3,0},{4,5},{5,6},{6,7},{7,4},{8,9},{9,10},{10,1... | collective-permute-start | bytes 3080 | tf_op jit(solution)/shard_map/ppermute | solution.py:223
  28.6 4.2 %collective-permute-start.3 = (f32[1,256]{1,0:T(1,128)S(1)}, f32[1,256]{1,0:T(1,128)S(1)}, u32[]{:S(2)}, u32[]{:S(2)}) collective-permute-start(f32[1,256]{1,0:T(1,128)S(1)} %get-tuple-element.25), channel_id=1, source_target_pairs={{0,3},{1,0},{2,1},{3,2},{4,7},{5,4},{6,5},{7,6},{8,11},{9,8},{10,9... | collective-permute-start | bytes 3080 | tf_op jit(solution)/shard_map/ppermute | solution.py:223
  32.9 1.3 %collective-permute-start.6 = (f32[4,256]{1,0:T(4,128)S(1)}, f32[4,256]{1,0:T(4,128)S(1)}, u32[]{:S(2)}, u32[]{:S(2)}) collective-permute-start(f32[4,256]{1,0:T(4,128)S(1)} %pad_maximum_fusion), channel_id=1, source_target_pairs={{0,4},{4,0},{8,12},{12,8},{16,20},{20,16},{24,28},{28,24},{32,36},... | collective-permute-start | bytes 12296 | tf_op jit(solution)/shard_map/ppermute | solution.py:227
  34.1 3.7 %collective-permute-start.7 = (f32[4,256]{1,0:T(4,128)S(1)}, f32[4,256]{1,0:T(4,128)S(1)}, u32[]{:S(2)}, u32[]{:S(2)}) collective-permute-start(f32[4,256]{1,0:T(4,128)S(1)} %fusion), channel_id=1, source_target_pairs={{0,8},{4,12},{8,0},{12,4},{16,24},{20,28},{24,16},{28,20},{32,40},... | collective-permute-start | bytes 12296 | tf_op jit(solution)/shard_map/ppermute | solution.py:227
  37.8 5.4 %collective-permute-start.8 = (f32[4,256]{1,0:T(4,128)S(1)}, f32[4,256]{1,0:T(4,128)S(1)}, u32[]{:S(2)}, u32[]{:S(2)}) collective-permute-start(f32[4,256]{1,0:T(4,128)S(1)} %fusion.3), channel_id=1, source_target_pairs={{0,16},{4,20},{8,24},{12,28},{16,0},{20,4},{24,8},{28,12},{32,48},... | collective-permute-start | bytes 12296 | tf_op jit(solution)/shard_map/ppermute | solution.py:227
  55.7 15.0 %collective-permute-start.12 = (bf16[32,32,256]{2,1,0:T(8,128)(2,1)S(1)}, bf16[32,32,256]{2,1,0:T(8,128)(2,1)S(1)}, u32[]{:S(2)}, u32[]{:S(2)}) collective-permute-start(bf16[32,32,256]{2,1,0:T(8,128)(2,1)S(1)} %get-tuple-element.37), channel_id=1, source_target_pairs={{0,3},{1,0},{2,1},{3,2},{4,7},{5,4},{6,5},{7,6},{8,11},{9,8},{10,9... | collective-permute-start | bytes 1572872 | tf_op jit(solution)/shard_map/ppermute | solution.py:235
  55.9 16.0 %collective-permute-start.11 = (bf16[32,32,256]{2,1,0:T(8,128)(2,1)S(1)}, bf16[32,32,256]{2,1,0:T(8,128)(2,1)S(1)}, u32[]{:S(2)}, u32[]{:S(2)}) collective-permute-start(bf16[32,32,256]{2,1,0:T(8,128)(2,1)S(1)} %get-tuple-element.38), channel_id=1, source_target_pairs={{0,1},{1,2},{2,3},{3,0},{4,5},{5,6},{6,7},{7,4},{8,9},{9,10},{10,1... | collective-permute-start | bytes 1572872 | tf_op jit(solution)/shard_map/ppermute | solution.py:234
  58.0 3.6 %collective-permute-start.9 = (f32[4,256]{1,0:T(4,128)S(1)}, f32[4,256]{1,0:T(4,128)S(1)}, u32[]{:S(2)}, u32[]{:S(2)}) collective-permute-start(f32[4,256]{1,0:T(4,128)S(1)} %add.20), channel_id=1, source_target_pairs={{0,32},{4,36},{8,40},{12,44},{16,48},{20,52},{24,56},{28,60},{32,0... | collective-permute-start | bytes 12296 | tf_op jit(solution)/shard_map/ppermute | solution.py:227
  62.6 20.7 %collective-permute-start.14 = (bf16[32,32,256]{2,1,0:T(8,128)(2,1)}, bf16[32,32,256]{2,1,0:T(8,128)(2,1)}, u32[]{:S(2)}, u32[]{:S(2)}) collective-permute-start(bf16[32,32,256]{2,1,0:T(8,128)(2,1)} %get-tuple-element.35), channel_id=1, source_target_pairs={{0,1},{1,2},{2,3},{3,0},{4,5},{5,6},{6,7},{7,4},{8,9},{9,10},{10,1... | collective-permute-start | bytes 1572872 | tf_op jit(solution)/shard_map/ppermute | solution.py:238
  62.6 20.7 %collective-permute-start.10 = (bf16[32,32,256]{2,1,0:T(8,128)(2,1)}, bf16[32,32,256]{2,1,0:T(8,128)(2,1)}, u32[]{:S(2)}, u32[]{:S(2)}) collective-permute-start(bf16[32,32,256]{2,1,0:T(8,128)(2,1)} %get-tuple-element.36), channel_id=1, source_target_pairs={{0,3},{1,0},{2,1},{3,2},{4,7},{5,4},{6,5},{7,6},{8,11},{9,8},{10,9... | collective-permute-start | bytes 1572872 | tf_op jit(solution)/shard_map/ppermute | solution.py:239
  65.8 4.5 %collective-permute-start.13 = (f32[4,256]{1,0:T(4,128)S(1)}, f32[4,256]{1,0:T(4,128)S(1)}, u32[]{:S(2)}, u32[]{:S(2)}) collective-permute-start(f32[4,256]{1,0:T(4,128)S(1)} %add.21), channel_id=1, source_target_pairs={{0,64},{4,68},{8,72},{12,76},{16,80},{20,84},{24,88},{28,92},{32,9... | collective-permute-start | bytes 12296 | tf_op jit(solution)/shard_map/ppermute | solution.py:227
  72.0 20.5 %collective-permute-start.17 = (bf16[32,32,256]{2,1,0:T(8,128)(2,1)S(1)}, bf16[32,32,256]{2,1,0:T(8,128)(2,1)S(1)}, u32[]{:S(2)}, u32[]{:S(2)}) collective-permute-start(bf16[32,32,256]{2,1,0:T(8,128)(2,1)S(1)} %collective-permute-done.12.right_b), channel_id=1, source_target_pairs={{0,3},{1,0},{2,1},{3,2},{4,7},{5,4},{6,5},{7,6},{8,11},{9,8},{10,9... | collective-permute-start | bytes 1572872 | tf_op jit(solution)/shard_map/ppermute | solution.py:243
  72.0 21.8 %collective-permute-start.16 = (bf16[32,32,256]{2,1,0:T(8,128)(2,1)S(1)}, bf16[32,32,256]{2,1,0:T(8,128)(2,1)S(1)}, u32[]{:S(2)}, u32[]{:S(2)}) collective-permute-start(bf16[32,32,256]{2,1,0:T(8,128)(2,1)S(1)} %collective-permute-done.11.left_a), channel_id=1, source_target_pairs={{0,1},{1,2},{2,3},{3,0},{4,5},{5,6},{6,7},{7,4},{8,9},{9,10},{10,1... | collective-permute-start | bytes 1572872 | tf_op jit(solution)/shard_map/ppermute | solution.py:242
  74.0 7.5 %collective-permute-start.15 = (f32[4,256]{1,0:T(4,128)S(1)}, f32[4,256]{1,0:T(4,128)S(1)}, u32[]{:S(2)}, u32[]{:S(2)}) collective-permute-start(f32[4,256]{1,0:T(4,128)S(1)} %add.22), channel_id=1, source_target_pairs={{0,128},{4,132},{8,136},{12,140},{16,144},{20,148},{24,152},{28,15... | collective-permute-start | bytes 12296 | tf_op jit(solution)/shard_map/ppermute | solution.py:227
